TPU v7x, 128 devices: a whole 4x4x4 slice. The times are simulated.
128 devices in a mesh: lon: 16 (over x, y_hi, core), lat: 4 (over z), grp: 2 (over y_lo).
Axes of the slice: x: 4, y: 4 (y_hi: 2, y_lo: 2; y = y_hi * 2 + y_lo), z: 4, core: 2. Of those that a mesh axis runs over, the one named last changes fastest.
Arguments:
- east_vel: float32 [8, 1024, 2048], P('grp', 'lon', 'lat'), may hold values from -6 to 6
- north_vel: float32 [8, 1024, 2048], P('grp', 'lon', 'lat'), may hold values from -6 to 6
- buoyancy: float32 [8, 1024, 2048], P('grp', 'lon', 'lat'), may hold values from -6 to 6
- wet_mask: int32 [8, 1024, 2048], P('grp', 'lon', 'lat'), may hold values from 0 to 1, as said below
- bottom_level: int32 [1024, 2048], P('lon', 'lat'), may hold values from 0 to 8
- surface: float32 [1024, 2048], P('lon', 'lat'), may hold values from -3 to 3
- w_in: bfloat16 [9, 8, 32], replicated, may hold values from -0.75 to 0.75
- b_in: float32 [32], replicated, may hold values from -3 to 3
- w_mid: bfloat16 [9, 32, 32], replicated, may hold values from -0.375 to 0.375
- b_mid: float32 [32], replicated, may hold values from -3 to 3
- w_out: bfloat16 [9, 32, 8], replicated, may hold values from -0.375 to 0.375
Outputs:
- east_new: float32 [8, 1024, 2048], P('grp', 'lon', 'lat')
- north_new: float32 [8, 1024, 2048], P('grp', 'lon', 'lat')
- surface_new: float32 [1024, 2048], P('lon', 'lat')
Inputs may be any that keep to these rules, and one draw needn't show every extreme that they name: wet_mask is 1 exactly at the levels below bottom_level of the column.
All inputs are finite; a program needn't handle non-finite values.
Results may differ from a plain program's by a relative error of at most 0.002.
Values may be sent and summed in bfloat16 or wider, within the bound.
No kernel may reach another device: no remote copies, remote signals or barrier semaphores. Data moves between devices by JAX's collectives and lax.ppermute only.
A program may use at most 128 MiB of HBM per device.

v0:
```python
import jax
import jax.numpy as jnp
from jax import lax
from jax.sharding import PartitionSpec as P

NSUB = 8


coriolis_base = 0.6
coriolis_slope = 0.8
press_coef = 0.3
drag_coef = 0.5
step_dt = 0.2
closure_coef = 0.5
gravity = 1.0
sub_dt = 0.4


def passed_along(shard, axis, by):
    length = lax.axis_size(axis)
    pairs = [(i, i + by) for i in range(length) if 0 <= i + by < length]
    return lax.ppermute(shard, axis, pairs)


def extended(shard, sides, width):
    for axis, dim in sides:
        size, length = (lax.axis_size(axis), shard.shape[dim])
        up = [(i, (i + 1) % size) for i in range(size)]
        down = [(j, i) for i, j in up]
        last = lax.slice_in_dim(shard, length - width, length, axis=dim)
        leading = lax.slice_in_dim(shard, 0, width, axis=dim)
        before = lax.ppermute(last, axis, up)
        after = lax.ppermute(leading, axis, down)
        shard = jnp.concatenate([before, shard, after], axis=dim)
    return shard


def thickness(count):
    return 1.0 + 0.25 * jnp.arange(count).astype(jnp.float32)


def conv_layer(field, weight, bias):
    width = field.shape[1] - 2
    height = field.shape[2] - 2
    total = jnp.zeros((weight.shape[2], width, height), jnp.float32)
    for offset in range(9):
        shift_x = offset // 3
        shift_y = offset % 3
        window = field[:, shift_x : shift_x + width, shift_y : shift_y + height]
        total = total + jnp.einsum(
            "io,ixy->oxy", weight[offset], window, preferred_element_type=jnp.float32
        )
    return total + bias[:, None, None]


def closure_stack(padded, inside, w_in, b_in, w_mid, b_mid, w_out):
    source = jnp.where(inside[None, None, :] > 0, padded, jnp.zeros_like(padded))
    first = jnp.maximum(conv_layer(source, w_in, b_in), 0.0)
    first = jnp.where(inside[None, None, 1:-1] > 0, first, 0.0).astype(jnp.bfloat16)
    second = jnp.maximum(conv_layer(first, w_mid, b_mid), 0.0)
    second = jnp.where(inside[None, None, 2:-2] > 0, second, 0.0).astype(jnp.bfloat16)
    final = conv_layer(second, w_out, jnp.zeros((w_out.shape[2],), jnp.float32))
    return (closure_coef * final).astype(jnp.bfloat16)


def ddx_inner(field):
    return (field[..., 2:, 1:-1] - field[..., :-2, 1:-1]) * 0.5


def ddy_inner(field):
    return (field[..., 1:-1, 2:] - field[..., 1:-1, :-2]) * 0.5


def local(
    east_vel, north_vel, buoyancy, wet_mask, bottom_level, surface, w_in, b_in, w_mid, b_mid, w_out
):
    depth_dev = east_vel.shape[0]
    height = east_vel.shape[2]
    group = lax.axis_index("grp")
    lat_index = lax.axis_index("lat")
    total_rows = height * lax.axis_size("lat")
    levels_all = depth_dev * lax.axis_size("grp")
    thick_all = thickness(levels_all)
    thick = lax.dynamic_slice_in_dim(thick_all, group * depth_dev, depth_dev)

    def inside_rows(margin):
        rows = lat_index * height + jnp.arange(-margin, height + margin)
        return ((rows >= 0) & (rows < total_rows)).astype(jnp.float32)

    wetf = wet_mask.astype(jnp.float32)
    weighted = buoyancy * wetf * thick[:, None, None]
    partial_load = jnp.cumsum(weighted, 0) - 0.5 * weighted
    above = passed_along(jnp.sum(weighted, 0), "grp", 1)
    pressure = above[None] + partial_load
    upper = jnp.concatenate([east_vel * wetf, north_vel * wetf], 0).astype(jnp.bfloat16)
    padded = extended(upper, (("lon", 1), ("lat", 2)), 3)
    inside = inside_rows(3)
    forcing = closure_stack(padded, inside, w_in, b_in, w_mid, b_mid, w_out)
    top_block = (group == 0).astype(jnp.float32)
    force_east = forcing[:depth_dev].astype(jnp.float32) * top_block
    force_north = forcing[depth_dev:].astype(jnp.float32) * top_block
    rim = extended(pressure, (("lon", 1), ("lat", 2)), 1) * inside_rows(1)
    grad_x = ddx_inner(rim)
    grad_y = ddy_inner(rim)
    coriolis = coriolis_base + coriolis_slope * (
        (lat_index * height + jnp.arange(height)).astype(jnp.float32) / total_rows - 0.5
    )
    levels_here = group * depth_dev + jnp.arange(depth_dev)
    bottom = (levels_here[:, None, None] == bottom_level[None] - 1).astype(jnp.float32)
    tend_east = wetf * (
        coriolis * north_vel - press_coef * grad_x + force_east - drag_coef * bottom * east_vel
    )
    tend_north = wetf * (
        -coriolis * east_vel - press_coef * grad_y + force_north - drag_coef * bottom * north_vel
    )
    weights_col = wetf * thick[:, None, None]
    sums = lax.psum(
        (
            jnp.sum(weights_col * tend_east, 0),
            jnp.sum(weights_col * tend_north, 0),
            jnp.sum(weights_col * east_vel, 0),
            jnp.sum(weights_col * north_vel, 0),
        ),
        "grp",
    )
    column_thick = (jnp.arange(levels_all)[:, None, None] < bottom_level[None]).astype(
        jnp.float32
    ) * thick_all[:, None, None]
    depth = jnp.sum(column_thick, 0)
    floored = jnp.maximum(depth, 1.0)
    relative = depth / jnp.sum(thick_all)
    column = (bottom_level > 0).astype(jnp.float32)
    mean_te = sums[0] / floored
    mean_tn = sums[1] / floored
    east_start = sums[2] / floored
    north_start = sums[3] / floored
    east_bar, north_bar, level_now = (east_start, north_start, surface)
    for step in range(NSUB):
        rim_level = extended(level_now, (("lon", 0), ("lat", 1)), 1) * inside_rows(1)[None, :]
        east_bar = column * (east_bar + sub_dt * (-gravity * ddx_inner(rim_level) + mean_te))
        north_bar = column * (north_bar + sub_dt * (-gravity * ddy_inner(rim_level) + mean_tn))
        fluxes = jnp.stack([relative * east_bar, relative * north_bar])
        rim_flux = extended(fluxes, (("lon", 1), ("lat", 2)), 1) * inside_rows(1)
        level_now = level_now - sub_dt * (ddx_inner(rim_flux[0]) + ddy_inner(rim_flux[1]))
    east_new = wetf * (east_vel + step_dt * (tend_east - mean_te) - east_start + east_bar)
    north_new = wetf * (north_vel + step_dt * (tend_north - mean_tn) - north_start + north_bar)
    return (east_new, north_new, level_now)


def solution(mesh):
    in_specs = (
        P("grp", "lon", "lat"),
        P("grp", "lon", "lat"),
        P("grp", "lon", "lat"),
        P("grp", "lon", "lat"),
        P("lon", "lat"),
        P("lon", "lat"),
        P(),
        P(),
        P(),
        P(),
        P(),
    )
    out_specs = (P("grp", "lon", "lat"), P("grp", "lon", "lat"), P("lon", "lat"))
    return jax.shard_map(local, mesh=mesh, in_specs=in_specs, out_specs=out_specs, check_vma=False)
```

profile of v0, /device:TPU:0, one launch (start us, length us, event | category | flops | bytes accessed | tf_op | source)
XLA Modules:
  0.0 403.7 jit_solution(4090296814767722350)
XLA Ops:
  7.3 4.0 fusion.281
  11.4 5.3 %collective-permute-start.6 = (bf16[8,3,512]{2,0,1:T(8,128)(2,1)S(1)}, bf16[8,3,512]{2,0,1:T(8,128)(2,1)S(1)}, u32[]{:S(2)}, u32[]{:S(2)}) collective-permute-start(bf16[8,3,512]{2,0,1:T(8,128)(2,1)S(1)} %get-tuple-element.63), channel_id=1, source_target_pairs={{8,0},{16,8},{24,16},{32,24},{40,32},{48,40},{56,48},{64,56},{72,6... | collective-permute-start | bytes 73736 | tf_op jit(solution)/shard_map/ppermute | solution.py:33
  16.7 4.2 %collective-permute-start = (f32[64,512]{1,0:T(8,128)}, f32[64,512]{1,0:T(8,128)}, u32[]{:S(2)}, u32[]{:S(2)}) collective-permute-start(f32[64,512]{1,0:T(8,128)} %get-tuple-element.44), channel_id=1, source_target_pairs={{0,1},{2,3},{4,5},{6,7},{8,9},{10,11},{12,13},{14,15},{16,17},{18,... | collective-permute-start | bytes 393224 | tf_op jit(solution)/shard_map/ppermute | solution.py:22
  27.0 15.3 %reduce_window_sum.11 = f32[4,64,512]{2,0,1:T(4,128)} reduce-window(f32[4,64,512]{2,0,1:T(4,128)S(1)} %get-tuple-element.45, f32[]{:T(128)} %constant.101.clone.1), window={size=4x1x1 pad=3_0x0_0x0_0}, to_apply=%region_1.2 | reduce-window | flops 393216 | bytes 1048580 | tf_op jit(solution)/shard_map/jit(cumsum)/reduce_window_sum | solution.py:92
  43.1 3.4 fusion.74
  69.7 15.6 %fusion = bf16[32,68,516]{2,0,1:T(8,128)(2,1)S(1)} fusion(f32[32]{0:T(128)S(1)} %copy-done.14, f32[68,516,32]{1,2,0:T(8,128)} %fusion.74, f32[68,516,32]{1,2,0:T(8,128)} %fusion.76, f32[68,516,32]{1,2,0:T(8,128)} %fusion.78, f32[68,516,32]{1,2,0:T(8,128)} %fusion.80, f32[68,516,32]{1,2,0:T(8,128)} %fusion.82, f32[68,516,32]{1,2,0:T(8,128)} %fusion.84, ...), kind=kOutput, calls=%fused_computation.2 | convolution fusion | flops 31438848 | bytes 38875648 | tf_op jit(solution)/shard_map/io,ixy->oxy/dot_general | solution.py:50
  85.3 4.2 %fusion.1 = f32[66,514,32]{1,2,0:T(8,128)} fusion(bf16[32,68,516]{2,0,1:T(8,128)(2,1)S(1)} %fusion, bf16[9,32,32]{2,1,0:T(8,128)(2,1)} %param.19), kind=kOutput, calls=%fused_computation.3 | convolution fusion | flops 69476352 | bytes 7053824 | tf_op jit(solution)/shard_map/io,ixy->oxy/dot_general | solution.py:50
  92.8 3.4 fusion.13
  96.2 3.4 fusion.15
  99.6 3.4 fusion.3
  106.2 3.4 fusion.7
  109.6 3.4 fusion.9
  113.0 17.2 %fusion.19 = bf16[32,66,514]{2,0,1:T(8,128)(2,1)} fusion(f32[32]{0:T(128)S(1)} %copy-done.16, f32[66,514,32]{1,2,0:T(8,128)} %fusion.1, f32[66,514,32]{1,2,0:T(8,128)} %fusion.3, f32[66,514,32]{1,2,0:T(8,128)} %fusion.5, f32[66,514,32]{1,2,0:T(8,128)} %fusion.7, f32[66,514,32]{1,2,0:T(8,128)} %fusion.9, f32[66,514,32]{1,2,0:T(8,128)} %fusion.11, ...), kind=kOutput, calls=%fused_computation.21 | convolution fusion | flops 82503168 | bytes 39622400 | tf_op jit(solution)/shard_map/io,ixy->oxy/dot_general | solution.py:50
  138.5 5.3 %collective-permute-start.2 = (f32[4,1,512]{2,0,1:T(4,128)S(1)}, f32[4,1,512]{2,0,1:T(4,128)S(1)}, u32[]{:S(2)}, u32[]{:S(2)}) collective-permute-start(f32[4,1,512]{2,0,1:T(4,128)S(1)} %get-tuple-element.59), channel_id=1, source_target_pairs={{8,0},{16,8},{24,16},{32,24},{40,32},{48,40},{56,48},{64,56},{72,6... | collective-permute-start | bytes 24584 | tf_op jit(solution)/shard_map/ppermute | solution.py:33
  155.5 4.2 %collective-permute-start.10 = (f32[1,512]{1,0:T(1,128)S(1)}, f32[1,512]{1,0:T(1,128)S(1)}, u32[]{:S(2)}, u32[]{:S(2)}) collective-permute-start(f32[1,512]{1,0:T(1,128)S(1)} %get-tuple-element.151), channel_id=1, source_target_pairs={{8,0},{16,8},{24,16},{32,24},{40,32},{48,40},{56,48},{64,56},{72,6... | collective-permute-start | bytes 6152 | tf_op jit(solution)/shard_map/ppermute | solution.py:33
  161.1 5.5 %collective-permute-done.9 = f32[1,512]{1,0:T(1,128)S(1)} collective-permute-done((f32[1,512]{1,0:T(1,128)S(1)}, f32[1,512]{1,0:T(1,128)S(1)}, u32[]{:S(2)}, u32[]{:S(2)}) %collective-permute-start.9) | collective-permute-done | bytes 2080 | tf_op jit(solution)/shard_map/ppermute | solution.py:32
  172.0 19.4 %all-reduce.3.cloned.1.call-done = (f32[64,512]{1,0:T(8,128)}, f32[64,512]{1,0:T(8,128)}, f32[64,512]{1,0:T(8,128)}, f32[64,512]{1,0:T(8,128)}) async-done(((f32[64,512]{1,0:T(8,128)}, f32[64,512]{1,0:T(8,128)}, f32[64,512]{1,0:T(8,128)}, f32[64,512]{1,0:T(8,128)}), (f32[64,512]{1,0:T(8,128)}, f32[64,512]{1,0:T(8,128)}, f32[64,512]{1,0:T(8,128)}, f32[64,512]{1,0:T(8,128)})) %all-reduce.3.cloned.1.call-update) | async-done | bytes 524304 | tf_op jit(solution)/shard_map/psum | solution.py:117
  195.1 5.3 %collective-permute-start.14 = (f32[2,1,512]{2,1,0:T(1,128)S(1)}, f32[2,1,512]{2,1,0:T(1,128)S(1)}, u32[]{:S(2)}, u32[]{:S(2)}) collective-permute-start(f32[2,1,512]{2,1,0:T(1,128)S(1)} %get-tuple-element.119), channel_id=1, source_target_pairs={{8,0},{16,8},{24,16},{32,24},{40,32},{48,40},{56,48},{64,56},{72,6... | collective-permute-start | bytes 12296 | tf_op jit(solution)/shard_map/ppermute | solution.py:33
  208.6 5.3 %collective-permute-start.18 = (f32[1,512]{1,0:T(1,128)S(1)}, f32[1,512]{1,0:T(1,128)S(1)}, u32[]{:S(2)}, u32[]{:S(2)}) collective-permute-start(f32[1,512]{1,0:T(1,128)S(1)} %get-tuple-element.149), channel_id=1, source_target_pairs={{8,0},{16,8},{24,16},{32,24},{40,32},{48,40},{56,48},{64,56},{72,6... | collective-permute-start | bytes 6152 | tf_op jit(solution)/shard_map/ppermute | solution.py:33
  222.0 5.3 %collective-permute-start.22 = (f32[2,1,512]{2,1,0:T(1,128)S(1)}, f32[2,1,512]{2,1,0:T(1,128)S(1)}, u32[]{:S(2)}, u32[]{:S(2)}) collective-permute-start(f32[2,1,512]{2,1,0:T(1,128)S(1)} %get-tuple-element.117), channel_id=1, source_target_pairs={{8,0},{16,8},{24,16},{32,24},{40,32},{48,40},{56,48},{64,56},{72,6... | collective-permute-start | bytes 12296 | tf_op jit(solution)/shard_map/ppermute | solution.py:33
  235.0 5.3 %collective-permute-start.26 = (f32[1,512]{1,0:T(1,128)S(1)}, f32[1,512]{1,0:T(1,128)S(1)}, u32[]{:S(2)}, u32[]{:S(2)}) collective-permute-start(f32[1,512]{1,0:T(1,128)S(1)} %get-tuple-element.147), channel_id=1, source_target_pairs={{8,0},{16,8},{24,16},{32,24},{40,32},{48,40},{56,48},{64,56},{72,6... | collective-permute-start | bytes 6152 | tf_op jit(solution)/shard_map/ppermute | solution.py:33
  248.5 5.3 %collective-permute-start.30 = (f32[2,1,512]{2,1,0:T(1,128)S(1)}, f32[2,1,512]{2,1,0:T(1,128)S(1)}, u32[]{:S(2)}, u32[]{:S(2)}) collective-permute-start(f32[2,1,512]{2,1,0:T(1,128)S(1)} %get-tuple-element.115), channel_id=1, source_target_pairs={{8,0},{16,8},{24,16},{32,24},{40,32},{48,40},{56,48},{64,56},{72,6... | collective-permute-start | bytes 12296 | tf_op jit(solution)/shard_map/ppermute | solution.py:33
  261.7 5.3 %collective-permute-start.34 = (f32[1,512]{1,0:T(1,128)S(1)}, f32[1,512]{1,0:T(1,128)S(1)}, u32[]{:S(2)}, u32[]{:S(2)}) collective-permute-start(f32[1,512]{1,0:T(1,128)S(1)} %get-tuple-element.145), channel_id=1, source_target_pairs={{8,0},{16,8},{24,16},{32,24},{40,32},{48,40},{56,48},{64,56},{72,6... | collective-permute-start | bytes 6152 | tf_op jit(solution)/shard_map/ppermute | solution.py:33
  275.3 5.3 %collective-permute-start.38 = (f32[2,1,512]{2,1,0:T(1,128)S(1)}, f32[2,1,512]{2,1,0:T(1,128)S(1)}, u32[]{:S(2)}, u32[]{:S(2)}) collective-permute-start(f32[2,1,512]{2,1,0:T(1,128)S(1)} %get-tuple-element.113), channel_id=1, source_target_pairs={{8,0},{16,8},{24,16},{32,24},{40,32},{48,40},{56,48},{64,56},{72,6... | collective-permute-start | bytes 12296 | tf_op jit(solution)/shard_map/ppermute | solution.py:33
  288.3 5.3 %collective-permute-start.42 = (f32[1,512]{1,0:T(1,128)S(1)}, f32[1,512]{1,0:T(1,128)S(1)}, u32[]{:S(2)}, u32[]{:S(2)}) collective-permute-start(f32[1,512]{1,0:T(1,128)S(1)} %get-tuple-element.143), channel_id=1, source_target_pairs={{8,0},{16,8},{24,16},{32,24},{40,32},{48,40},{56,48},{64,56},{72,6... | collective-permute-start | bytes 6152 | tf_op jit(solution)/shard_map/ppermute | solution.py:33
  301.8 5.3 %collective-permute-start.46 = (f32[2,1,512]{2,1,0:T(1,128)S(1)}, f32[2,1,512]{2,1,0:T(1,128)S(1)}, u32[]{:S(2)}, u32[]{:S(2)}) collective-permute-start(f32[2,1,512]{2,1,0:T(1,128)S(1)} %get-tuple-element.111), channel_id=1, source_target_pairs={{8,0},{16,8},{24,16},{32,24},{40,32},{48,40},{56,48},{64,56},{72,6... | collective-permute-start | bytes 12296 | tf_op jit(solution)/shard_map/ppermute | solution.py:33
  315.0 5.3 %collective-permute-start.50 = (f32[1,512]{1,0:T(1,128)S(1)}, f32[1,512]{1,0:T(1,128)S(1)}, u32[]{:S(2)}, u32[]{:S(2)}) collective-permute-start(f32[1,512]{1,0:T(1,128)S(1)} %get-tuple-element.141), channel_id=1, source_target_pairs={{8,0},{16,8},{24,16},{32,24},{40,32},{48,40},{56,48},{64,56},{72,6... | collective-permute-start | bytes 6152 | tf_op jit(solution)/shard_map/ppermute | solution.py:33
  328.4 5.3 %collective-permute-start.54 = (f32[2,1,512]{2,1,0:T(1,128)S(1)}, f32[2,1,512]{2,1,0:T(1,128)S(1)}, u32[]{:S(2)}, u32[]{:S(2)}) collective-permute-start(f32[2,1,512]{2,1,0:T(1,128)S(1)} %get-tuple-element.109), channel_id=1, source_target_pairs={{8,0},{16,8},{24,16},{32,24},{40,32},{48,40},{56,48},{64,56},{72,6... | collective-permute-start | bytes 12296 | tf_op jit(solution)/shard_map/ppermute | solution.py:33
  341.4 5.3 %collective-permute-start.58 = (f32[1,512]{1,0:T(1,128)S(1)}, f32[1,512]{1,0:T(1,128)S(1)}, u32[]{:S(2)}, u32[]{:S(2)}) collective-permute-start(f32[1,512]{1,0:T(1,128)S(1)} %get-tuple-element.139), channel_id=1, source_target_pairs={{8,0},{16,8},{24,16},{32,24},{40,32},{48,40},{56,48},{64,56},{72,6... | collective-permute-start | bytes 6152 | tf_op jit(solution)/shard_map/ppermute | solution.py:33
  355.1 5.3 %collective-permute-start.62 = (f32[2,1,512]{2,1,0:T(1,128)S(1)}, f32[2,1,512]{2,1,0:T(1,128)S(1)}, u32[]{:S(2)}, u32[]{:S(2)}) collective-permute-start(f32[2,1,512]{2,1,0:T(1,128)S(1)} %get-tuple-element.107), channel_id=1, source_target_pairs={{8,0},{16,8},{24,16},{32,24},{40,32},{48,40},{56,48},{64,56},{72,6... | collective-permute-start | bytes 12296 | tf_op jit(solution)/shard_map/ppermute | solution.py:33
  368.4 5.3 %collective-permute-start.66 = (f32[1,512]{1,0:T(1,128)S(1)}, f32[1,512]{1,0:T(1,128)S(1)}, u32[]{:S(2)}, u32[]{:S(2)}) collective-permute-start(f32[1,512]{1,0:T(1,128)S(1)} %get-tuple-element.137), channel_id=1, source_target_pairs={{8,0},{16,8},{24,16},{32,24},{40,32},{48,40},{56,48},{64,56},{72,6... | collective-permute-start | bytes 6152 | tf_op jit(solution)/shard_map/ppermute | solution.py:33
  381.8 5.3 %collective-permute-start.70 = (f32[2,1,512]{2,1,0:T(1,128)S(1)}, f32[2,1,512]{2,1,0:T(1,128)S(1)}, u32[]{:S(2)}, u32[]{:S(2)}) collective-permute-start(f32[2,1,512]{2,1,0:T(1,128)S(1)} %get-tuple-element.105), channel_id=1, source_target_pairs={{8,0},{16,8},{24,16},{32,24},{40,32},{48,40},{56,48},{64,56},{72,6... | collective-permute-start | bytes 12296 | tf_op jit(solution)/shard_map/ppermute | solution.py:33
  (275 shorter events, 187.5 us)
Async XLA Ops:
  7.2 184.2 %all-reduce.3.cloned.1.call-start = ((), (), s32[]{:S(2)}) async-start(), calls=%async_computation | async-start | bytes 1048576 | tf_op jit(solution)/shard_map/psum | solution.py:117
  11.3 10.5 %collective-permute-start.5 = (bf16[8,3,512]{2,0,1:T(8,128)(2,1)S(1)}, bf16[8,3,512]{2,0,1:T(8,128)(2,1)S(1)}, u32[]{:S(2)}, u32[]{:S(2)}) collective-permute-start(bf16[8,3,512]{2,0,1:T(8,128)(2,1)S(1)} %get-tuple-element.62), channel_id=1, source_target_pairs={{0,8},{8,16},{16,24},{24,32},{32,40},{40,48},{48,56},{56,64},{64,7... | collective-permute-start | bytes 73736 | tf_op jit(solution)/shard_map/ppermute | solution.py:32
  11.4 10.4 %collective-permute-start.6 = (bf16[8,3,512]{2,0,1:T(8,128)(2,1)S(1)}, bf16[8,3,512]{2,0,1:T(8,128)(2,1)S(1)}, u32[]{:S(2)}, u32[]{:S(2)}) collective-permute-start(bf16[8,3,512]{2,0,1:T(8,128)(2,1)S(1)} %get-tuple-element.63), channel_id=1, source_target_pairs={{8,0},{16,8},{24,16},{32,24},{40,32},{48,40},{56,48},{64,56},{72,6... | collective-permute-start | bytes 73736 | tf_op jit(solution)/shard_map/ppermute | solution.py:33
  16.7 120.3 %collective-permute-start = (f32[64,512]{1,0:T(8,128)}, f32[64,512]{1,0:T(8,128)}, u32[]{:S(2)}, u32[]{:S(2)}) collective-permute-start(f32[64,512]{1,0:T(8,128)} %get-tuple-element.44), channel_id=1, source_target_pairs={{0,1},{2,3},{4,5},{6,7},{8,9},{10,11},{12,13},{14,15},{16,17},{18,... | collective-permute-start | bytes 393224 | tf_op jit(solution)/shard_map/ppermute | solution.py:22
  22.0 20.2 %collective-permute-start.7 = (bf16[8,70,3]{2,0,1:T(8,128)(2,1)S(1)}, bf16[8,70,3]{2,0,1:T(8,128)(2,1)S(1)}, u32[]{:S(2)}, u32[]{:S(2)}) collective-permute-start(bf16[8,70,3]{2,0,1:T(8,128)(2,1)S(1)} %get-tuple-element.46), channel_id=1, source_target_pairs={{0,2},{2,4},{4,6},{6,0},{1,3},{3,5},{5,7},{7,1},{8,10},{10,12},{12... | collective-permute-start | bytes 10088 | tf_op jit(solution)/shard_map/ppermute | solution.py:32
  24.0 18.2 %collective-permute-start.8 = (bf16[8,70,3]{2,0,1:T(8,128)(2,1)S(1)}, bf16[8,70,3]{2,0,1:T(8,128)(2,1)S(1)}, u32[]{:S(2)}, u32[]{:S(2)}) collective-permute-start(bf16[8,70,3]{2,0,1:T(8,128)(2,1)S(1)} %get-tuple-element.47), channel_id=1, source_target_pairs={{2,0},{4,2},{6,4},{0,6},{3,1},{5,3},{7,5},{1,7},{10,8},{12,10},{14... | collective-permute-start | bytes 10088 | tf_op jit(solution)/shard_map/ppermute | solution.py:33
  138.4 6.8 %collective-permute-start.1 = (f32[4,1,512]{2,0,1:T(4,128)S(1)}, f32[4,1,512]{2,0,1:T(4,128)S(1)}, u32[]{:S(2)}, u32[]{:S(2)}) collective-permute-start(f32[4,1,512]{2,0,1:T(4,128)S(1)} %get-tuple-element.58), channel_id=1, source_target_pairs={{0,8},{8,16},{16,24},{24,32},{32,40},{40,48},{48,56},{56,64},{64,7... | collective-permute-start | bytes 24584 | tf_op jit(solution)/shard_map/ppermute | solution.py:32
  138.5 6.7 %collective-permute-start.2 = (f32[4,1,512]{2,0,1:T(4,128)S(1)}, f32[4,1,512]{2,0,1:T(4,128)S(1)}, u32[]{:S(2)}, u32[]{:S(2)}) collective-permute-start(f32[4,1,512]{2,0,1:T(4,128)S(1)} %get-tuple-element.59), channel_id=1, source_target_pairs={{8,0},{16,8},{24,16},{32,24},{40,32},{48,40},{56,48},{64,56},{72,6... | collective-permute-start | bytes 24584 | tf_op jit(solution)/shard_map/ppermute | solution.py:33
  159.8 6.8 %collective-permute-start.9 = (f32[1,512]{1,0:T(1,128)S(1)}, f32[1,512]{1,0:T(1,128)S(1)}, u32[]{:S(2)}, u32[]{:S(2)}) collective-permute-start(f32[1,512]{1,0:T(1,128)S(1)} %get-tuple-element.150), channel_id=1, source_target_pairs={{0,8},{8,16},{16,24},{24,32},{32,40},{40,48},{48,56},{56,64},{64,7... | collective-permute-start | bytes 6152 | tf_op jit(solution)/shard_map/ppermute | solution.py:32
  195.0 6.7 %collective-permute-start.13 = (f32[2,1,512]{2,1,0:T(1,128)S(1)}, f32[2,1,512]{2,1,0:T(1,128)S(1)}, u32[]{:S(2)}, u32[]{:S(2)}) collective-permute-start(f32[2,1,512]{2,1,0:T(1,128)S(1)} %get-tuple-element.118), channel_id=1, source_target_pairs={{0,8},{8,16},{16,24},{24,32},{32,40},{40,48},{48,56},{56,64},{64,7... | collective-permute-start | bytes 12296 | tf_op jit(solution)/shard_map/ppermute | solution.py:32
  195.1 6.7 %collective-permute-start.14 = (f32[2,1,512]{2,1,0:T(1,128)S(1)}, f32[2,1,512]{2,1,0:T(1,128)S(1)}, u32[]{:S(2)}, u32[]{:S(2)}) collective-permute-start(f32[2,1,512]{2,1,0:T(1,128)S(1)} %get-tuple-element.119), channel_id=1, source_target_pairs={{8,0},{16,8},{24,16},{32,24},{40,32},{48,40},{56,48},{64,56},{72,6... | collective-permute-start | bytes 12296 | tf_op jit(solution)/shard_map/ppermute | solution.py:33
  208.5 6.7 %collective-permute-start.17 = (f32[1,512]{1,0:T(1,128)S(1)}, f32[1,512]{1,0:T(1,128)S(1)}, u32[]{:S(2)}, u32[]{:S(2)}) collective-permute-start(f32[1,512]{1,0:T(1,128)S(1)} %get-tuple-element.148), channel_id=1, source_target_pairs={{0,8},{8,16},{16,24},{24,32},{32,40},{40,48},{48,56},{56,64},{64,7... | collective-permute-start | bytes 6152 | tf_op jit(solution)/shard_map/ppermute | solution.py:32
  221.9 6.7 %collective-permute-start.21 = (f32[2,1,512]{2,1,0:T(1,128)S(1)}, f32[2,1,512]{2,1,0:T(1,128)S(1)}, u32[]{:S(2)}, u32[]{:S(2)}) collective-permute-start(f32[2,1,512]{2,1,0:T(1,128)S(1)} %get-tuple-element.116), channel_id=1, source_target_pairs={{0,8},{8,16},{16,24},{24,32},{32,40},{40,48},{48,56},{56,64},{64,7... | collective-permute-start | bytes 12296 | tf_op jit(solution)/shard_map/ppermute | solution.py:32
  222.0 6.7 %collective-permute-start.22 = (f32[2,1,512]{2,1,0:T(1,128)S(1)}, f32[2,1,512]{2,1,0:T(1,128)S(1)}, u32[]{:S(2)}, u32[]{:S(2)}) collective-permute-start(f32[2,1,512]{2,1,0:T(1,128)S(1)} %get-tuple-element.117), channel_id=1, source_target_pairs={{8,0},{16,8},{24,16},{32,24},{40,32},{48,40},{56,48},{64,56},{72,6... | collective-permute-start | bytes 12296 | tf_op jit(solution)/shard_map/ppermute | solution.py:33
  234.9 6.7 %collective-permute-start.25 = (f32[1,512]{1,0:T(1,128)S(1)}, f32[1,512]{1,0:T(1,128)S(1)}, u32[]{:S(2)}, u32[]{:S(2)}) collective-permute-start(f32[1,512]{1,0:T(1,128)S(1)} %get-tuple-element.146), channel_id=1, source_target_pairs={{0,8},{8,16},{16,24},{24,32},{32,40},{40,48},{48,56},{56,64},{64,7... | collective-permute-start | bytes 6152 | tf_op jit(solution)/shard_map/ppermute | solution.py:32
  248.4 6.7 %collective-permute-start.29 = (f32[2,1,512]{2,1,0:T(1,128)S(1)}, f32[2,1,512]{2,1,0:T(1,128)S(1)}, u32[]{:S(2)}, u32[]{:S(2)}) collective-permute-start(f32[2,1,512]{2,1,0:T(1,128)S(1)} %get-tuple-element.114), channel_id=1, source_target_pairs={{0,8},{8,16},{16,24},{24,32},{32,40},{40,48},{48,56},{56,64},{64,7... | collective-permute-start | bytes 12296 | tf_op jit(solution)/shard_map/ppermute | solution.py:32
  248.5 6.7 %collective-permute-start.30 = (f32[2,1,512]{2,1,0:T(1,128)S(1)}, f32[2,1,512]{2,1,0:T(1,128)S(1)}, u32[]{:S(2)}, u32[]{:S(2)}) collective-permute-start(f32[2,1,512]{2,1,0:T(1,128)S(1)} %get-tuple-element.115), channel_id=1, source_target_pairs={{8,0},{16,8},{24,16},{32,24},{40,32},{48,40},{56,48},{64,56},{72,6... | collective-permute-start | bytes 12296 | tf_op jit(solution)/shard_map/ppermute | solution.py:33
  261.6 6.7 %collective-permute-start.33 = (f32[1,512]{1,0:T(1,128)S(1)}, f32[1,512]{1,0:T(1,128)S(1)}, u32[]{:S(2)}, u32[]{:S(2)}) collective-permute-start(f32[1,512]{1,0:T(1,128)S(1)} %get-tuple-element.144), channel_id=1, source_target_pairs={{0,8},{8,16},{16,24},{24,32},{32,40},{40,48},{48,56},{56,64},{64,7... | collective-permute-start | bytes 6152 | tf_op jit(solution)/shard_map/ppermute | solution.py:32
  275.2 6.7 %collective-permute-start.37 = (f32[2,1,512]{2,1,0:T(1,128)S(1)}, f32[2,1,512]{2,1,0:T(1,128)S(1)}, u32[]{:S(2)}, u32[]{:S(2)}) collective-permute-start(f32[2,1,512]{2,1,0:T(1,128)S(1)} %get-tuple-element.112), channel_id=1, source_target_pairs={{0,8},{8,16},{16,24},{24,32},{32,40},{40,48},{48,56},{56,64},{64,7... | collective-permute-start | bytes 12296 | tf_op jit(solution)/shard_map/ppermute | solution.py:32
  275.3 6.7 %collective-permute-start.38 = (f32[2,1,512]{2,1,0:T(1,128)S(1)}, f32[2,1,512]{2,1,0:T(1,128)S(1)}, u32[]{:S(2)}, u32[]{:S(2)}) collective-permute-start(f32[2,1,512]{2,1,0:T(1,128)S(1)} %get-tuple-element.113), channel_id=1, source_target_pairs={{8,0},{16,8},{24,16},{32,24},{40,32},{48,40},{56,48},{64,56},{72,6... | collective-permute-start | bytes 12296 | tf_op jit(solution)/shard_map/ppermute | solution.py:33
  288.3 6.7 %collective-permute-start.41 = (f32[1,512]{1,0:T(1,128)S(1)}, f32[1,512]{1,0:T(1,128)S(1)}, u32[]{:S(2)}, u32[]{:S(2)}) collective-permute-start(f32[1,512]{1,0:T(1,128)S(1)} %get-tuple-element.142), channel_id=1, source_target_pairs={{0,8},{8,16},{16,24},{24,32},{32,40},{40,48},{48,56},{56,64},{64,7... | collective-permute-start | bytes 6152 | tf_op jit(solution)/shard_map/ppermute | solution.py:32
  301.7 6.7 %collective-permute-start.45 = (f32[2,1,512]{2,1,0:T(1,128)S(1)}, f32[2,1,512]{2,1,0:T(1,128)S(1)}, u32[]{:S(2)}, u32[]{:S(2)}) collective-permute-start(f32[2,1,512]{2,1,0:T(1,128)S(1)} %get-tuple-element.110), channel_id=1, source_target_pairs={{0,8},{8,16},{16,24},{24,32},{32,40},{40,48},{48,56},{56,64},{64,7... | collective-permute-start | bytes 12296 | tf_op jit(solution)/shard_map/ppermute | solution.py:32
  301.8 6.7 %collective-permute-start.46 = (f32[2,1,512]{2,1,0:T(1,128)S(1)}, f32[2,1,512]{2,1,0:T(1,128)S(1)}, u32[]{:S(2)}, u32[]{:S(2)}) collective-permute-start(f32[2,1,512]{2,1,0:T(1,128)S(1)} %get-tuple-element.111), channel_id=1, source_target_pairs={{8,0},{16,8},{24,16},{32,24},{40,32},{48,40},{56,48},{64,56},{72,6... | collective-permute-start | bytes 12296 | tf_op jit(solution)/shard_map/ppermute | solution.py:33
  315.0 6.7 %collective-permute-start.49 = (f32[1,512]{1,0:T(1,128)S(1)}, f32[1,512]{1,0:T(1,128)S(1)}, u32[]{:S(2)}, u32[]{:S(2)}) collective-permute-start(f32[1,512]{1,0:T(1,128)S(1)} %get-tuple-element.140), channel_id=1, source_target_pairs={{0,8},{8,16},{16,24},{24,32},{32,40},{40,48},{48,56},{56,64},{64,7... | collective-permute-start | bytes 6152 | tf_op jit(solution)/shard_map/ppermute | solution.py:32
  328.3 6.7 %collective-permute-start.53 = (f32[2,1,512]{2,1,0:T(1,128)S(1)}, f32[2,1,512]{2,1,0:T(1,128)S(1)}, u32[]{:S(2)}, u32[]{:S(2)}) collective-permute-start(f32[2,1,512]{2,1,0:T(1,128)S(1)} %get-tuple-element.108), channel_id=1, source_target_pairs={{0,8},{8,16},{16,24},{24,32},{32,40},{40,48},{48,56},{56,64},{64,7... | collective-permute-start | bytes 12296 | tf_op jit(solution)/shard_map/ppermute | solution.py:32
  328.4 6.7 %collective-permute-start.54 = (f32[2,1,512]{2,1,0:T(1,128)S(1)}, f32[2,1,512]{2,1,0:T(1,128)S(1)}, u32[]{:S(2)}, u32[]{:S(2)}) collective-permute-start(f32[2,1,512]{2,1,0:T(1,128)S(1)} %get-tuple-element.109), channel_id=1, source_target_pairs={{8,0},{16,8},{24,16},{32,24},{40,32},{48,40},{56,48},{64,56},{72,6... | collective-permute-start | bytes 12296 | tf_op jit(solution)/shard_map/ppermute | solution.py:33
  341.4 6.7 %collective-permute-start.57 = (f32[1,512]{1,0:T(1,128)S(1)}, f32[1,512]{1,0:T(1,128)S(1)}, u32[]{:S(2)}, u32[]{:S(2)}) collective-permute-start(f32[1,512]{1,0:T(1,128)S(1)} %get-tuple-element.138), channel_id=1, source_target_pairs={{0,8},{8,16},{16,24},{24,32},{32,40},{40,48},{48,56},{56,64},{64,7... | collective-permute-start | bytes 6152 | tf_op jit(solution)/shard_map/ppermute | solution.py:32
  355.1 6.7 %collective-permute-start.61 = (f32[2,1,512]{2,1,0:T(1,128)S(1)}, f32[2,1,512]{2,1,0:T(1,128)S(1)}, u32[]{:S(2)}, u32[]{:S(2)}) collective-permute-start(f32[2,1,512]{2,1,0:T(1,128)S(1)} %get-tuple-element.106), channel_id=1, source_target_pairs={{0,8},{8,16},{16,24},{24,32},{32,40},{40,48},{48,56},{56,64},{64,7... | collective-permute-start | bytes 12296 | tf_op jit(solution)/shard_map/ppermute | solution.py:32
  355.1 6.7 %collective-permute-start.62 = (f32[2,1,512]{2,1,0:T(1,128)S(1)}, f32[2,1,512]{2,1,0:T(1,128)S(1)}, u32[]{:S(2)}, u32[]{:S(2)}) collective-permute-start(f32[2,1,512]{2,1,0:T(1,128)S(1)} %get-tuple-element.107), channel_id=1, source_target_pairs={{8,0},{16,8},{24,16},{32,24},{40,32},{48,40},{56,48},{64,56},{72,6... | collective-permute-start | bytes 12296 | tf_op jit(solution)/shard_map/ppermute | solution.py:33
  368.3 6.7 %collective-permute-start.65 = (f32[1,512]{1,0:T(1,128)S(1)}, f32[1,512]{1,0:T(1,128)S(1)}, u32[]{:S(2)}, u32[]{:S(2)}) collective-permute-start(f32[1,512]{1,0:T(1,128)S(1)} %get-tuple-element.136), channel_id=1, source_target_pairs={{0,8},{8,16},{16,24},{24,32},{32,40},{40,48},{48,56},{56,64},{64,7... | collective-permute-start | bytes 6152 | tf_op jit(solution)/shard_map/ppermute | solution.py:32
  381.7 6.7 %collective-permute-start.69 = (f32[2,1,512]{2,1,0:T(1,128)S(1)}, f32[2,1,512]{2,1,0:T(1,128)S(1)}, u32[]{:S(2)}, u32[]{:S(2)}) collective-permute-start(f32[2,1,512]{2,1,0:T(1,128)S(1)} %get-tuple-element.104), channel_id=1, source_target_pairs={{0,8},{8,16},{16,24},{24,32},{32,40},{40,48},{48,56},{56,64},{64,7... | collective-permute-start | bytes 12296 | tf_op jit(solution)/shard_map/ppermute | solution.py:32
  388.6 6.7 %collective-permute-start.71 = (f32[2,66,1]{2,1,0:T(8,128)S(1)}, f32[2,66,1]{2,1,0:T(8,128)S(1)}, u32[]{:S(2)}, u32[]{:S(2)}) collective-permute-start(f32[2,66,1]{2,1,0:T(8,128)S(1)} %get-tuple-element.88), channel_id=1, source_target_pairs={{0,2},{2,4},{4,6},{6,0},{1,3},{3,5},{5,7},{7,1},{8,10},{10,12},{12... | collective-permute-start | bytes 1592 | tf_op jit(solution)/shard_map/ppermute | solution.py:32
  (59 other events, 390.6 us)
Sparse Core Ops, SparseCore 0:
  155.6 35.6 all-reduce.2
where the time goes:
time: 407 us; the launch traced here: 404 us
  starting transfers between devices  162 us (40%)
  matrix products  95.8 us (24%)
  waiting for transfers between devices  83 us (20%)
  other arithmetic  45.4 us (11%)
  between operations  15.4 us (4%)
    ppermute x36, starting transfers between devices, extended(): after = lax.ppermute(leading, axis, down)  130 us
    dot_general x27, matrix products, conv_layer(): jnp.einsum('io,ixy->oxy', weight[offset], window, preferred_element_type=...  95.8 us
    ppermute x36, waiting for transfers between devices, extended(): before = lax.ppermute(last, axis, up)  58 us
    ppermute x36, starting transfers between devices, extended(): before = lax.ppermute(last, axis, up)  26.9 us
    psum x1, waiting for transfers between devices, local(): lax.psum((jnp.sum(weights_col * tend_east, 0), jnp.sum(weights_col * tend...  19.4 us
    another operation x1, other arithmetic, local(): partial_load = jnp.cumsum(weighted, 0) - 0.5 * weighted  15.3 us
    another operation x9, other arithmetic, local(): fluxes = jnp.stack([relative * east_bar, relative * north_bar])  9.97 us
  transfers between devices with their start and end apart: 74, of which 48 were waited for; matrix products, arithmetic and copies ran while one was open for 29% of the time, Pallas kernels for 0%

commit v1 on v0

v1 whole, which is shorter than its diff:
```python
import functools

import jax
import jax.numpy as jnp
from jax import lax
from jax.experimental import pallas as pl
from jax.experimental.pallas import tpu as pltpu
from jax.sharding import PartitionSpec as P

NSUB = 8
TX, TY = 64, 512
LANES = 640
ROWS = 104
TOP = 20
EDGE = 18
FIELDS = 14
F32 = jnp.float32
BF = jnp.bfloat16

coriolis_base = 0.6
coriolis_slope = 0.8
press_coef = 0.3
drag_coef = 0.5
step_dt = 0.2
closure_coef = 0.5
gravity = 1.0
sub_dt = 0.4
TOTAL_DEPTH = 15.0

VMEM = pl.BlockSpec(memory_space=pltpu.VMEM)
SMEM = pl.BlockSpec(memory_space=pltpu.SMEM)
PARAMS = pltpu.CompilerParams(vmem_limit_bytes=48 * 2**20)


def sds(shape, dtype=F32):
    return jax.ShapeDtypeStruct(shape, dtype)


def wet_of(bl, level):
    return jnp.where(bl > level, 1.0, 0.0)


def latitudes(lat, shape):
    lane = lax.broadcasted_iota(jnp.int32, shape, len(shape) - 1)
    return lat * TY + jnp.where(lane < TY + 64, lane, lane - LANES)


def inside_of(lat, total, shape):
    y = latitudes(lat, shape)
    return jnp.where((y >= 0) & (y < total), 1.0, 0.0)


def pack_lat(sc, u0, v0, b0, l0, s0, u3, v3, b3, l3, s3, to_down, to_up):
    base = 4 * sc[0]
    lane = lax.broadcasted_iota(jnp.int32, (TX, 128), 1)

    def fields(u, v, b, l, s):
        bl = l[...].astype(F32)
        wets = [wet_of(bl, (base + k).astype(F32)) for k in range(4)]
        for a in (u, v, b):
            for k in range(4):
                yield a[k] * wets[k]
        yield bl
        yield s[...]

    for out, args, origin in ((to_down, (u0, v0, b0, l0, s0), 0), (to_up, (u3, v3, b3, l3, s3), 128 - EDGE)):
        for i, field in enumerate(fields(*args)):
            tile, place = divmod(i, 7)
            if place == 0:
                acc = jnp.zeros((TX, 128), F32)
            moved = pltpu.roll(field, (EDGE * place - origin) % 128, 1)
            acc = jnp.where((lane >= EDGE * place) & (lane < EDGE * (place + 1)), moved, acc)
            if place == 6:
                out[tile] = acc.astype(BF)


def pack_lon(sc, before, after, *refs):
    tops, bots, extra_t, extra_b = refs[0:5], refs[5:10], refs[10:13], refs[13:16]
    hal, to_down, to_up, work = refs[16:]
    base = 4 * sc[0]
    lane = lax.broadcasted_iota(jnp.int32, (TX, 128), 1)
    for tile in range(2):
        low, high = before[tile].astype(F32), after[tile].astype(F32)
        for place in range(7):
            a = pltpu.roll(high, (-EDGE * place) % 128, 1)
            b = pltpu.roll(low, (128 - EDGE - EDGE * place) % 128, 1)
            hal[tile * 7 + place] = jnp.where(lane < EDGE, a, jnp.where(lane >= 128 - EDGE, b, 0.0))
    for out, (u, v, b, l, s), row in ((to_down, tops, 0), (to_up, bots, TX - 16)):
        bl = l[...].astype(F32)
        for k in range(4):
            wet = wet_of(bl, (base + k).astype(F32))
            for n, a in enumerate((u, v, b)):
                out[4 * n + k, :, :TY] = (a[k] * wet).astype(BF)
        out[12, :, :TY] = bl.astype(BF)
        out[13, :, :TY] = s[...].astype(BF)
        for i in range(FIELDS):
            out[i, :, TY:] = hal[i, row : row + 16, :].astype(BF)
    for out, (u, v, l), first, row in ((to_down, extra_t, 0, 16), (to_up, extra_b, 6, 46)):
        bl = l[first : first + 2, :].astype(F32)
        for k in range(4):
            wet = wet_of(bl, (base + k).astype(F32))
            for n, a in enumerate((u, v)):
                work[2 * (4 * n + k) : 2 * (4 * n + k) + 2, :TY] = a[k, first : first + 2, :] * wet
        for i in range(8):
            work[2 * i : 2 * i + 2, TY:] = hal[i, row : row + 2, :]
        out[14] = work[...].astype(BF)


def build_weights(w_in, b_in, w_mid, b_mid, w_out, w1, w2, w3, b1, b2, spread):
    def across(parts, rows, cols):
        rows_all = sum(p.shape[0] for p in parts)
        full = jnp.concatenate(parts + [jnp.zeros((128 - rows_all, 128), F32)], 0)
        return full.T[:rows, :]

    def wide(a):
        return jnp.concatenate([a, jnp.zeros((a.shape[0], 128 - a.shape[1]), F32)], 1)

    zero8 = jnp.zeros((8, 128), F32)
    parts = []
    for a in range(3):
        parts += [wide(w_in[3 * a + b].astype(F32)) for b in range(3)] + [zero8]
    first = across(parts, 32, 96)
    first = jnp.concatenate([first, jnp.zeros((32, 128), F32)], 1)
    for p in range(6):
        w1[32 * p : 32 * p + 32, :] = pltpu.roll(first, 32 * p, 1).astype(BF)
    for b in range(3):
        mid = across([wide(w_mid[3 * a + b].astype(F32)) for a in range(3)], 32, 96)
        mid = jnp.concatenate([mid, jnp.zeros((32, 128), F32)], 1)
        for p in range(6):
            w2[192 * b + 32 * p : 192 * b + 32 * p + 32, :] = pltpu.roll(mid, 32 * p, 1).astype(BF)
        last = across([wide(w_out[3 * a + b].astype(F32)) for a in range(3)], 8, 96)
        last = jnp.concatenate([last, jnp.zeros((8, 256), F32)], 1)
        for p in range(8):
            spread[:, p, :] = pltpu.roll(last, 32 * p, 1)
        w3[64 * b : 64 * b + 64, :] = spread[...].reshape(64, 384)[:, :320].astype(BF)
    eye = lax.broadcasted_iota(jnp.int32, (32, 32), 0) == lax.broadcasted_iota(jnp.int32, (32, 32), 1)
    for src, dst in ((b_in, b1), (b_mid, b2)):
        column = jnp.sum(jnp.where(eye, src[...], 0.0), 1, keepdims=True)
        for p in range(6):
            dst[32 * p : 32 * p + 32, :] = jnp.broadcast_to(column, (32, 128))


def load_slots(up, start, count, in0):
    def one(s, _):
        c = up[:, start + s, :]
        r = pl.multiple_of(s * 32, 32)
        in0[pl.ds(r, 16), :] = jnp.concatenate([pltpu.roll(c, 1, 1), c], 0).astype(BF)
        in0[pl.ds(r + 16, 16), :] = jnp.concatenate([pltpu.roll(c, LANES - 1, 1), jnp.zeros_like(c)], 0).astype(BF)
        return 0

    lax.fori_loop(0, count, one, 0, unroll=2)


def closure(in0, act1, act2, weights, inside, n1, n2, n3, shift, store, unroll):
    w1, w2, w3, b1, b2 = weights
    bias1, bias2 = b1[:, :1], b2[:, :1]

    def combined(o, m):
        return pltpu.roll(o[:m], 1, 1) + o[m : 2 * m] + pltpu.roll(o[2 * m :], LANES - 1, 1)

    def first(j, _):
        x = in0[pl.ds(pl.multiple_of(j * 192, 64), 256), :]
        o = jnp.dot(w1[...], x, preferred_element_type=F32)
        act1[pl.ds(pl.multiple_of(j * 192, 64), 192), :] = (jnp.maximum(o + bias1, 0.0) * inside).astype(BF)
        return 0

    def second(j, _):
        x = act1[pl.ds(pl.multiple_of(j * 192, 64), 256), :]
        o = combined(jnp.dot(w2[...], x, preferred_element_type=F32), 192)
        o = (jnp.maximum(o + bias2, 0.0) * inside).astype(BF)
        act2[pl.ds(pl.multiple_of(j * 192 + 32 * shift, 32), 192), :] = o
        return 0

    def third(j, _):
        x = act2[pl.ds(pl.multiple_of(j * 256, 256), 320), :]
        o = combined(jnp.dot(w3[...], x, preferred_element_type=F32), 64)
        store(j, (closure_coef * o).astype(BF).astype(F32).reshape(8, 8, LANES))
        return 0

    lax.fori_loop(0, n1, first, 0, unroll=unroll)
    lax.fori_loop(0, n2, second, 0, unroll=unroll)
    lax.fori_loop(0, n3, third, 0, unroll=min(unroll, n3))


def interior(total, sc, u, v, bl, hal, w1, w2, w3, b1, b2, out, up, in0, act1, act2):
    @pl.when(sc[0] == 0)
    def _():
        level = bl[...].astype(F32)
        for k in range(4):
            wet = wet_of(level, float(k))
            up[k, :, :TY] = u[k] * wet
            up[4 + k, :, :TY] = v[k] * wet
        for i in range(8):
            up[i, :, TY:] = hal[i]
        load_slots(up, 1, 62, in0)
        act1[1920:1984, :] = jnp.zeros((64, LANES), BF)
        inside = inside_of(sc[1], total, (1, LANES))

        def store(j, f):
            out[:, pl.ds(pl.multiple_of(8 * j, 8), 8), :] = f

        closure(in0, act1, act2, (w1, w2, w3, b1, b2), inside, 10, 10, 7, 0, store, 5)

    @pl.when(sc[0] != 0)
    def _():
        out[...] = jnp.zeros_like(out)


def assemble(sc, u, v, b, bl, s, hal, low, high, ext):
    base = 4 * sc[0]
    level = bl[...].astype(F32)
    for i in range(FIELDS):
        ext[i, 0:8, :] = jnp.zeros((8, LANES), F32)
        ext[i, 96:104, :] = jnp.zeros((8, LANES), F32)
        ext[i, 4:20, :] = low[i].astype(F32)
        ext[i, 84:100, :] = high[i].astype(F32)
        ext[i, 20:84, TY:] = hal[i]
    for k in range(4):
        wet = wet_of(level, (base + k).astype(F32))
        for n, a in enumerate((u, v, b)):
            ext[4 * n + k, 20:84, :TY] = a[k] * wet
    ext[12, 20:84, :TY] = level
    ext[13, 20:84, :TY] = s[...]
    more_low, more_high = low[14].astype(F32), high[14].astype(F32)
    for i in range(8):
        ext[i, 2:4, :] = more_low[2 * i : 2 * i + 2, :]
        ext[i, 100:102, :] = more_high[2 * i : 2 * i + 2, :]


def pressures(base, ext, pr, load, rows):
    for r in range(0, rows, 8):
        run = jnp.zeros((8, LANES), F32)
        for k in range(4):
            weighted = ext[8 + k, r : r + 8, :] * (1.0 + 0.25 * (base + k).astype(F32))
            pr[k, r + 8 : r + 16, :] = run + 0.5 * weighted
            run = run + weighted
        load[r + 8 : r + 16, :] = run


def grads(ref, r):
    here = ref[r + 8 : r + 16, :]
    gx = (ref[r + 9 : r + 17, :] - ref[r + 7 : r + 15, :]) * 0.5
    gy = (pltpu.roll(here, LANES - 1, 1) - pltpu.roll(here, 1, 1)) * 0.5
    return gx, gy


def column_sums(total, sc, u, v, b, bl, s, hal, low, high, sums, early, two, edge, ext, pr, load):
    assemble(sc, u, v, b, bl, s, hal, low, high, ext)
    base = 4 * sc[0]
    upper = jnp.where(sc[0] == 0, 1.0, 0.0)
    pr4 = [pr.at[k] for k in range(4)]
    for ref in pr4 + [load]:
        ref[0:8, :] = jnp.zeros((8, LANES), F32)
        ref[ROWS + 8 : ROWS + 16, :] = jnp.zeros((8, LANES), F32)
    pressures(base, ext, pr, load, ROWS)
    y = latitudes(sc[1], (8, LANES)).astype(F32)
    coriolis = coriolis_base + coriolis_slope * (y * (1.0 / total) - 0.5)
    for r in range(0, ROWS, 8):
        rr = slice(r, r + 8)
        level = ext[12, rr, :]
        te = jnp.zeros((8, LANES), F32)
        tn, us, vs = te, te, te
        for k in range(4):
            number = (base + k).astype(F32)
            thick = 1.0 + 0.25 * number
            weight = jnp.where(level > number, thick, 0.0)
            drag = jnp.where(level == number + 1.0, drag_coef, 0.0)
            east, north = ext[k, rr, :], ext[4 + k, rr, :]
            gx, gy = grads(pr4[k], r)
            te = te + weight * (coriolis * north - press_coef * gx - drag * east)
            tn = tn + weight * (-coriolis * east - press_coef * gy - drag * north)
            us = us + thick * east
            vs = vs + thick * north
        below = jnp.zeros((8, LANES), F32)
        for k in range(4, 8):
            below = below + jnp.where(level > float(k), 1.0 + 0.25 * k, 0.0)
        gx, gy = grads(load, r)
        below = below * (press_coef * upper)
        sums[0, rr, :] = te - below * gx
        sums[1, rr, :] = tn - below * gy
        sums[2, rr, :] = us
        sums[3, rr, :] = vs
        for i, a in enumerate((us, vs, gx, gy)):
            early[i, rr, :] = a.astype(BF)
        two[0, rr, :] = level
        two[1, rr, :] = ext[13, rr, :]
    edge[:, 0:32, :] = ext[0:8, 0:32, :]
    edge[:, 32:64, :] = ext[0:8, 72:104, :]


def edges(total, sc, edge, inner, two, sums, w1, w2, w3, b1, b2, out, force, in0, act1, act2):
    @pl.when(sc[0] == 0)
    def _():
        inside = inside_of(sc[1], total, (1, LANES))
        for side, (start, shift) in enumerate(((2, 5), (37, 0))):
            load_slots(edge, start, 26, in0)
            act1[768:832, :] = jnp.zeros((64, LANES), BF)
            act2[...] = jnp.zeros_like(act2)

            def store(j, f, side=side):
                force[:, pl.ds(pl.multiple_of(8 * j + 24 * side, 8), 8), :] = f

            closure(in0, act1, act2, (w1, w2, w3, b1, b2), inside, 4, 4, 3, shift, store, 4)
        for r in range(0, ROWS, 8):
            rr = slice(r, r + 8)
            level = two[0, rr, :]
            te, tn = sums[0, rr, :], sums[1, rr, :]
            for k in range(4):
                weight = jnp.where(level > float(k), 1.0 + 0.25 * k, 0.0)
                if r < 24:
                    fe, fn = force[k, rr, :], force[4 + k, rr, :]
                elif r >= 80:
                    fe, fn = force[k, r - 56 : r - 48, :], force[4 + k, r - 56 : r - 48, :]
                else:
                    fe, fn = inner[k, r - 24 : r - 16, :], inner[4 + k, r - 24 : r - 16, :]
                te = te + weight * fe
                tn = tn + weight * fn
            out[0, rr, :] = te
            out[1, rr, :] = tn

    @pl.when(sc[0] != 0)
    def _():
        out[...] = sums[0:2]
        force[...] = jnp.zeros_like(force)


def own_part(total, sc, u, v, b, bl, hal, low, high, inner, force, out, pb, pr, load):
    base = 4 * sc[0]
    level = bl[...].astype(F32)
    for k in range(4):
        number = (base + k).astype(F32)
        pb[8 + k, 0:8, :] = low[8 + k, 8:16, :].astype(F32)
        pb[8 + k, 72:80, :] = high[8 + k, 0:8, :].astype(F32)
        pb[8 + k, 8:72, :TY] = b[k] * wet_of(level, number)
        pb[8 + k, 8:72, TY:] = hal[8 + k]
    pressures(base, pb, pr, load, 80)
    y = latitudes(sc[1], (8, LANES)).astype(F32)
    coriolis = (coriolis_base + coriolis_slope * (y * (1.0 / total) - 0.5))[:, :TY]
    for r in range(0, TX, 8):
        rr = slice(r, r + 8)
        lev = bl[rr, :].astype(F32)
        for k in range(4):
            number = (base + k).astype(F32)
            wet = wet_of(lev, number)
            drag = jnp.where(lev == number + 1.0, drag_coef, 0.0)
            east, north = u[k, rr, :], v[k, rr, :]
            gx, gy = grads(pr.at[k], r + 8)
            r20 = r + TOP

            def forcing(c):
                pieces, at = [], r20
                while at < r20 + 8:
                    if at < 24:
                        end, piece = min(24, r20 + 8), lambda s, e: force[c, s:e, :TY]
                    elif at < 80:
                        end, piece = min(80, r20 + 8), lambda s, e: inner[c, s - 24 : e - 24, :TY]
                    else:
                        end, piece = r20 + 8, lambda s, e: force[c, s - 56 : e - 56, :TY]
                    pieces.append(piece(at, end))
                    at = end
                return pieces[0] if len(pieces) == 1 else jnp.concatenate(pieces, 0)

            te = coriolis * north - press_coef * gx[:, :TY] + forcing(k) - drag * east
            tn = -coriolis * east - press_coef * gy[:, :TY] + forcing(4 + k) - drag * north
            out[k, rr, :] = wet * (east + step_dt * te)
            out[4 + k, rr, :] = wet * (north + step_dt * tn)


def finish(total, sc, two, mine, theirs, sums, early, own, east_out, north_out, surface_out, lv, fx, fy, eb, nb, ae, an, rel, c2):
    upper = jnp.where(sc[0] == 0, 0.0, 1.0)
    zero8 = jnp.zeros((8, LANES), F32)
    for ref in (lv, fx):
        ref[0:8, :] = zero8
        ref[ROWS + 8 : ROWS + 16, :] = zero8
    for r in range(0, ROWS, 8):
        rr = slice(r, r + 8)
        level = two[0, rr, :]
        depth = level + 0.125 * level * (level - 1.0)
        over = 1.0 / jnp.maximum(depth, 1.0)
        rel[rr, :] = depth * (1.0 / TOTAL_DEPTH)
        c2[rr, :] = jnp.where(level > 0.0, 0.5 * sub_dt * gravity, 0.0)
        ae[rr, :] = sub_dt * (mine[0, rr, :] + theirs[0, rr, :]) * over
        an[rr, :] = sub_dt * (mine[1, rr, :] + theirs[1, rr, :]) * over
        eb[rr, :] = (sums[2, rr, :] + early[0, rr, :].astype(F32)) * over
        nb[rr, :] = (sums[3, rr, :] + early[1, rr, :].astype(F32)) * over
        lv[r + 8 : r + 16, :] = two[1, rr, :]
    inside = inside_of(sc[1], total, (8, LANES)) * 1.0

    def step(_, carry):
        for r in range(0, ROWS, 8):
            rr = slice(r, r + 8)
            here = lv[r + 8 : r + 16, :]
            dx = lv[r + 9 : r + 17, :] - lv[r + 7 : r + 15, :]
            dy = pltpu.roll(here, LANES - 1, 1) - pltpu.roll(here, 1, 1)
            c = c2[rr, :]
            e = eb[rr, :] + (ae[rr, :] - c * dx)
            n = nb[rr, :] + (an[rr, :] - c * dy)
            eb[rr, :] = e
            nb[rr, :] = n
            fx[r + 8 : r + 16, :] = rel[rr, :] * e
            fy[rr, :] = rel[rr, :] * n
        for r in range(0, ROWS, 8):
            rr = slice(r, r + 8)
            dx = fx[r + 9 : r + 17, :] - fx[r + 7 : r + 15, :]
            f = fy[rr, :]
            dy = pltpu.roll(f, LANES - 1, 1) - pltpu.roll(f, 1, 1)
            lv[r + 8 : r + 16, :] = inside * (lv[r + 8 : r + 16, :] - (0.5 * sub_dt) * (dx + dy))
        return carry

    lax.fori_loop(0, NSUB, step, 0)
    base = 4 * sc[0]
    for r in range(TOP, TOP + TX, 8):
        rr, at = slice(r, r + 8), slice(r - TOP, r - TOP + 8)
        level = two[0, rr, :TY]
        depth = level + 0.125 * level * (level - 1.0)
        over = 1.0 / jnp.maximum(depth, 1.0)
        back = (step_dt * press_coef) * upper
        gx, gy = early[2, rr, :TY].astype(F32), early[3, rr, :TY].astype(F32)
        estart = (sums[2, rr, :TY] + early[0, rr, :TY].astype(F32)) * over
        nstart = (sums[3, rr, :TY] + early[1, rr, :TY].astype(F32)) * over
        fe = eb[rr, :TY] - estart - (step_dt / sub_dt) * ae[rr, :TY] - back * gx
        fn = nb[rr, :TY] - nstart - (step_dt / sub_dt) * an[rr, :TY] - back * gy
        for k in range(4):
            wet = wet_of(level, (base + k).astype(F32))
            east_out[k, at, :] = own[k, at, :] + wet * fe
            north_out[k, at, :] = own[4 + k, at, :] + wet * fn
        surface_out[at, :] = lv[r + 8 : r + 16, :TY]


def call(kernel, name, out_shape, n_in, scratch=(), in_specs=None, cost=None, grid=()):
    single = not isinstance(out_shape, (list, tuple))
    return pl.pallas_call(
        kernel,
        name=name,
        grid=grid,
        out_shape=out_shape,
        in_specs=in_specs or [SMEM] + [VMEM] * (n_in - 1),
        out_specs=VMEM if single else [VMEM] * len(out_shape),
        scratch_shapes=list(scratch),
        compiler_params=PARAMS,
        cost_estimate=cost,
    )


def micros(us):
    return pl.CostEstimate(flops=int(us * 1e6), bytes_accessed=int(us * 3e6), transcendentals=0)


def shifted(x, axis, by, ring):
    size = lax.axis_size(axis)
    pairs = [(i, (i + by) % size) for i in range(size) if ring or 0 <= i + by < size]
    return lax.ppermute(x, axis, pairs)


def local(u, v, b, wet_mask, bl, s, w_in, b_in, w_mid, b_mid, w_out):
    total = TY * lax.axis_size("lat")
    sc = jnp.stack([lax.axis_index("grp"), lax.axis_index("lat")]).astype(jnp.int32)

    def lanes(i):
        return [pl.BlockSpec((4, TX, 128), lambda _: (0, 0, i))] * 3 + [pl.BlockSpec((TX, 128), lambda _: (0, i))] * 2

    half = sds((2, TX, 128), BF)
    to_down, to_up = call(pack_lat, "pack_lat", [half, half], 11, in_specs=[SMEM] + lanes(0) + lanes(3), grid=(1,))(
        sc, u, v, b, bl, s, u, v, b, bl, s
    )
    before = shifted(to_up, "lat", 1, False)
    after = shifted(to_down, "lat", -1, False)
    vb = [sds((192, 256), BF), sds((576, 256), BF), sds((192, 320), BF), sds((192, 128)), sds((192, 128))]
    weights = call(build_weights, "weights", vb, 5, [pltpu.VMEM((8, 8, 384), F32)], in_specs=[VMEM] * 5)(
        w_in, b_in[None, :], w_mid, b_mid[None, :], w_out
    )

    def rows(n, i, three):
        return [pl.BlockSpec((4, n, TY), lambda _: (0, i, 0))] * three + [pl.BlockSpec((n, TY), lambda _: (i, 0))] * (three - 1)

    out = sds((15, 16, LANES), BF)
    hal, down, up = call(
        pack_lon,
        "pack_lon",
        [sds((FIELDS, TX, 128)), out, out],
        19,
        [pltpu.VMEM((16, LANES), F32)],
        in_specs=[SMEM, VMEM, VMEM] + rows(16, 0, 3) + rows(16, 3, 3) + rows(8, 2, 2) + rows(8, 5, 2),
        grid=(1,),
    )(sc, before, after, u, v, b, bl, s, u, v, b, bl, s, u, v, bl, u, v, bl)
    low = shifted(up, "lon", 1, True)
    high = shifted(down, "lon", -1, True)
    inner = call(
        functools.partial(interior, total),
        "interior",
        sds((8, 56, LANES)),
        10,
        [
            pltpu.VMEM((8, TX, LANES), F32),
            pltpu.VMEM((62 * 32, LANES), BF),
            pltpu.VMEM((62 * 32, LANES), BF),
            pltpu.VMEM((60 * 32, LANES), BF),
        ],
        cost=micros(6),
    )(sc, u, v, bl, hal, *weights)
    ext2 = sds((2, ROWS, LANES))
    sums, early, two, edge = call(
        functools.partial(column_sums, total),
        "column_sums",
        [sds((4, ROWS, LANES)), sds((4, ROWS, LANES), BF), ext2, sds((8, 64, LANES))],
        9,
        [
            pltpu.VMEM((FIELDS, ROWS, LANES), F32),
            pltpu.VMEM((4, ROWS + 16, LANES), F32),
            pltpu.VMEM((ROWS + 16, LANES), F32),
        ],
        cost=micros(3),
    )(sc, u, v, b, bl, s, hal, low, high)
    early_in = shifted(early, "grp", 1, True)
    mine, force = call(
        functools.partial(edges, total),
        "edges",
        [ext2, sds((8, 48, LANES))],
        10,
        [pltpu.VMEM((26 * 32, LANES), BF), pltpu.VMEM((26 * 32, LANES), BF), pltpu.VMEM((29 * 32, LANES), BF)],
        cost=micros(5),
    )(sc, edge, inner, two, sums, *weights)
    theirs = shifted(mine, "grp", 1, True)
    own = call(
        functools.partial(own_part, total),
        "own_part",
        sds((8, TX, TY)),
        10,
        [pltpu.VMEM((12, 80, LANES), F32), pltpu.VMEM((4, 96, LANES), F32), pltpu.VMEM((96, LANES), F32)],
        cost=micros(3),
    )(sc, u, v, b, bl, hal, low, high, inner, force)
    plane = pltpu.VMEM((ROWS, LANES), F32)
    tall = pltpu.VMEM((ROWS + 16, LANES), F32)
    return tuple(
        call(
            functools.partial(finish, total),
            "finish",
            [sds((4, TX, TY)), sds((4, TX, TY)), sds((TX, TY))],
            7,
            [tall, tall, plane, plane, plane, plane, plane, plane, plane],
            cost=micros(5),
        )(sc, two, mine, theirs, sums, early_in, own)
    )


def solution(mesh):
    tile = P("grp", "lon", "lat")
    flat = P("lon", "lat")
    return jax.shard_map(
        local,
        mesh=mesh,
        in_specs=(tile, tile, tile, tile, flat, flat, P(), P(), P(), P(), P()),
        out_specs=(tile, tile, flat),
        check_vma=False,
    )
```

time: 407 us -> 74.9 us (0.18)
  starting transfers between devices: 162 us -> 12.8 us
  matrix products: 95.8 us -> 0 us
  waiting for transfers between devices: 83 us -> 24.3 us
  other arithmetic: 45.4 us -> 0.08 us
  Pallas kernels: 0 us -> 31.3 us
  between operations: 15.4 us -> 0.88 us
    ppermute x73 -> x6, starting transfers between devices: 162 us -> 12.8 us  [shifted(): return lax.ppermute(x, axis, pairs)]
    dot_general x27 -> x0, matrix products: 95.8 us -> none  [conv_layer(): jnp.einsum('io,ixy->oxy', weight[offset], window, preferred_element_type=...]
    ppermute x73 -> x6, waiting for transfers between devices: 63.6 us -> 24.3 us  [shifted(): return lax.ppermute(x, axis, pairs)]
    pallas_call x0 -> x8, Pallas kernels: none -> 31.3 us  [the longest x1 10.5 us: local(): call(functools.partial(interior, total), 'interior', sds((8, 56, LANES)),...]
    another operation x10 -> x1, other arithmetic: 25.3 us -> 0.08 us  [local(): jnp.stack([lax.axis_index('grp'), lax.axis_index('lat')]).astype(jnp.int32)]
    psum x1 -> x0, waiting for transfers between devices: 19.4 us -> none  [local(): lax.psum((jnp.sum(weights_col * tend_east, 0), jnp.sum(weights_col * tend...]
    reduce_sum x4 -> x0, other arithmetic: 8.13 us -> none  [the longest x1 3.97 us: local(): above = passed_along(jnp.sum(weighted, 0), 'grp', 1)]
    mul x18 -> x0, other arithmetic: 4.72 us -> none  [the longest x8 1.64 us: local(): rim_flux = extended(fluxes, (('lon', 1), ('lat', 2)), 1) * inside_rows(1)]
  transfers between devices with their start and end apart: 74 -> 6, of which waited for: 48 -> 3; matrix products, arithmetic and copies ran while one was open for 29% -> 0% of each run, Pallas kernels for 0% -> 16%
where the time goes in v1:
time: 74.9 us; the launch traced here: 74.5 us
  Pallas kernels  31.3 us (42%)
  waiting for transfers between devices  24.3 us (32%)
  starting transfers between devices  12.8 us (17%)
  local copies, waits for them, and re-layouts  5.1 us (7%)
  between operations  0.88 us (1%)
    ppermute x6, waiting for transfers between devices, shifted(): return lax.ppermute(x, axis, pairs)  24.3 us
    ppermute x6, starting transfers between devices, shifted(): return lax.ppermute(x, axis, pairs)  12.8 us
    pallas_call x1, Pallas kernels, local(): call(functools.partial(interior, total), 'interior', sds((8, 56, LANES)),...  10.5 us
    pallas_call x1, Pallas kernels, local(): call(functools.partial(edges, total), 'edges', [ext2, sds((8, 48, LANES))...  8.61 us
    unnamed x31, local copies, waits for them, and re-layouts  5.1 us
    pallas_call x1, Pallas kernels, local(): call(functools.partial(finish, total), 'finish', [sds((4, TX, TY)), sds((...  4.94 us
    pallas_call x1, Pallas kernels, local(): call(functools.partial(column_sums, total), 'column_sums', [sds((4, ROWS,...  3.93 us
    pallas_call x1, Pallas kernels, local(): call(functools.partial(own_part, total), 'own_part', sds((8, TX, TY)), 10...  1.53 us
  transfers between devices with their start and end apart: 6, of which 3 were waited for; matrix products, arithmetic and copies ran while one was open for 0% of the time, Pallas kernels for 16%

profile of v1, /device:TPU:0, one launch (start us, length us, event | category | flops | bytes accessed | tf_op | source)
XLA Modules:
  0.0 74.5 jit_solution(3438057878925073025)
XLA Ops:
  0.6 0.1 pad_add_fusion.sc
  0.7 1.0 %copy-done = f32[4,64,512]{2,1,0:T(8,128)S(1)} copy-done((f32[4,64,512]{2,1,0:T(8,128)S(1)}, f32[4,64,512]{2,1,0:T(8,128)}, u32[]{:S(2)}) %copy-start) | copy-done | bytes 524312
  1.8 1.0 %copy-done.2 = f32[4,64,512]{2,1,0:T(8,128)S(1)} copy-done((f32[4,64,512]{2,1,0:T(8,128)S(1)}, f32[4,64,512]{2,1,0:T(8,128)}, u32[]{:S(2)}) %copy-start.2) | copy-done | bytes 524312
  2.8 1.0 %copy-done.4 = f32[4,64,512]{2,1,0:T(8,128)S(1)} copy-done((f32[4,64,512]{2,1,0:T(8,128)S(1)}, f32[4,64,512]{2,1,0:T(8,128)}, u32[]{:S(2)}) %copy-start.4) | copy-done | bytes 524312
  3.8 0.9 %copy-done.6 = s32[64,512]{1,0:T(8,128)S(1)} copy-done((s32[64,512]{1,0:T(8,128)S(1)}, s32[64,512]{1,0:T(8,128)}, u32[]{:S(2)}) %copy-start.6) | copy-done | bytes 131096
  4.7 0.9 %copy-done.8 = f32[64,512]{1,0:T(8,128)S(1)} copy-done((f32[64,512]{1,0:T(8,128)S(1)}, f32[64,512]{1,0:T(8,128)}, u32[]{:S(2)}) %copy-start.8) | copy-done | bytes 131096
  5.6 0.7 pack_lat.1
  6.4 3.9 %collective-permute-start = (bf16[2,64,128]{2,1,0:T(8,128)(2,1)S(1)}, bf16[2,64,128]{2,1,0:T(8,128)(2,1)S(1)}, u32[]{:S(2)}, u32[]{:S(2)}) collective-permute-start(bf16[2,64,128]{2,1,0:T(8,128)(2,1)S(1)} %get-tuple-element.19), channel_id=1, source_target_pairs={{0,2},{2,4},{4,6},{1,3},{3,5},{5,7},{8,10},{10,12},{12,14},{9,11},... | collective-permute-start | bytes 98312 | tf_op jit(solution)/shard_map/ppermute | solution.py:452
  10.3 0.0 copy-start.14
  10.3 0.0 copy-start.10
  10.3 0.0 copy-start.11
  10.3 0.0 copy-start.13
  10.4 0.0 copy-start.1
  10.4 0.0 copy-start.7
  10.4 1.4 %collective-permute-start.1 = (bf16[2,64,128]{2,1,0:T(8,128)(2,1)S(1)}, bf16[2,64,128]{2,1,0:T(8,128)(2,1)S(1)}, u32[]{:S(2)}, u32[]{:S(2)}) collective-permute-start(bf16[2,64,128]{2,1,0:T(8,128)(2,1)S(1)} %get-tuple-element.20), channel_id=1, source_target_pairs={{2,0},{4,2},{6,4},{3,1},{5,3},{7,5},{10,8},{12,10},{14,12},{11,9},... | collective-permute-start | bytes 98312 | tf_op jit(solution)/shard_map/ppermute | solution.py:452
  11.8 0.1 collective-permute-done.before
  11.9 4.5 %collective-permute-done.1.after = bf16[2,64,128]{2,1,0:T(8,128)(2,1)S(1)} collective-permute-done((bf16[2,64,128]{2,1,0:T(8,128)(2,1)S(1)}, bf16[2,64,128]{2,1,0:T(8,128)(2,1)S(1)}, u32[]{:S(2)}, u32[]{:S(2)}) %collective-permute-start.1) | collective-permute-done | bytes 32800 | tf_op jit(solution)/shard_map/ppermute | solution.py:452
  16.3 0.8 %pack_lon.1 = (f32[14,64,128]{2,1,0:T(8,128)S(1)}, bf16[15,16,640]{2,1,0:T(8,128)(2,1)S(1)}, bf16[15,16,640]{2,1,0:T(8,128)(2,1)S(1)}) custom-call(s32[2]{0:T(128)S(1)} %pad_add_fusion.sc, bf16[2,64,128]{2,1,0:T(8,128)(2,1)S(1)} %collective-permute-done.before, bf16[2,64,128]{2,1,0:T(8,128)(2,1)S(1)} %collective-permute-done.1.after, ...), custom_call_target="tpu_custom_call" | custom-call | tf_op jit(solution)/shard_map/pack_lon/pallas_call | solution.py:477
  17.1 0.1 collective-permute-start.2
  17.2 5.3 %collective-permute-start.3 = (bf16[15,16,640]{2,1,0:T(8,128)(2,1)S(1)}, bf16[15,16,640]{2,1,0:T(8,128)(2,1)S(1)}, u32[]{:S(2)}, u32[]{:S(2)}) collective-permute-start(bf16[15,16,640]{2,1,0:T(8,128)(2,1)S(1)} %get-tuple-element.23), channel_id=1, source_target_pairs={{0,120},{8,0},{16,8},{24,16},{32,24},{40,32},{48,40},{56,48},{64,5... | collective-permute-start | bytes 921608 | tf_op jit(solution)/shard_map/ppermute | solution.py:452
  22.6 0.1 copy.13.w_out
  22.7 0.3 weights.1
  23.1 0.0 copy-start.9
  23.1 10.5 %interior.1.inner = f32[8,56,640]{2,1,0:T(8,128)S(1)} custom-call(s32[2]{0:T(128)S(1)} %pad_add_fusion.sc, f32[4,64,512]{2,1,0:T(8,128)S(1)} %copy-done.1, f32[4,64,512]{2,1,0:T(8,128)S(1)} %copy-done.3, s32[64,512]{1,0:T(8,128)S(1)} %copy-done.7, f32[14,64,128]{2,1,0:T(8,128)S(1)} %get-tuple-element.21.hal, bf16[192,256]{1,0:T(8,128)(2,1)S(1)} %get-tuple-element.26.w1, ...), custom_call_target="tpu_custom_call" | custom-call | flops 6000000 | bytes 18000000 | tf_op jit(solution)/shard_map/interior/pallas_call | solution.py:488
  33.6 3.9 %column_sums.1 = (f32[4,104,640]{2,1,0:T(8,128)S(1)}, bf16[4,104,640]{2,1,0:T(8,128)(2,1)S(1)}, f32[2,104,640]{2,1,0:T(8,128)S(1)}, f32[8,64,640]{2,1,0:T(8,128)}) custom-call(s32[2]{0:T(128)S(1)} %pad_add_fusion.sc, f32[4,64,512]{2,1,0:T(8,128)S(1)} %copy-done.1, f32[4,64,512]{2,1,0:T(8,128)S(1)} %copy-done.3, f32[4,64,512]{2,1,0:T(8,128)S(1)} %copy-done.5, ...), custom_call_target="tpu_custom_call" | custom-call | flops 3000000 | bytes 9000000 | tf_op jit(solution)/shard_map/column_sums/pallas_call | solution.py:502
  37.5 8.6 %edges.1 = (f32[2,104,640]{2,1,0:T(8,128)S(1)}, f32[8,48,640]{2,1,0:T(8,128)S(1)}) custom-call(s32[2]{0:T(128)S(1)} %pad_add_fusion.sc, f32[8,64,640]{2,1,0:T(8,128)} %get-tuple-element.25.edge, f32[8,56,640]{2,1,0:T(8,128)S(1)} %interior.1.inner, f32[2,104,640]{2,1,0:T(8,128)S(1)} %get-tuple-element.24.two, f32[4,104,640]{2,1,0:T(8,128)S(1)} %get-tuple-element.31.sums, ...), custom_call_target="tpu_custom_call" | custom-call | flops 5000000 | bytes 15000000 | tf_op jit(solution)/shard_map/edges/pallas_call | solution.py:515
  46.1 0.1 collective-permute-start.4
  46.2 2.0 %collective-permute-start.5 = (bf16[4,104,640]{2,1,0:T(8,128)(2,1)S(1)}, bf16[4,104,640]{2,1,0:T(8,128)(2,1)S(1)}, u32[]{:S(2)}, u32[]{:S(2)}) collective-permute-start(bf16[4,104,640]{2,1,0:T(8,128)(2,1)S(1)} %get-tuple-element.33), channel_id=1, source_target_pairs={{0,1},{1,0},{2,3},{3,2},{4,5},{5,4},{6,7},{7,6},{8,9},{9,8},{10,11... | collective-permute-start | bytes 1597448 | tf_op jit(solution)/shard_map/ppermute | solution.py:452
  48.3 1.5 %own_part.1.own = f32[8,64,512]{2,1,0:T(8,128)S(1)} custom-call(s32[2]{0:T(128)S(1)} %pad_add_fusion.sc, f32[4,64,512]{2,1,0:T(8,128)S(1)} %copy-done.1, f32[4,64,512]{2,1,0:T(8,128)S(1)} %copy-done.3, f32[4,64,512]{2,1,0:T(8,128)S(1)} %copy-done.5, s32[64,512]{1,0:T(8,128)S(1)} %copy-done.7, f32[14,64,128]{2,1,0:T(8,128)S(1)} %get-tuple-element.21.hal, ...), custom_call_target="tpu_custom_call" | custom-call | flops 3000000 | bytes 9000000 | tf_op jit(solution)/shard_map/own_part/pallas_call | solution.py:524
  49.8 11.5 %collective-permute-done.4.theirs = f32[2,104,640]{2,1,0:T(8,128)S(1)} collective-permute-done((f32[2,104,640]{2,1,0:T(8,128)S(1)}, f32[2,104,640]{2,1,0:T(8,128)S(1)}, u32[]{:S(2)}, u32[]{:S(2)}) %collective-permute-start.4) | collective-permute-done | bytes 532512 | tf_op jit(solution)/shard_map/ppermute | solution.py:452
  61.3 8.3 %collective-permute-done.5.early = bf16[4,104,640]{2,1,0:T(8,128)(2,1)S(1)} collective-permute-done((bf16[4,104,640]{2,1,0:T(8,128)(2,1)S(1)}, bf16[4,104,640]{2,1,0:T(8,128)(2,1)S(1)}, u32[]{:S(2)}, u32[]{:S(2)}) %collective-permute-start.5) | collective-permute-done | bytes 532512 | tf_op jit(solution)/shard_map/ppermute | solution.py:452
  69.6 4.9 %finish.1 = (f32[4,64,512]{2,1,0:T(8,128)}, f32[4,64,512]{2,1,0:T(8,128)}, f32[64,512]{1,0:T(8,128)}) custom-call(s32[2]{0:T(128)S(1)} %pad_add_fusion.sc, f32[2,104,640]{2,1,0:T(8,128)S(1)} %get-tuple-element.24.two, f32[2,104,640]{2,1,0:T(8,128)S(1)} %get-tuple-element.32.mine, f32[2,104,640]{2,1,0:T(8,128)S(1)} %collective-permute-done.4.theirs, ...), custom_call_target="tpu_custom_call" | custom-call | flops 5000000 | bytes 15000000 | tf_op jit(solution)/shard_map/finish/pallas_call | solution.py:535
  (20 shorter events, 0.0 us)
Async XLA Ops:
  0.7 1.0 %copy-start = (f32[4,64,512]{2,1,0:T(8,128)S(1)}, f32[4,64,512]{2,1,0:T(8,128)}, u32[]{:S(2)}) copy-start(f32[4,64,512]{2,1,0:T(8,128)} %u.5) | copy-start | bytes 1572868
  1.8 1.0 %copy-start.2 = (f32[4,64,512]{2,1,0:T(8,128)S(1)}, f32[4,64,512]{2,1,0:T(8,128)}, u32[]{:S(2)}) copy-start(f32[4,64,512]{2,1,0:T(8,128)} %v.5) | copy-start | bytes 1572868
  2.8 1.0 %copy-start.4 = (f32[4,64,512]{2,1,0:T(8,128)S(1)}, f32[4,64,512]{2,1,0:T(8,128)}, u32[]{:S(2)}) copy-start(f32[4,64,512]{2,1,0:T(8,128)} %b.3) | copy-start | bytes 1572868
  3.8 0.9 %copy-start.6 = (s32[64,512]{1,0:T(8,128)S(1)}, s32[64,512]{1,0:T(8,128)}, u32[]{:S(2)}) copy-start(s32[64,512]{1,0:T(8,128)} %bl.5) | copy-start | bytes 393220
  4.7 0.9 %copy-start.8 = (f32[64,512]{1,0:T(8,128)S(1)}, f32[64,512]{1,0:T(8,128)}, u32[]{:S(2)}) copy-start(f32[64,512]{1,0:T(8,128)} %s.1) | copy-start | bytes 393220
  6.4 5.5 %collective-permute-start = (bf16[2,64,128]{2,1,0:T(8,128)(2,1)S(1)}, bf16[2,64,128]{2,1,0:T(8,128)(2,1)S(1)}, u32[]{:S(2)}, u32[]{:S(2)}) collective-permute-start(bf16[2,64,128]{2,1,0:T(8,128)(2,1)S(1)} %get-tuple-element.19), channel_id=1, source_target_pairs={{0,2},{2,4},{4,6},{1,3},{3,5},{5,7},{8,10},{10,12},{12,14},{9,11},... | collective-permute-start | bytes 98312 | tf_op jit(solution)/shard_map/ppermute | solution.py:452
  10.3 12.3 %copy-start.14 = (bf16[9,32,8]{1,2,0:T(8,128)(2,1)S(1)}, bf16[9,32,8]{1,2,0:T(8,128)(2,1)}, u32[]{:S(2)}) copy-start(bf16[9,32,8]{1,2,0:T(8,128)(2,1)} %param.20) | copy-start | bytes 13828
  10.3 12.4 %copy-start.10 = (bf16[9,32,32]{2,1,0:T(8,128)(2,1)S(1)}, bf16[9,32,32]{2,1,0:T(8,128)(2,1)}, u32[]{:S(2)}) copy-start(bf16[9,32,32]{2,1,0:T(8,128)(2,1)} %w_mid.1) | copy-start | bytes 55300
  10.3 12.4 %copy-start.11 = (bf16[9,8,32]{2,1,0:T(8,128)(2,1)S(1)}, bf16[9,8,32]{2,1,0:T(8,128)(2,1)}, u32[]{:S(2)}) copy-start(bf16[9,8,32]{2,1,0:T(8,128)(2,1)} %w_in.1) | copy-start | bytes 13828
  10.3 12.4 %copy-start.12 = (f32[32]{0:T(128)S(1)}, f32[32]{0:T(128)}, u32[]{:S(2)}) copy-start(f32[32]{0:T(128)} %param.17) | copy-start | bytes 388
  10.3 12.4 %copy-start.13 = (f32[32]{0:T(128)S(1)}, f32[32]{0:T(128)}, u32[]{:S(2)}) copy-start(f32[32]{0:T(128)} %param.19) | copy-start | bytes 388
  10.4 12.7 %copy-start.1 = (f32[4,64,512]{2,1,0:T(8,128)S(1)}, f32[4,64,512]{2,1,0:T(8,128)}, u32[]{:S(2)}) copy-start(f32[4,64,512]{2,1,0:T(8,128)} %u.5) | copy-start | bytes 1572868
  10.4 12.7 %copy-start.3 = (f32[4,64,512]{2,1,0:T(8,128)S(1)}, f32[4,64,512]{2,1,0:T(8,128)}, u32[]{:S(2)}) copy-start(f32[4,64,512]{2,1,0:T(8,128)} %v.5) | copy-start | bytes 1572868
  10.4 12.7 %copy-start.7 = (s32[64,512]{1,0:T(8,128)S(1)}, s32[64,512]{1,0:T(8,128)}, u32[]{:S(2)}) copy-start(s32[64,512]{1,0:T(8,128)} %bl.5) | copy-start | bytes 393220
  10.4 5.9 %collective-permute-start.1 = (bf16[2,64,128]{2,1,0:T(8,128)(2,1)S(1)}, bf16[2,64,128]{2,1,0:T(8,128)(2,1)S(1)}, u32[]{:S(2)}, u32[]{:S(2)}) collective-permute-start(bf16[2,64,128]{2,1,0:T(8,128)(2,1)S(1)} %get-tuple-element.20), channel_id=1, source_target_pairs={{2,0},{4,2},{6,4},{3,1},{5,3},{7,5},{10,8},{12,10},{14,12},{11,9},... | collective-permute-start | bytes 98312 | tf_op jit(solution)/shard_map/ppermute | solution.py:452
  17.1 16.4 %collective-permute-start.2 = (bf16[15,16,640]{2,1,0:T(8,128)(2,1)S(1)}, bf16[15,16,640]{2,1,0:T(8,128)(2,1)S(1)}, u32[]{:S(2)}, u32[]{:S(2)}) collective-permute-start(bf16[15,16,640]{2,1,0:T(8,128)(2,1)S(1)} %get-tuple-element.22), channel_id=1, source_target_pairs={{0,8},{8,16},{16,24},{24,32},{32,40},{40,48},{48,56},{56,64},{64,7... | collective-permute-start | bytes 921608 | tf_op jit(solution)/shard_map/ppermute | solution.py:452
  17.2 16.3 %collective-permute-start.3 = (bf16[15,16,640]{2,1,0:T(8,128)(2,1)S(1)}, bf16[15,16,640]{2,1,0:T(8,128)(2,1)S(1)}, u32[]{:S(2)}, u32[]{:S(2)}) collective-permute-start(bf16[15,16,640]{2,1,0:T(8,128)(2,1)S(1)} %get-tuple-element.23), channel_id=1, source_target_pairs={{0,120},{8,0},{16,8},{24,16},{32,24},{40,32},{48,40},{56,48},{64,5... | collective-permute-start | bytes 921608 | tf_op jit(solution)/shard_map/ppermute | solution.py:452
  23.0 10.5 %copy-start.5 = (f32[4,64,512]{2,1,0:T(8,128)S(1)}, f32[4,64,512]{2,1,0:T(8,128)}, u32[]{:S(2)}) copy-start(f32[4,64,512]{2,1,0:T(8,128)} %b.3) | copy-start | bytes 1572868
  23.1 10.5 %copy-start.9 = (f32[64,512]{1,0:T(8,128)S(1)}, f32[64,512]{1,0:T(8,128)}, u32[]{:S(2)}) copy-start(f32[64,512]{1,0:T(8,128)} %s.1) | copy-start | bytes 393220
  46.1 15.1 %collective-permute-start.4 = (f32[2,104,640]{2,1,0:T(8,128)S(1)}, f32[2,104,640]{2,1,0:T(8,128)S(1)}, u32[]{:S(2)}, u32[]{:S(2)}) collective-permute-start(f32[2,104,640]{2,1,0:T(8,128)S(1)} %get-tuple-element.32.mine), channel_id=1, source_target_pairs={{0,1},{1,0},{2,3},{3,2},{4,5},{5,4},{6,7},{7,6},{8,9},{9,8},{10,11... | collective-permute-start | bytes 1597448 | tf_op jit(solution)/shard_map/ppermute | solution.py:452
  46.2 23.4 %collective-permute-start.5 = (bf16[4,104,640]{2,1,0:T(8,128)(2,1)S(1)}, bf16[4,104,640]{2,1,0:T(8,128)(2,1)S(1)}, u32[]{:S(2)}, u32[]{:S(2)}) collective-permute-start(bf16[4,104,640]{2,1,0:T(8,128)(2,1)S(1)} %get-tuple-element.33), channel_id=1, source_target_pairs={{0,1},{1,0},{2,3},{3,2},{4,5},{5,4},{6,7},{7,6},{8,9},{9,8},{10,11... | collective-permute-start | bytes 1597448 | tf_op jit(solution)/shard_map/ppermute | solution.py:452

commit v2 on v1

v2 whole, which is shorter than its diff:
```python
import jax
import jax.numpy as jnp
from jax import lax
from jax.experimental import pallas as pl
from jax.experimental.pallas import tpu as pltpu
from jax.sharding import PartitionSpec as P

NSUB = 8
TX, TY = 64, 512
LANES = 640
ROWS = 96
HALO = 16
RIM = 24
EDGE = 18
FORCED = 104
FIELDS = 14
F32 = jnp.float32
BF = jnp.bfloat16

coriolis_base = 0.6
coriolis_slope = 0.8
press_coef = 0.3
drag_coef = 0.5
step_dt = 0.2
closure_coef = 0.5
gravity = 1.0
sub_dt = 0.4
TOTAL_DEPTH = 15.0

TOKEN = jax.ShapeDtypeStruct((8, 128), jnp.float32)
VMEM = pl.BlockSpec(memory_space=pltpu.VMEM)


def sds(shape, dtype=F32):
    return jax.ShapeDtypeStruct(shape, dtype)


def wet_of(bl, level):
    return jnp.where(bl > level, 1.0, 0.0)


def latitudes(lat, shape):
    lane = lax.broadcasted_iota(jnp.int32, shape, len(shape) - 1)
    return lat * TY + jnp.where(lane < TY + 64, lane, lane - LANES)


def inside_of(lat, total, shape):
    y = latitudes(lat, shape)
    return jnp.where((y >= 0) & (y < total), 1.0, 0.0)


def pack_lat(sc, u, v, b, l, s, to_down, to_up, ub, vb, bb, lb, sb, sem):
    base = 4 * sc[0]
    lane = lax.broadcasted_iota(jnp.int32, (TX, 128), 1)
    copies = []
    for side, at in enumerate((0, TY - 128)):
        for n, (src, dst) in enumerate(((u, ub), (v, vb), (b, bb))):
            copies.append(pltpu.make_async_copy(src.at[:, :, at : at + 128], dst.at[side], sem.at[side, n]))
        for n, (src, dst) in enumerate(((l, lb), (s, sb))):
            copies.append(pltpu.make_async_copy(src.at[:, at : at + 128], dst.at[side], sem.at[side, 3 + n]))
    for copy in copies:
        copy.start()
    for copy in copies:
        copy.wait()

    def fields(side):
        bl = lb[side].astype(F32)
        wets = [wet_of(bl, (base + k).astype(F32)) for k in range(4)]
        for a in (ub, vb, bb):
            for k in range(4):
                yield a[side, k] * wets[k]
        yield bl
        yield sb[side]

    for side, (out, origin) in enumerate(((to_down, 0), (to_up, 128 - EDGE))):
        for i, field in enumerate(fields(side)):
            tile, place = divmod(i, 7)
            if place == 0:
                acc = jnp.zeros((TX, 128), F32)
            moved = pltpu.roll(field, (EDGE * place - origin) % 128, 1)
            acc = jnp.where((lane >= EDGE * place) & (lane < EDGE * (place + 1)), moved, acc)
            if place == 6:
                out[tile] = acc.astype(BF)


def pack_lon(sc, ready, before, after, *refs):
    tops, bots, extra_t, extra_b = refs[0:5], refs[5:10], refs[10:13], refs[13:16]
    hal, to_down, to_up, work = refs[16:]
    base = 4 * sc[0]
    lane = lax.broadcasted_iota(jnp.int32, (TX, 128), 1)
    for tile in range(2):
        low, high = before[tile].astype(F32), after[tile].astype(F32)
        for place in range(7):
            a = pltpu.roll(high, (-EDGE * place) % 128, 1)
            b = pltpu.roll(low, (128 - EDGE - EDGE * place) % 128, 1)
            hal[tile * 7 + place] = jnp.where(lane < EDGE, a, jnp.where(lane >= 128 - EDGE, b, 0.0))
    for out, (u, v, b, l, s), row in ((to_down, tops, 0), (to_up, bots, TX - 16)):
        bl = l[...].astype(F32)
        for k in range(4):
            wet = wet_of(bl, (base + k).astype(F32))
            for n, a in enumerate((u, v, b)):
                out[4 * n + k, :, :TY] = (a[k] * wet).astype(BF)
        out[12, :, :TY] = bl.astype(BF)
        out[13, :, :TY] = s[...].astype(BF)
        for i in range(FIELDS):
            out[i, :, TY:] = hal[i, row : row + 16, :].astype(BF)
    for out, (u, v, l), first, row in ((to_down, extra_t, 0, 16), (to_up, extra_b, 6, 46)):
        bl = l[first : first + 2, :].astype(F32)
        for k in range(4):
            wet = wet_of(bl, (base + k).astype(F32))
            for n, a in enumerate((u, v)):
                work[2 * (4 * n + k) : 2 * (4 * n + k) + 2, :TY] = a[k, first : first + 2, :] * wet
        for i in range(8):
            work[2 * i : 2 * i + 2, TY:] = hal[i, row : row + 2, :]
        out[14] = work[...].astype(BF)


def build_weights(sc, w_in, b_in, w_mid, b_mid, w_out, w1, w2, w3, b1, b2, done, spread):
    done[...] = jnp.zeros_like(done)

    def across(parts, rows, cols):
        rows_all = sum(p.shape[0] for p in parts)
        full = jnp.concatenate(parts + [jnp.zeros((128 - rows_all, 128), F32)], 0)
        return full.T[:rows, :]

    def wide(a):
        return jnp.concatenate([a, jnp.zeros((a.shape[0], 128 - a.shape[1]), F32)], 1)

    zero8 = jnp.zeros((8, 128), F32)
    parts = []
    for a in range(3):
        parts += [wide(w_in[3 * a + b].astype(F32)) for b in range(3)] + [zero8]
    first = across(parts, 32, 96)
    first = jnp.concatenate([first, jnp.zeros((32, 128), F32)], 1)
    for p in range(6):
        w1[32 * p : 32 * p + 32, :] = pltpu.roll(first, 32 * p, 1).astype(BF)
    for b in range(3):
        mid = across([wide(w_mid[3 * a + b].astype(F32)) for a in range(3)], 32, 96)
        mid = jnp.concatenate([mid, jnp.zeros((32, 128), F32)], 1)
        for p in range(6):
            w2[192 * b + 32 * p : 192 * b + 32 * p + 32, :] = pltpu.roll(mid, 32 * p, 1).astype(BF)
        last = across([wide(w_out[3 * a + b].astype(F32)) for a in range(3)], 8, 96)
        last = jnp.concatenate([last, jnp.zeros((8, 256), F32)], 1)
        for p in range(8):
            spread[:, p, :] = pltpu.roll(last, 32 * p, 1)
        w3[64 * b : 64 * b + 64, :] = spread[...].reshape(64, 384)[:, :320].astype(BF)
    eye = lax.broadcasted_iota(jnp.int32, (32, 32), 0) == lax.broadcasted_iota(jnp.int32, (32, 32), 1)
    for src, dst in ((b_in, b1), (b_mid, b2)):
        column = jnp.sum(jnp.where(eye, src[...], 0.0), 1, keepdims=True)
        for p in range(6):
            dst[32 * p : 32 * p + 32, :] = jnp.broadcast_to(column, (32, 128))


def load_slots(up, start, count, in0, at):
    for i in range(count):
        c = up[:, start + i, :]
        r = 32 * (at + i)
        in0[r : r + 16, :] = jnp.concatenate([pltpu.roll(c, 1, 1), c], 0).astype(BF)
        in0[r + 16 : r + 32, :] = jnp.concatenate([pltpu.roll(c, LANES - 1, 1), jnp.zeros_like(c)], 0).astype(BF)


def closure(in0, act1, act2, weights, inside, parts, store):
    w1, w2, w3, b1, b2 = weights
    bias1, bias2 = b1[:, :1], b2[:, :1]

    def combined(o, m):
        return pltpu.roll(o[:m], 1, 1) + o[m : 2 * m] + pltpu.roll(o[2 * m :], LANES - 1, 1)

    for s1, _, _, n1, _, _ in parts:
        for j in range(n1):
            r = 32 * (s1 + 6 * j)
            o = jnp.dot(w1[...], in0[r : r + 256, :], preferred_element_type=F32)
            act1[r : r + 192, :] = (jnp.maximum(o + bias1, 0.0) * inside).astype(BF)
    for s1, s2, shift, _, n2, _ in parts:
        for j in range(n2):
            r, to = 32 * (s1 + 6 * j), 32 * (s2 + shift + 6 * j)
            o = combined(jnp.dot(w2[...], act1[r : r + 256, :], preferred_element_type=F32), 192)
            act2[to : to + 192, :] = (jnp.maximum(o + bias2, 0.0) * inside).astype(BF)
    for part, (_, s2, _, _, _, n3) in enumerate(parts):
        for j in range(n3):
            r = 32 * (s2 + 8 * j)
            o = combined(jnp.dot(w3[...], act2[r : r + 320, :], preferred_element_type=F32), 64)
            store(part, j, (closure_coef * o).astype(BF).astype(F32).reshape(8, 8, LANES))


def interior(total, sc, u, v, bl, hal, w1, w2, w3, b1, b2, out, done, up, in0, act1, act2):
    done[...] = jnp.zeros_like(done)

    @pl.when(sc[0] == 0)
    def _():
        level = bl[...].astype(F32)
        for k in range(4):
            wet = wet_of(level, float(k))
            up[k, :, :TY] = u[k] * wet
            up[4 + k, :, :TY] = v[k] * wet
        for i in range(8):
            up[i, :, TY:] = hal[i]
        load_slots(up, 1, 62, in0, 0)
        act1[1920:1984, :] = jnp.zeros((64, LANES), BF)

        def store(part, j, f):
            out[:, 24 + 8 * j : 32 + 8 * j, :] = f

        closure(in0, act1, act2, (w1, w2, w3, b1, b2), inside_of(sc[1], total, (1, LANES)), [(0, 0, 0, 10, 10, 7)], store)


def edges(total, sc, edge, w1, w2, w3, b1, b2, inner, out, in0, act1, act2):
    @pl.when(sc[0] == 0)
    def _():
        for at, start in ((0, 6), (26, 33)):
            load_slots(edge, start, 26, in0, at)
            act1[32 * at + 768 : 32 * at + 832, :] = jnp.zeros((64, LANES), BF)
        act2[0:160, :] = jnp.zeros((160, LANES), BF)
        act2[29 * 32 + 768 :, :] = jnp.zeros((64, LANES), BF)

        def store(part, j, f):
            row = 80 * part + 8 * j
            out[:, row : row + 8, :] = f

        parts = [(0, 0, 5, 4, 4, 3), (26, 29, 0, 4, 4, 3)]
        closure(in0, act1, act2, (w1, w2, w3, b1, b2), inside_of(sc[1], total, (1, LANES)), parts, store)


def pressures(base, b_rows, pr, load, rows):
    for r in range(0, rows, 8):
        run = jnp.zeros((8, LANES), F32)
        for k in range(4):
            weighted = b_rows(k, r) * (1.0 + 0.25 * (base + k).astype(F32))
            pr[k, r + 8 : r + 16, :] = run + 0.5 * weighted
            run = run + weighted
        load[r + 8 : r + 16, :] = run


def grads(ref, r):
    here = ref[r + 8 : r + 16, :]
    gx = (ref[r + 9 : r + 17, :] - ref[r + 7 : r + 15, :]) * 0.5
    gy = (pltpu.roll(here, LANES - 1, 1) - pltpu.roll(here, 1, 1)) * 0.5
    return gx, gy


def coriolis_of(lat, total, shape):
    return coriolis_base + coriolis_slope * (latitudes(lat, shape).astype(F32) * (1.0 / total) - 0.5)


def sums_of(sc, coriolis, level, east, north, pr, load, r):
    base = 4 * sc[0]
    te = jnp.zeros((8, LANES), F32)
    tn, us, vs = te, te, te
    for k in range(4):
        number = (base + k).astype(F32)
        thick = 1.0 + 0.25 * number
        weight = jnp.where(level > number, thick, 0.0)
        drag = jnp.where(level == number + 1.0, drag_coef, 0.0)
        e, n = east(k), north(k)
        gx, gy = grads(pr.at[k], r)
        te = te + weight * (coriolis * n - press_coef * gx - drag * e)
        tn = tn + weight * (-coriolis * e - press_coef * gy - drag * n)
        us = us + thick * e
        vs = vs + thick * n
    below = jnp.zeros((8, LANES), F32)
    for k in range(4, 8):
        below = below + jnp.where(level > float(k), 1.0 + 0.25 * k, 0.0)
    gx, gy = grads(load, r)
    below = below * (press_coef * jnp.where(sc[0] == 0, 1.0, 0.0))
    return te - below * gx, tn - below * gy, us, vs, gx, gy


def middle_sums(total, sc, u, v, b, bl, hal, sums, send, ext, lev, pr, load):
    base = 4 * sc[0]
    level = bl[...].astype(F32)
    for k in range(4):
        wet = wet_of(level, (base + k).astype(F32))
        for n, a in enumerate((u, v, b)):
            ext[4 * n + k, :, :TY] = a[k] * wet
    for i in range(12):
        ext[i, :, TY:] = hal[i]
    lev[:, :TY] = level
    lev[:, TY:] = hal[12]
    pressures(base, lambda k, r: ext[8 + k, r : r + 8, :], pr, load, TX)
    coriolis = coriolis_of(sc[1], total, (8, LANES))
    for q in range(0, 48, 16):
        halves = []
        for r in (q + 8, q + 16):
            rr = slice(r, r + 8)
            found = sums_of(sc, coriolis, lev[rr, :], lambda k: ext[k, rr, :], lambda k: ext[4 + k, rr, :], pr, load, r)
            for i, a in enumerate(found):
                sums[i, r - 8 : r, :] = a
            halves.append(found)
        for i in range(4):
            a = jnp.concatenate([halves[0][i], halves[1][i]], 0)
            high = a.astype(BF)
            send[i, q : q + 16, :] = high
            if i < 2:
                send[4 + i, q : q + 16, :] = (a - high.astype(F32)).astype(BF)


def rim_sums(total, sc, ready, u, v, b, bl, s, hal, low, high, sums, send, two, edge, ext, pr, load):
    base = 4 * sc[0]
    tall = 32
    for side, halo in ((0, low), (1, high)):
        own = slice(0, 16) if side == 0 else slice(TX - 16, TX)
        hr, orr = (slice(0, 16), slice(16, 32)) if side == 0 else (slice(16, 32), slice(0, 16))
        level = bl[own, :].astype(F32)
        for i in range(13):
            ext[i, hr, :] = halo[i].astype(F32)
            ext[i, orr, TY:] = hal[i, own, :]
        for k in range(4):
            wet = wet_of(level, (base + k).astype(F32))
            for n, a in enumerate((u, v, b)):
                ext[4 * n + k, orr, :TY] = a[k, own, :] * wet
        ext[12, orr, :TY] = level
        pressures(base, lambda k, r: ext[8 + k, r : r + 8, :], pr, load, tall)
        for ref in [pr.at[k] for k in range(4)] + [load]:
            if side == 0:
                ref[0:8, :] = jnp.zeros((8, LANES), F32)
            else:
                ref[40:48, :] = jnp.zeros((8, LANES), F32)
        coriolis = coriolis_of(sc[1], total, (8, LANES))
        for j in range(3):
            r = 8 * j + 8 * side
            rr = slice(r, r + 8)
            found = sums_of(sc, coriolis, ext[12, rr, :], lambda k: ext[k, rr, :], lambda k: ext[4 + k, rr, :], pr, load, r)
            for i, a in enumerate(found):
                sums[i, RIM * side + 8 * j : RIM * side + 8 * j + 8, :] = a
        more = halo[14].astype(F32)
        for i in range(8):
            if side == 0:
                edge[i, 0:8, :] = jnp.zeros((8, LANES), F32)
                edge[i, 8:32, :] = ext[i, 0:24, :]
                edge[i, 6:8, :] = more[2 * i : 2 * i + 2, :]
            else:
                edge[i, 32:56, :] = ext[i, 8:32, :]
                edge[i, 56:64, :] = jnp.zeros((8, LANES), F32)
                edge[i, 56:58, :] = more[2 * i : 2 * i + 2, :]
        at = slice(0, 16) if side == 0 else slice(80, 96)
        two[0, at, :] = halo[12].astype(F32)
        two[1, at, :] = halo[13].astype(F32)
    two[0, 16:80, :TY] = bl[...].astype(F32)
    two[1, 16:80, :TY] = s[...]
    for i in range(2):
        two[i, 16:80, TY:] = hal[12 + i]
    for i in range(4):
        send[i] = sums[i].astype(BF)


def own_part(total, sc, u, v, b, bl, hal, low, high, force, out, pr, load):
    base = 4 * sc[0]
    upper = jnp.where(sc[0] == 0, step_dt, 0.0)

    def b_rows(k, r):
        if r == 0:
            return low[8 + k].astype(F32)[8:16]
        if r == TX + 8:
            return high[8 + k].astype(F32)[0:8]
        at = slice(r - 8, r)
        wet = wet_of(bl[at, :].astype(F32), (base + k).astype(F32))
        return jnp.concatenate([b[k, at, :] * wet, hal[8 + k, at, :]], 1)

    pressures(base, b_rows, pr, load, TX + 16)
    coriolis = coriolis_of(sc[1], total, (8, LANES))[:, :TY]
    for r in range(0, TX, 8):
        rr = slice(r, r + 8)
        lev = bl[rr, :].astype(F32)
        for k in range(4):
            number = (base + k).astype(F32)
            wet = wet_of(lev, number)
            drag = jnp.where(lev == number + 1.0, drag_coef, 0.0)
            east, north = u[k, rr, :], v[k, rr, :]
            gx, gy = grads(pr.at[k], r + 8)
            te = coriolis * north - press_coef * gx[:, :TY] - drag * east
            tn = -coriolis * east - press_coef * gy[:, :TY] - drag * north
            at = slice(r + 20, r + 28)
            fe = jnp.where(upper > 0.0, force[k, at, :TY], 0.0)
            fn = jnp.where(upper > 0.0, force[4 + k, at, :TY], 0.0)
            out[k, rr, :] = wet * (east + step_dt * (te + fe))
            out[4 + k, rr, :] = wet * (north + step_dt * (tn + fn))


def substeps(total, sc, two, mid, rim, mid_in, rim_in, force, fin, send, lv, fx, fy, eb, nb, ae, an, es, ns, rel, c2):
    @pl.when(sc[0] == 0)
    def _():
        zero8 = jnp.zeros((8, LANES), F32)
        for ref in (lv, fx):
            ref[0:8, :] = zero8
            ref[ROWS + 8 : ROWS + 16, :] = zero8
        for r in range(0, ROWS, 8):
            rr = slice(r, r + 8)
            level = two[0, rr, :]
            depth = level + 0.125 * level * (level - 1.0)
            over = 1.0 / jnp.maximum(depth, 1.0)
            rel[rr, :] = depth * (1.0 / TOTAL_DEPTH)
            c2[rr, :] = jnp.where(level > 0.0, 0.5 * sub_dt * gravity, 0.0)
            middle = RIM <= r < ROWS - RIM
            at = r - RIM if middle else (r if r < RIM else r - 48)
            at = slice(at, at + 8)
            mine, theirs = (mid, mid_in) if middle else (rim, rim_in)
            pair, half = at.start // 16 * 16, at.start % 16

            def other(i):
                return theirs[i, pair : pair + 16, :].astype(F32)[half : half + 8]

            found = [mine[i, at, :] + other(i) for i in range(4)]
            if middle:
                found[:2] = [found[i] + other(4 + i) for i in range(2)]
            for k in range(4):
                weight = jnp.where(level > float(k), 1.0 + 0.25 * k, 0.0)
                found[0] = found[0] + weight * force[k, r + 4 : r + 12, :]
                found[1] = found[1] + weight * force[4 + k, r + 4 : r + 12, :]
            ae[rr, :] = sub_dt * found[0] * over
            an[rr, :] = sub_dt * found[1] * over
            e, n = found[2] * over, found[3] * over
            es[rr, :], ns[rr, :] = e, n
            eb[rr, :], nb[rr, :] = e, n
            lv[r + 8 : r + 16, :] = two[1, rr, :]
        inside = inside_of(sc[1], total, (8, LANES))

        def step(_, carry):
            for r in range(0, ROWS, 8):
                rr = slice(r, r + 8)
                here = lv[r + 8 : r + 16, :]
                dx = lv[r + 9 : r + 17, :] - lv[r + 7 : r + 15, :]
                dy = pltpu.roll(here, LANES - 1, 1) - pltpu.roll(here, 1, 1)
                c = c2[rr, :]
                e = eb[rr, :] + (ae[rr, :] - c * dx)
                n = nb[rr, :] + (an[rr, :] - c * dy)
                eb[rr, :] = e
                nb[rr, :] = n
                fx[r + 8 : r + 16, :] = rel[rr, :] * e
                fy[rr, :] = rel[rr, :] * n
            for r in range(0, ROWS, 8):
                rr = slice(r, r + 8)
                dx = fx[r + 9 : r + 17, :] - fx[r + 7 : r + 15, :]
                f = fy[rr, :]
                dy = pltpu.roll(f, LANES - 1, 1) - pltpu.roll(f, 1, 1)
                lv[r + 8 : r + 16, :] = inside * (lv[r + 8 : r + 16, :] - (0.5 * sub_dt) * (dx + dy))
            return carry

        lax.fori_loop(0, NSUB, step, 0)
        for q in range(0, TX, 16):
            r = q + HALO
            rr, at = slice(r, r + 16), slice(q, q + 16)
            fe = eb[rr, :TY] - es[rr, :TY] - (step_dt / sub_dt) * ae[rr, :TY]
            fn = nb[rr, :TY] - ns[rr, :TY] - (step_dt / sub_dt) * an[rr, :TY]
            fin[0, at, :], fin[1, at, :] = fe, fn
            slopes = []
            for i in (4, 5):
                pieces = []
                for p in (r, r + 8):
                    if RIM <= p < ROWS - RIM:
                        pieces.append(mid[i, p - RIM : p - RIM + 8, :TY])
                    else:
                        p = p if p < RIM else p - 48
                        pieces.append(rim[i, p : p + 8, :TY])
                slopes.append(jnp.concatenate(pieces, 0))
            send[0, at, :] = (fe - (step_dt * press_coef) * slopes[0]).astype(BF)
            send[1, at, :] = (fn - (step_dt * press_coef) * slopes[1]).astype(BF)
            level = lv[r + 8 : r + 24, :TY]
            high = level.astype(BF)
            send[2, at, :] = high
            send[3, at, :] = (level - high.astype(F32)).astype(BF)


def finish(sc, bl, fin, mine, theirs, own, east_out, north_out, surface_out):
    base = 4 * sc[0]
    upper = jnp.where(sc[0] == 0, 1.0, 0.0) > 0.0
    for r in range(0, TX, 16):
        rr = slice(r, r + 16)
        level = bl[rr, :].astype(F32)
        fe = jnp.where(upper, fin[0, rr, :], theirs[0, rr, :].astype(F32))
        fn = jnp.where(upper, fin[1, rr, :], theirs[1, rr, :].astype(F32))
        for k in range(4):
            wet = wet_of(level, (base + k).astype(F32))
            east_out[k, rr, :] = own[k, rr, :] + wet * fe
            north_out[k, rr, :] = own[4 + k, rr, :] + wet * fn
        parts = [jnp.where(upper, mine[i, rr, :].astype(F32), theirs[i, rr, :].astype(F32)) for i in (2, 3)]
        surface_out[rr, :] = parts[0] + parts[1]


def call(kernel, name, out_shape, n_in, scratch=(), in_specs=None, cost=None, grid=(), aliases=None, room=28):
    single = not isinstance(out_shape, (list, tuple))

    def placed(*refs):
        kernel((lax.axis_index("grp"), lax.axis_index("lat")), *refs)

    return pl.pallas_call(
        placed,
        name=name,
        grid=grid,
        out_shape=out_shape,
        in_specs=in_specs or [VMEM] * n_in,
        out_specs=VMEM if single else [VMEM] * len(out_shape),
        scratch_shapes=list(scratch),
        compiler_params=pltpu.CompilerParams(vmem_limit_bytes=room * 2**20),
        cost_estimate=cost,
        input_output_aliases=aliases or {},
    )


def with_total(kernel, total):
    return lambda sc, *refs: kernel(total, sc, *refs)


def micros(us):
    return pl.CostEstimate(flops=int(us * 1e6), bytes_accessed=int(us * 3e6), transcendentals=0)


def shifted(x, axis, by, ring):
    size = lax.axis_size(axis)
    pairs = [(i, (i + by) % size) for i in range(size) if ring or 0 <= i + by < size]
    return lax.ppermute(x, axis, pairs)


def local(u, v, b, wet_mask, bl, s, w_in, b_in, w_mid, b_mid, w_out):
    total = TY * lax.axis_size("lat")
    wide, half = pltpu.VMEM((2, 4, TX, 128), F32), sds((2, TX, 128), BF)
    to_down, to_up = call(
        pack_lat,
        "pack_lat",
        [half, half],
        6,
        [wide, wide, wide, pltpu.VMEM((2, TX, 128), jnp.int32), pltpu.VMEM((2, TX, 128), F32), pltpu.SemaphoreType.DMA((2, 5))],
        in_specs=[pl.BlockSpec(memory_space=pltpu.HBM)] * 5,
        room=60,
    )(u, v, b, bl, s)
    before = shifted(to_up, "lat", 1, False)
    after = shifted(to_down, "lat", -1, False)
    vb = [sds((192, 256), BF), sds((576, 256), BF), sds((192, 320), BF), sds((192, 128)), sds((192, 128)), TOKEN]
    *weights, ready = call(build_weights, "weights", vb, 5, [pltpu.VMEM((8, 8, 384), F32)], in_specs=[VMEM] * 5)(
        w_in, b_in[None, :], w_mid, b_mid[None, :], w_out
    )

    def rows(n, i, three):
        return [pl.BlockSpec((4, n, TY), lambda _: (0, i, 0))] * three + [pl.BlockSpec((n, TY), lambda _: (i, 0))] * (three - 1)

    out = sds((15, 16, LANES), BF)
    hal, down, up = call(
        pack_lon,
        "pack_lon",
        [sds((FIELDS, TX, 128)), out, out],
        20,
        [pltpu.VMEM((16, LANES), F32)],
        in_specs=[VMEM, VMEM, VMEM] + rows(16, 0, 3) + rows(16, 3, 3) + rows(8, 2, 2) + rows(8, 5, 2),
        grid=(1,),
    )(ready, before, after, u, v, b, bl, s, u, v, b, bl, s, u, v, bl, u, v, bl)
    low = shifted(up, "lon", 1, True)
    high = shifted(down, "lon", -1, True)
    mid, mid_send = call(
        with_total(middle_sums, total),
        "middle_sums",
        [sds((6, 48, LANES)), sds((6, 48, LANES), BF)],
        5,
        [
            pltpu.VMEM((12, TX, LANES), F32),
            pltpu.VMEM((TX, LANES), F32),
            pltpu.VMEM((4, TX + 16, LANES), F32),
            pltpu.VMEM((TX + 16, LANES), F32),
        ],
        cost=micros(2),
    )(u, v, b, bl, hal)
    mid_in = lax.ppermute(mid_send, "grp", [(1, 0)])
    inner, ready = call(
        with_total(interior, total),
        "interior",
        [sds((8, FORCED, LANES)), TOKEN],
        9,
        [
            pltpu.VMEM((8, TX, LANES), F32),
            pltpu.VMEM((62 * 32, LANES), BF),
            pltpu.VMEM((62 * 32, LANES), BF),
            pltpu.VMEM((60 * 32, LANES), BF),
        ],
        cost=micros(7),
    )(u, v, bl, hal, *weights)
    rim, rim_send, two, edge = call(
        with_total(rim_sums, total),
        "rim_sums",
        [sds((6, 48, LANES)), sds((4, 48, LANES), BF), sds((2, ROWS, LANES)), sds((8, 64, LANES))],
        9,
        [pltpu.VMEM((13, 32, LANES), F32), pltpu.VMEM((4, 48, LANES), F32), pltpu.VMEM((48, LANES), F32)],
        cost=micros(2),
    )(ready, u, v, b, bl, s, hal, low, high)
    rim_in = lax.ppermute(rim_send, "grp", [(1, 0)])
    force = call(
        with_total(edges, total),
        "edges",
        sds((8, FORCED, LANES)),
        7,
        [pltpu.VMEM((52 * 32, LANES), BF), pltpu.VMEM((52 * 32, LANES), BF), pltpu.VMEM((55 * 32, LANES), BF)],
        cost=micros(6),
        aliases={6: 0},
    )(edge, *weights, inner)
    plane = pltpu.VMEM((ROWS, LANES), F32)
    tall = pltpu.VMEM((ROWS + 16, LANES), F32)
    fin, fin_send = call(
        with_total(substeps, total),
        "substeps",
        [sds((2, TX, TY)), sds((4, TX, TY), BF)],
        6,
        [tall, tall] + [plane] * 9,
        cost=micros(5),
    )(two, mid, rim, mid_in, rim_in, force)
    fin_in = lax.ppermute(fin_send, "grp", [(0, 1)])
    own = call(
        with_total(own_part, total),
        "own_part",
        sds((8, TX, TY)),
        8,
        [pltpu.VMEM((4, 96, LANES), F32), pltpu.VMEM((96, LANES), F32)],
        cost=micros(2),
    )(u, v, b, bl, hal, low, high, force)
    return tuple(
        call(finish, "finish", [sds((4, TX, TY)), sds((4, TX, TY)), sds((TX, TY))], 5, cost=micros(2))(
            bl, fin, fin_send, fin_in, own
        )
    )


def solution(mesh):
    tile = P("grp", "lon", "lat")
    flat = P("lon", "lat")
    return jax.shard_map(
        local,
        mesh=mesh,
        in_specs=(tile, tile, tile, tile, flat, flat, P(), P(), P(), P(), P()),
        out_specs=(tile, tile, flat),
        check_vma=False,
    )
```

time: 74.9 us -> 51.2 us (0.68)
  the two profiles are of different devices: /device:TPU:0 before, /device:TPU:1 now
where the time goes in v2:
time: 51.2 us; the launch traced here: 50.8 us
  Pallas kernels  20.8 us (41%)
  starting transfers between devices  14 us (27%)
  waiting for transfers between devices  11.3 us (22%)
  local copies, waits for them, and re-layouts  3.76 us (7%)
  between operations  0.86 us (2%)
    ppermute x4, starting transfers between devices, shifted(): return lax.ppermute(x, axis, pairs)  10.1 us
    pallas_call x1, Pallas kernels, local(): call(with_total(interior, total), 'interior', [sds((8, FORCED, LANES)), T...  5.73 us
    ppermute x1, waiting for transfers between devices, local(): rim_in = lax.ppermute(rim_send, 'grp', [(1, 0)])  4.85 us
    ppermute x1, waiting for transfers between devices, local(): fin_in = lax.ppermute(fin_send, 'grp', [(0, 1)])  4.81 us
    pallas_call x1, Pallas kernels, local(): call(with_total(edges, total), 'edges', sds((8, FORCED, LANES)), 7, [pltp...  4.77 us
    unnamed x19, local copies, waits for them, and re-layouts  3.76 us
    pallas_call x1, Pallas kernels, local(): call(with_total(substeps, total), 'substeps', [sds((2, TX, TY)), sds((4,...  3.34 us
    pallas_call x1, Pallas kernels, local(): call(pack_lat, 'pack_lat', [half, half], 6, [wide, wide, wide, pltpu.VMEM...  2.25 us
  transfers between devices with their start and end apart: 7, of which 3 were waited for; matrix products, arithmetic and copies ran while one was open for 2% of the time, Pallas kernels for 27%

profile of v2, /device:TPU:1, one launch (start us, length us, event | category | flops | bytes accessed | tf_op | source)
XLA Modules:
  0.0 50.8 jit_solution(5848366515363817521)
XLA Ops:
  0.6 0.0 copy-start
  0.6 0.0 copy-start.1
  0.7 2.3 %pack_lat.1 = (bf16[2,64,128]{2,1,0:T(8,128)(2,1)}, bf16[2,64,128]{2,1,0:T(8,128)(2,1)}) custom-call(f32[4,64,512]{2,1,0:T(8,128)} %refs_0_.10, f32[4,64,512]{2,1,0:T(8,128)} %refs_1_.9, f32[4,64,512]{2,1,0:T(8,128)} %refs_2_.11, s32[64,512]{1,0:T(8,128)} %refs_0_.11, f32[64,512]{1,0:T(8,128)} %refs_5_.3), custom_call_target="tpu_custom_call" | custom-call | tf_op jit(solution)/shard_map/pack_lat/pallas_call | solution.py:516
  2.9 4.4 %collective-permute-start = (bf16[2,64,128]{2,1,0:T(8,128)(2,1)}, bf16[2,64,128]{2,1,0:T(8,128)(2,1)S(1)}, u32[]{:S(2)}, u32[]{:S(2)}) collective-permute-start(bf16[2,64,128]{2,1,0:T(8,128)(2,1)} %get-tuple-element.25), channel_id=1, source_target_pairs={{0,2},{2,4},{4,6},{1,3},{3,5},{5,7},{8,10},{10,12},{12,14},{9,11},... | collective-permute-start | bytes 98312 | tf_op jit(solution)/shard_map/ppermute | solution.py:510
  7.3 1.3 %collective-permute-start.1 = (bf16[2,64,128]{2,1,0:T(8,128)(2,1)}, bf16[2,64,128]{2,1,0:T(8,128)(2,1)S(1)}, u32[]{:S(2)}, u32[]{:S(2)}) collective-permute-start(bf16[2,64,128]{2,1,0:T(8,128)(2,1)} %get-tuple-element.26), channel_id=1, source_target_pairs={{2,0},{4,2},{6,4},{3,1},{5,3},{7,5},{10,8},{12,10},{14,12},{11,9},... | collective-permute-start | bytes 98312 | tf_op jit(solution)/shard_map/ppermute | solution.py:510
  8.6 0.8 %copy.14.refs_4_ = bf16[9,32,8]{2,1,0:T(8,128)(2,1)S(1)} copy(bf16[9,32,8]{1,2,0:T(8,128)(2,1)} %param.20) | data formatting | bytes 9216 | tf_op args[10]
  9.5 0.0 copy-start.5
  9.5 0.9 %copy-done.5 = bf16[9,32,32]{2,1,0:T(8,128)(2,1)S(1)} copy-done((bf16[9,32,32]{2,1,0:T(8,128)(2,1)S(1)}, bf16[9,32,32]{2,1,0:T(8,128)(2,1)}, u32[]{:S(2)}) %copy-start.5) | copy-done | bytes 18456
  10.3 0.7 %copy-done.6 = bf16[9,8,32]{2,1,0:T(8,128)(2,1)S(1)} copy-done((bf16[9,8,32]{2,1,0:T(8,128)(2,1)S(1)}, bf16[9,8,32]{2,1,0:T(8,128)(2,1)}, u32[]{:S(2)}) %copy-start.6) | copy-done | bytes 4632
  11.1 0.7 %copy-done.7 = f32[32]{0:T(128)S(1)} copy-done((f32[32]{0:T(128)S(1)}, f32[32]{0:T(128)}, u32[]{:S(2)}) %copy-start.7) | copy-done | bytes 152
  11.7 0.7 %copy-done.8 = f32[32]{0:T(128)S(1)} copy-done((f32[32]{0:T(128)S(1)}, f32[32]{0:T(128)}, u32[]{:S(2)}) %copy-start.8) | copy-done | bytes 152
  12.4 0.3 weights.1
  12.7 0.0 collective-permute-done.refs_1_
  12.7 0.0 collective-permute-done.1.refs_2_
  12.7 0.3 pack_lon.1
  13.0 4.5 %collective-permute-start.2 = (bf16[15,16,640]{2,1,0:T(8,128)(2,1)S(1)}, bf16[15,16,640]{2,1,0:T(8,128)(2,1)S(1)}, u32[]{:S(2)}, u32[]{:S(2)}) collective-permute-start(bf16[15,16,640]{2,1,0:T(8,128)(2,1)S(1)} %get-tuple-element.34), channel_id=1, source_target_pairs={{0,8},{8,16},{16,24},{24,32},{32,40},{40,48},{48,56},{56,64},{64,7... | collective-permute-start | bytes 921608 | tf_op jit(solution)/shard_map/ppermute | solution.py:510
  17.5 0.0 collective-permute-start.3
  17.5 1.0 %middle_sums.1 = (f32[6,48,640]{2,1,0:T(8,128)S(1)}, bf16[6,48,640]{2,1,0:T(8,128)(2,1)S(1)}) custom-call(f32[4,64,512]{2,1,0:T(8,128)S(1)} %copy-done, f32[4,64,512]{2,1,0:T(8,128)S(1)} %copy-done.1, f32[4,64,512]{2,1,0:T(8,128)S(1)} %copy-done.2, s32[64,512]{1,0:T(8,128)S(1)} %copy-done.3, f32[14,64,128]{2,1,0:T(8,128)S(1)} %get-tuple-element.27.refs_3_.refs_6_.refs_4_), custom_call_target="tpu_custom_call" | custom-call | flops 2000000 | bytes 6000000 | tf_op jit(solution)/shard_map/middle_sums/pallas_call | solution.py:547
  18.5 1.3 %collective-permute-start.4 = (bf16[6,48,640]{2,1,0:T(8,128)(2,1)S(1)}, bf16[6,48,640]{2,1,0:T(8,128)(2,1)S(1)}, u32[]{:S(2)}, u32[]{:S(2)}) collective-permute-start(bf16[6,48,640]{2,1,0:T(8,128)(2,1)S(1)} %get-tuple-element.39), channel_id=1, source_target_pairs={{1,0},{3,2},{5,4},{7,6},{9,8},{11,10},{13,12},{15,14},{17,16},{19,... | collective-permute-start | bytes 1105928 | tf_op jit(solution)/shard_map/ppermute | solution.py:560
  19.8 5.7 %interior.1 = (f32[8,104,640]{2,1,0:T(8,128)S(1)}, f32[8,128]{1,0:T(8,128)S(1)}) custom-call(f32[4,64,512]{2,1,0:T(8,128)S(1)} %copy-done, f32[4,64,512]{2,1,0:T(8,128)S(1)} %copy-done.1, s32[64,512]{1,0:T(8,128)S(1)} %copy-done.3, f32[14,64,128]{2,1,0:T(8,128)S(1)} %get-tuple-element.27.refs_3_.refs_6_.refs_4_, ...), custom_call_target="tpu_custom_call" | custom-call | flops 7000000 | bytes 21000000 | tf_op jit(solution)/shard_map/interior/pallas_call | solution.py:561
  25.5 0.0 collective-permute-done.2.refs_7_.refs_5_
  25.5 1.7 %collective-permute-done.3.refs_8_.refs_6_ = bf16[15,16,640]{2,1,0:T(8,128)(2,1)S(1)} collective-permute-done((bf16[15,16,640]{2,1,0:T(8,128)(2,1)S(1)}, bf16[15,16,640]{2,1,0:T(8,128)(2,1)S(1)}, u32[]{:S(2)}, u32[]{:S(2)}) %collective-permute-start.3) | collective-permute-done | bytes 307232 | tf_op jit(solution)/shard_map/ppermute | solution.py:510
  27.2 1.0 %rim_sums.1 = (f32[6,48,640]{2,1,0:T(8,128)S(1)}, bf16[4,48,640]{2,1,0:T(8,128)(2,1)S(1)}, f32[2,96,640]{2,1,0:T(8,128)S(1)}, f32[8,64,640]{2,1,0:T(8,128)S(1)}) custom-call(f32[8,128]{1,0:T(8,128)S(1)} %get-tuple-element.33.refs_0_, f32[4,64,512]{2,1,0:T(8,128)S(1)} %copy-done, f32[4,64,512]{2,1,0:T(8,128)S(1)} %copy-done.1, f32[4,64,512]{2,1,0:T(8,128)S(1)} %copy-done.2, ...), custom_call_target="tpu_custom_call" | custom-call | flops 2000000 | bytes 6000000 | tf_op jit(solution)/shard_map/rim_sums/pallas_call | solution.py:574
  28.2 1.3 %collective-permute-start.5 = (bf16[4,48,640]{2,1,0:T(8,128)(2,1)S(1)}, bf16[4,48,640]{2,1,0:T(8,128)(2,1)S(1)}, u32[]{:S(2)}, u32[]{:S(2)}) collective-permute-start(bf16[4,48,640]{2,1,0:T(8,128)(2,1)S(1)} %get-tuple-element.40), channel_id=1, source_target_pairs={{1,0},{3,2},{5,4},{7,6},{9,8},{11,10},{13,12},{15,14},{17,16},{19,... | collective-permute-start | bytes 737288 | tf_op jit(solution)/shard_map/ppermute | solution.py:582
  29.5 4.8 %edges.1.refs_5_.refs_7_ = f32[8,104,640]{2,1,0:T(8,128)S(1)} custom-call(f32[8,64,640]{2,1,0:T(8,128)S(1)} %get-tuple-element.41.refs_0_, bf16[192,256]{1,0:T(8,128)(2,1)S(1)} %get-tuple-element.28.refs_4_.refs_1_, bf16[576,256]{1,0:T(8,128)(2,1)S(1)} %get-tuple-element.29.refs_5_.refs_2_, ...), custom_call_target="tpu_custom_call", output_to_operand_aliasing={{}: (6, {})} | custom-call | flops 6000000 | bytes 18000000 | tf_op jit(solution)/shard_map/edges/pallas_call | solution.py:583
  34.3 0.0 collective-permute-done.4.refs_3_
  34.3 4.8 %collective-permute-done.5.refs_4_ = bf16[4,48,640]{2,1,0:T(8,128)(2,1)S(1)} collective-permute-done((bf16[4,48,640]{2,1,0:T(8,128)(2,1)S(1)}, bf16[4,48,640]{2,1,0:T(8,128)(2,1)S(1)}, u32[]{:S(2)}, u32[]{:S(2)}) %collective-permute-start.5) | collective-permute-done | bytes 245792 | tf_op jit(solution)/shard_map/ppermute | solution.py:582
  39.1 3.3 %substeps.1 = (f32[2,64,512]{2,1,0:T(8,128)S(1)}, bf16[4,64,512]{2,1,0:T(8,128)(2,1)S(1)}) custom-call(f32[2,96,640]{2,1,0:T(8,128)S(1)} %get-tuple-element.36.refs_0_, f32[6,48,640]{2,1,0:T(8,128)S(1)} %get-tuple-element.37.refs_1_, f32[6,48,640]{2,1,0:T(8,128)S(1)} %get-tuple-element.38.refs_2_, bf16[6,48,640]{2,1,0:T(8,128)(2,1)S(1)} %collective-permute-done.4.refs_3_, ...), custom_call_target="tpu_custom_call" | custom-call | flops 5000000 | bytes 15000000 | tf_op jit(solution)/shard_map/substeps/pallas_call | solution.py:594
  42.5 1.3 %collective-permute-start.6 = (bf16[4,64,512]{2,1,0:T(8,128)(2,1)S(1)}, bf16[4,64,512]{2,1,0:T(8,128)(2,1)S(1)}, u32[]{:S(2)}, u32[]{:S(2)}) collective-permute-start(bf16[4,64,512]{2,1,0:T(8,128)(2,1)S(1)} %get-tuple-element.44.refs_2_), channel_id=1, source_target_pairs={{0,1},{2,3},{4,5},{6,7},{8,9},{10,11},{12,13},{14,15},{16,17},{18,... | collective-permute-start | bytes 786440 | tf_op jit(solution)/shard_map/ppermute | solution.py:602
  43.8 1.1 %own_part.1.refs_4_ = f32[8,64,512]{2,1,0:T(8,128)S(1)} custom-call(f32[4,64,512]{2,1,0:T(8,128)S(1)} %copy-done, f32[4,64,512]{2,1,0:T(8,128)S(1)} %copy-done.1, f32[4,64,512]{2,1,0:T(8,128)S(1)} %copy-done.2, s32[64,512]{1,0:T(8,128)S(1)} %copy-done.3, f32[14,64,128]{2,1,0:T(8,128)S(1)} %get-tuple-element.27.refs_3_.refs_6_.refs_4_, ...), custom_call_target="tpu_custom_call" | custom-call | flops 2000000 | bytes 6000000 | tf_op jit(solution)/shard_map/own_part/pallas_call | solution.py:603
  44.9 4.8 %collective-permute-done.6.refs_3_ = bf16[4,64,512]{2,1,0:T(8,128)(2,1)S(1)} collective-permute-done((bf16[4,64,512]{2,1,0:T(8,128)(2,1)S(1)}, bf16[4,64,512]{2,1,0:T(8,128)(2,1)S(1)}, u32[]{:S(2)}, u32[]{:S(2)}) %collective-permute-start.6) | collective-permute-done | bytes 262176 | tf_op jit(solution)/shard_map/ppermute | solution.py:602
  49.7 1.1 %finish.1 = (f32[4,64,512]{2,1,0:T(8,128)}, f32[4,64,512]{2,1,0:T(8,128)}, f32[64,512]{1,0:T(8,128)}) custom-call(s32[64,512]{1,0:T(8,128)S(1)} %copy-done.3, f32[2,64,512]{2,1,0:T(8,128)S(1)} %get-tuple-element.43.refs_1_, bf16[4,64,512]{2,1,0:T(8,128)(2,1)S(1)} %get-tuple-element.44.refs_2_, bf16[4,64,512]{2,1,0:T(8,128)(2,1)S(1)} %collective-permute-done.6.refs_3_, ...), custom_call_target="tpu_custom_call" | custom-call | flops 2000000 | bytes 6000000 | tf_op jit(solution)/shard_map/finish/pallas_call | solution.py:612
  (11 shorter events, 0.0 us)
Async XLA Ops:
  0.6 12.1 %copy-start = (f32[4,64,512]{2,1,0:T(8,128)S(1)}, f32[4,64,512]{2,1,0:T(8,128)}, u32[]{:S(2)}) copy-start(f32[4,64,512]{2,1,0:T(8,128)} %refs_0_.10) | copy-start | bytes 1572868
  0.6 12.1 %copy-start.1 = (f32[4,64,512]{2,1,0:T(8,128)S(1)}, f32[4,64,512]{2,1,0:T(8,128)}, u32[]{:S(2)}) copy-start(f32[4,64,512]{2,1,0:T(8,128)} %refs_1_.9) | copy-start | bytes 1572868
  0.7 12.1 %copy-start.2 = (f32[4,64,512]{2,1,0:T(8,128)S(1)}, f32[4,64,512]{2,1,0:T(8,128)}, u32[]{:S(2)}) copy-start(f32[4,64,512]{2,1,0:T(8,128)} %refs_2_.11) | copy-start | bytes 1572868
  0.7 12.1 %copy-start.3 = (s32[64,512]{1,0:T(8,128)S(1)}, s32[64,512]{1,0:T(8,128)}, u32[]{:S(2)}) copy-start(s32[64,512]{1,0:T(8,128)} %refs_0_.11) | copy-start | bytes 393220
  0.7 12.1 %copy-start.4 = (f32[64,512]{1,0:T(8,128)S(1)}, f32[64,512]{1,0:T(8,128)}, u32[]{:S(2)}) copy-start(f32[64,512]{1,0:T(8,128)} %refs_5_.3) | copy-start | bytes 393220
  2.9 9.7 %collective-permute-start = (bf16[2,64,128]{2,1,0:T(8,128)(2,1)}, bf16[2,64,128]{2,1,0:T(8,128)(2,1)S(1)}, u32[]{:S(2)}, u32[]{:S(2)}) collective-permute-start(bf16[2,64,128]{2,1,0:T(8,128)(2,1)} %get-tuple-element.25), channel_id=1, source_target_pairs={{0,2},{2,4},{4,6},{1,3},{3,5},{5,7},{8,10},{10,12},{12,14},{9,11},... | collective-permute-start | bytes 98312 | tf_op jit(solution)/shard_map/ppermute | solution.py:510
  7.3 5.3 %collective-permute-start.1 = (bf16[2,64,128]{2,1,0:T(8,128)(2,1)}, bf16[2,64,128]{2,1,0:T(8,128)(2,1)S(1)}, u32[]{:S(2)}, u32[]{:S(2)}) collective-permute-start(bf16[2,64,128]{2,1,0:T(8,128)(2,1)} %get-tuple-element.26), channel_id=1, source_target_pairs={{2,0},{4,2},{6,4},{3,1},{5,3},{7,5},{10,8},{12,10},{14,12},{11,9},... | collective-permute-start | bytes 98312 | tf_op jit(solution)/shard_map/ppermute | solution.py:510
  9.5 0.9 %copy-start.5 = (bf16[9,32,32]{2,1,0:T(8,128)(2,1)S(1)}, bf16[9,32,32]{2,1,0:T(8,128)(2,1)}, u32[]{:S(2)}) copy-start(bf16[9,32,32]{2,1,0:T(8,128)(2,1)} %refs_2_.6) | copy-start | bytes 55300
  10.3 0.7 %copy-start.6 = (bf16[9,8,32]{2,1,0:T(8,128)(2,1)S(1)}, bf16[9,8,32]{2,1,0:T(8,128)(2,1)}, u32[]{:S(2)}) copy-start(bf16[9,8,32]{2,1,0:T(8,128)(2,1)} %refs_0_.6) | copy-start | bytes 13828
  11.1 0.7 %copy-start.7 = (f32[32]{0:T(128)S(1)}, f32[32]{0:T(128)}, u32[]{:S(2)}) copy-start(f32[32]{0:T(128)} %param.17) | copy-start | bytes 388
  11.7 0.7 %copy-start.8 = (f32[32]{0:T(128)S(1)}, f32[32]{0:T(128)}, u32[]{:S(2)}) copy-start(f32[32]{0:T(128)} %param.19) | copy-start | bytes 388
  13.0 12.5 %collective-permute-start.2 = (bf16[15,16,640]{2,1,0:T(8,128)(2,1)S(1)}, bf16[15,16,640]{2,1,0:T(8,128)(2,1)S(1)}, u32[]{:S(2)}, u32[]{:S(2)}) collective-permute-start(bf16[15,16,640]{2,1,0:T(8,128)(2,1)S(1)} %get-tuple-element.34), channel_id=1, source_target_pairs={{0,8},{8,16},{16,24},{24,32},{32,40},{40,48},{48,56},{56,64},{64,7... | collective-permute-start | bytes 921608 | tf_op jit(solution)/shard_map/ppermute | solution.py:510
  17.5 9.7 %collective-permute-start.3 = (bf16[15,16,640]{2,1,0:T(8,128)(2,1)S(1)}, bf16[15,16,640]{2,1,0:T(8,128)(2,1)S(1)}, u32[]{:S(2)}, u32[]{:S(2)}) collective-permute-start(bf16[15,16,640]{2,1,0:T(8,128)(2,1)S(1)} %get-tuple-element.35), channel_id=1, source_target_pairs={{0,120},{8,0},{16,8},{24,16},{32,24},{40,32},{48,40},{56,48},{64,5... | collective-permute-start | bytes 921608 | tf_op jit(solution)/shard_map/ppermute | solution.py:510
  18.5 15.8 %collective-permute-start.4 = (bf16[6,48,640]{2,1,0:T(8,128)(2,1)S(1)}, bf16[6,48,640]{2,1,0:T(8,128)(2,1)S(1)}, u32[]{:S(2)}, u32[]{:S(2)}) collective-permute-start(bf16[6,48,640]{2,1,0:T(8,128)(2,1)S(1)} %get-tuple-element.39), channel_id=1, source_target_pairs={{1,0},{3,2},{5,4},{7,6},{9,8},{11,10},{13,12},{15,14},{17,16},{19,... | collective-permute-start | bytes 1105928 | tf_op jit(solution)/shard_map/ppermute | solution.py:560
  28.2 10.9 %collective-permute-start.5 = (bf16[4,48,640]{2,1,0:T(8,128)(2,1)S(1)}, bf16[4,48,640]{2,1,0:T(8,128)(2,1)S(1)}, u32[]{:S(2)}, u32[]{:S(2)}) collective-permute-start(bf16[4,48,640]{2,1,0:T(8,128)(2,1)S(1)} %get-tuple-element.40), channel_id=1, source_target_pairs={{1,0},{3,2},{5,4},{7,6},{9,8},{11,10},{13,12},{15,14},{17,16},{19,... | collective-permute-start | bytes 737288 | tf_op jit(solution)/shard_map/ppermute | solution.py:582
  42.5 7.2 %collective-permute-start.6 = (bf16[4,64,512]{2,1,0:T(8,128)(2,1)S(1)}, bf16[4,64,512]{2,1,0:T(8,128)(2,1)S(1)}, u32[]{:S(2)}, u32[]{:S(2)}) collective-permute-start(bf16[4,64,512]{2,1,0:T(8,128)(2,1)S(1)} %get-tuple-element.44.refs_2_), channel_id=1, source_target_pairs={{0,1},{2,3},{4,5},{6,7},{8,9},{10,11},{12,13},{14,15},{16,17},{18,... | collective-permute-start | bytes 786440 | tf_op jit(solution)/shard_map/ppermute | solution.py:602

commit v3 on v2

--- a/solution.py
+++ b/solution.py
@@ -49,7 +49,10 @@
     return jnp.where((y >= 0) & (y < total), 1.0, 0.0)
 
 
-def pack_lat(sc, u, v, b, l, s, to_down, to_up, ub, vb, bb, lb, sb, sem):
+def pack_lat(sc, u, v, b, l, s, *refs):
+    raw, to_down, to_up, made = refs[:5], refs[5], refs[6], refs[7:12]
+    ub, vb, bb, lb, sb, sem = refs[12:18]
+    held, spread, weight_sem = refs[18:23], refs[23], refs[24]
     base = 4 * sc[0]
     lane = lax.broadcasted_iota(jnp.int32, (TX, 128), 1)
     copies = []
@@ -58,10 +61,9 @@
             copies.append(pltpu.make_async_copy(src.at[:, :, at : at + 128], dst.at[side], sem.at[side, n]))
         for n, (src, dst) in enumerate(((l, lb), (s, sb))):
             copies.append(pltpu.make_async_copy(src.at[:, at : at + 128], dst.at[side], sem.at[side, 3 + n]))
-    for copy in copies:
+    more = [pltpu.make_async_copy(src, dst, weight_sem.at[n]) for n, (src, dst) in enumerate(zip(raw, held))]
+    for copy in copies + more:
         copy.start()
-    for copy in copies:
-        copy.wait()
 
     def fields(side):
         bl = lb[side].astype(F32)
@@ -73,6 +75,8 @@
         yield sb[side]
 
     for side, (out, origin) in enumerate(((to_down, 0), (to_up, 128 - EDGE))):
+        for copy in copies[5 * side : 5 * side + 5]:
+            copy.wait()
         for i, field in enumerate(fields(side)):
             tile, place = divmod(i, 7)
             if place == 0:
@@ -81,19 +85,24 @@
             acc = jnp.where((lane >= EDGE * place) & (lane < EDGE * (place + 1)), moved, acc)
             if place == 6:
                 out[tile] = acc.astype(BF)
-
-
-def pack_lon(sc, ready, before, after, *refs):
+    for copy in more:
+        copy.wait()
+    build_weights(*held, *made, spread)
+
+
+def pack_lon(total, sc, summed, before, after, *refs):
     tops, bots, extra_t, extra_b = refs[0:5], refs[5:10], refs[10:13], refs[13:16]
     hal, to_down, to_up, work = refs[16:]
     base = 4 * sc[0]
     lane = lax.broadcasted_iota(jnp.int32, (TX, 128), 1)
+    low_from = jnp.where(sc[1] > 0, 128 - EDGE, 128)
+    high_to = jnp.where(sc[1] < total // TY - 1, EDGE, 0)
     for tile in range(2):
         low, high = before[tile].astype(F32), after[tile].astype(F32)
         for place in range(7):
             a = pltpu.roll(high, (-EDGE * place) % 128, 1)
             b = pltpu.roll(low, (128 - EDGE - EDGE * place) % 128, 1)
-            hal[tile * 7 + place] = jnp.where(lane < EDGE, a, jnp.where(lane >= 128 - EDGE, b, 0.0))
+            hal[tile * 7 + place] = jnp.where(lane < high_to, a, jnp.where(lane >= low_from, b, 0.0))
     for out, (u, v, b, l, s), row in ((to_down, tops, 0), (to_up, bots, TX - 16)):
         bl = l[...].astype(F32)
         for k in range(4):
@@ -115,9 +124,7 @@
         out[14] = work[...].astype(BF)
 
 
-def build_weights(sc, w_in, b_in, w_mid, b_mid, w_out, w1, w2, w3, b1, b2, done, spread):
-    done[...] = jnp.zeros_like(done)
-
+def build_weights(w_in, b_in, w_mid, b_mid, w_out, w1, w2, w3, b1, b2, spread):
     def across(parts, rows, cols):
         rows_all = sum(p.shape[0] for p in parts)
         full = jnp.concatenate(parts + [jnp.zeros((128 - rows_all, 128), F32)], 0)
@@ -139,8 +146,7 @@
         mid = jnp.concatenate([mid, jnp.zeros((32, 128), F32)], 1)
         for p in range(6):
             w2[192 * b + 32 * p : 192 * b + 32 * p + 32, :] = pltpu.roll(mid, 32 * p, 1).astype(BF)
-        last = across([wide(w_out[3 * a + b].astype(F32)) for a in range(3)], 8, 96)
-        last = jnp.concatenate([last, jnp.zeros((8, 256), F32)], 1)
+        last = jnp.concatenate([w_out[3 * a + b].astype(F32) for a in range(3)] + [jnp.zeros((8, 288), F32)], 1)
         for p in range(8):
             spread[:, p, :] = pltpu.roll(last, 32 * p, 1)
         w3[64 * b : 64 * b + 64, :] = spread[...].reshape(64, 384)[:, :320].astype(BF)
@@ -223,7 +229,7 @@
 
 def pressures(base, b_rows, pr, load, rows):
     for r in range(0, rows, 8):
-        run = jnp.zeros((8, LANES), F32)
+        run = jnp.zeros((8, pr.shape[2]), F32)
         for k in range(4):
             weighted = b_rows(k, r) * (1.0 + 0.25 * (base + k).astype(F32))
             pr[k, r + 8 : r + 16, :] = run + 0.5 * weighted
@@ -234,17 +240,26 @@
 def grads(ref, r):
     here = ref[r + 8 : r + 16, :]
     gx = (ref[r + 9 : r + 17, :] - ref[r + 7 : r + 15, :]) * 0.5
-    gy = (pltpu.roll(here, LANES - 1, 1) - pltpu.roll(here, 1, 1)) * 0.5
+    gy = (pltpu.roll(here, here.shape[1] - 1, 1) - pltpu.roll(here, 1, 1)) * 0.5
     return gx, gy
+
+
+def open_grads(ref, r):
+    here = ref[r + 8 : r + 16, :]
+    lane = lax.broadcasted_iota(jnp.int32, here.shape, 1)
+    gx = (ref[r + 9 : r + 17, :] - ref[r + 7 : r + 15, :]) * 0.5
+    right = jnp.where(lane == TY - 1, 0.0, pltpu.roll(here, TY - 1, 1))
+    left = jnp.where(lane == 0, 0.0, pltpu.roll(here, 1, 1))
+    return gx, (right - left) * 0.5
 
 
 def coriolis_of(lat, total, shape):
     return coriolis_base + coriolis_slope * (latitudes(lat, shape).astype(F32) * (1.0 / total) - 0.5)
 
 
-def sums_of(sc, coriolis, level, east, north, pr, load, r):
+def sums_of(sc, coriolis, level, east, north, pr, load, r, grads=grads):
     base = 4 * sc[0]
-    te = jnp.zeros((8, LANES), F32)
+    te = jnp.zeros(level.shape, F32)
     tn, us, vs = te, te, te
     for k in range(4):
         number = (base + k).astype(F32)
@@ -257,7 +272,7 @@
         tn = tn + weight * (-coriolis * e - press_coef * gy - drag * n)
         us = us + thick * e
         vs = vs + thick * n
-    below = jnp.zeros((8, LANES), F32)
+    below = jnp.zeros(level.shape, F32)
     for k in range(4, 8):
         below = below + jnp.where(level > float(k), 1.0 + 0.25 * k, 0.0)
     gx, gy = grads(load, r)
@@ -265,36 +280,70 @@
     return te - below * gx, tn - below * gy, us, vs, gx, gy
 
 
-def middle_sums(total, sc, u, v, b, bl, hal, sums, send, ext, lev, pr, load):
+def closed(pr, load):
+    for ref in [pr.at[k] for k in range(4)] + [load]:
+        end = ref.shape[0]
+        ref[0:8, :] = jnp.zeros((8, ref.shape[1]), F32)
+        ref[end - 8 : end, :] = jnp.zeros((8, ref.shape[1]), F32)
+
+
+def middle_sums(total, sc, u, v, b, bl, s, sums, send, done, pr, load):
+    done[...] = jnp.zeros_like(done)
     base = 4 * sc[0]
-    level = bl[...].astype(F32)
-    for k in range(4):
-        wet = wet_of(level, (base + k).astype(F32))
-        for n, a in enumerate((u, v, b)):
-            ext[4 * n + k, :, :TY] = a[k] * wet
-    for i in range(12):
-        ext[i, :, TY:] = hal[i]
-    lev[:, :TY] = level
-    lev[:, TY:] = hal[12]
-    pressures(base, lambda k, r: ext[8 + k, r : r + 8, :], pr, load, TX)
-    coriolis = coriolis_of(sc[1], total, (8, LANES))
-    for q in range(0, 48, 16):
+
+    def wet(k, rr):
+        return wet_of(bl[rr, :].astype(F32), (base + k).astype(F32))
+
+    def b_rows(k, r):
+        rr = slice(r, r + 8)
+        return b[k, rr, :] * wet(k, rr)
+
+    pressures(base, b_rows, pr, load, TX)
+    closed(pr, load)
+    coriolis = coriolis_of(sc[1], total, (8, LANES))[:, :TY]
+    for q in range(0, TX, 16):
         halves = []
-        for r in (q + 8, q + 16):
+        for r in (q, q + 8):
             rr = slice(r, r + 8)
-            found = sums_of(sc, coriolis, lev[rr, :], lambda k: ext[k, rr, :], lambda k: ext[4 + k, rr, :], pr, load, r)
+            level = bl[rr, :].astype(F32)
+            found = sums_of(
+                sc, coriolis, level, lambda k: u[k, rr, :] * wet(k, rr), lambda k: v[k, rr, :] * wet(k, rr), pr, load, r, open_grads
+            )
             for i, a in enumerate(found):
-                sums[i, r - 8 : r, :] = a
+                sums[i, rr, :] = a
             halves.append(found)
         for i in range(4):
             a = jnp.concatenate([halves[0][i], halves[1][i]], 0)
-            high = a.astype(BF)
-            send[i, q : q + 16, :] = high
-            if i < 2:
-                send[4 + i, q : q + 16, :] = (a - high.astype(F32)).astype(BF)
-
-
-def rim_sums(total, sc, ready, u, v, b, bl, s, hal, low, high, sums, send, two, edge, ext, pr, load):
+            send[i, q : q + 16, :] = a.astype(BF)
+
+
+def seam_sums(total, sc, u, v, b, bl, hal, sums, ext, pr, load):
+    base = 4 * sc[0]
+    last, first = slice(TY - 128, TY), slice(0, 128)
+
+    def three(a, outer, b):
+        return jnp.concatenate([a, outer, b], 1)
+
+    for r in range(0, TX, 8):
+        rr = slice(r, r + 8)
+        levels = [bl[rr, at].astype(F32) for at in (last, first)]
+        ext[12, rr, :] = three(levels[0], hal[12, rr, :], levels[1])
+        for k in range(4):
+            wets = [wet_of(level, (base + k).astype(F32)) for level in levels]
+            for n, a in enumerate((u, v, b)):
+                ext[4 * n + k, rr, :] = three(a[k, rr, last] * wets[0], hal[4 * n + k, rr, :], a[k, rr, first] * wets[1])
+    pressures(base, lambda k, r: ext[8 + k, r : r + 8, :], pr, load, TX)
+    closed(pr, load)
+    whole = coriolis_of(sc[1], total, (8, LANES))
+    coriolis = three(whole[:, last], whole[:, TY:], whole[:, first])
+    for r in range(0, TX, 8):
+        rr = slice(r, r + 8)
+        found = sums_of(sc, coriolis, ext[12, rr, :], lambda k: ext[k, rr, :], lambda k: ext[4 + k, rr, :], pr, load, r)
+        for i, a in enumerate(found):
+            sums[i, rr, :] = a
+
+
+def rim_sums(total, sc, ready, u, v, b, bl, s, hal, low, high, seam, sums, send, two, edge, ext, pr, load):
     base = 4 * sc[0]
     tall = 32
     for side, halo in ((0, low), (1, high)):
@@ -339,8 +388,23 @@
     two[1, 16:80, :TY] = s[...]
     for i in range(2):
         two[i, 16:80, TY:] = hal[12 + i]
+    lane = lax.broadcasted_iota(jnp.int32, (16, 128), 1)
     for i in range(4):
-        send[i] = sums[i].astype(BF)
+        for side in range(2):
+            at = slice(0, 16) if side == 0 else slice(32, 48)
+            packed = sums[i, at, TY:]
+            for turn in range(2):
+                base = 16 + 34 * turn
+                own = slice(16 * (2 * turn + side), 16 * (2 * turn + side) + 16)
+                outer, before, after = seam[i, own, 128:256], seam[i, own, 0:128], seam[i, own, 256:384]
+                packed = jnp.where((lane >= base) & (lane < base + 16), pltpu.roll(outer, base, 1), packed)
+                packed = jnp.where((lane >= base + 16) & (lane < base + 32), pltpu.roll(outer, base + 32, 1), packed)
+                packed = jnp.where(lane == base + 32, pltpu.roll(before, base + 33, 1), packed)
+                packed = jnp.where(lane == base + 33, pltpu.roll(after, base + 33, 1), packed)
+            send[2 * i + side, :, :TY] = sums[i, at, :TY].astype(BF)
+            send[2 * i + side, :, TY:] = packed.astype(BF)
+    ends = [sums[i, row : row + 1, :] for i in range(4) for row in (16, 31)]
+    send[8] = jnp.concatenate(ends + [jnp.zeros((8, LANES), F32)], 0).astype(BF)
 
 
 def own_part(total, sc, u, v, b, bl, hal, low, high, force, out, pr, load):
@@ -376,10 +440,18 @@
             out[4 + k, rr, :] = wet * (north + step_dt * (tn + fn))
 
 
-def substeps(total, sc, two, mid, rim, mid_in, rim_in, force, fin, send, lv, fx, fy, eb, nb, ae, an, es, ns, rel, c2):
+def substeps(total, sc, two, mid, seam, rim, mid_in, rim_in, force, fin, send, lv, fx, fy, eb, nb, ae, an, es, ns, rel, c2):
     @pl.when(sc[0] == 0)
     def _():
         zero8 = jnp.zeros((8, LANES), F32)
+        lane = lax.broadcasted_iota(jnp.int32, (8, 128), 1)
+
+        def ended(i, at, outer):
+            first = jnp.where(lane == 0, seam[i, at, 256:384], mid[i, at, 0:128])
+            last = jnp.where(lane == 127, seam[i, at, 0:128], mid[i, at, TY - 128 :])
+            pieces = [first, mid[i, at, 128 : TY - 128], last]
+            return jnp.concatenate(pieces + [seam[i, at, 128:256]] if outer else pieces, 1)
+
         for ref in (lv, fx):
             ref[0:8, :] = zero8
             ref[ROWS + 8 : ROWS + 16, :] = zero8
@@ -393,15 +465,27 @@
             middle = RIM <= r < ROWS - RIM
             at = r - RIM if middle else (r if r < RIM else r - 48)
             at = slice(at, at + 8)
-            mine, theirs = (mid, mid_in) if middle else (rim, rim_in)
-            pair, half = at.start // 16 * 16, at.start % 16
-
-            def other(i):
-                return theirs[i, pair : pair + 16, :].astype(F32)[half : half + 8]
-
-            found = [mine[i, at, :] + other(i) for i in range(4)]
-            if middle:
-                found[:2] = [found[i] + other(4 + i) for i in range(2)]
+            x = r - HALO
+            found = []
+            for i in range(4):
+                own = ended(i, slice(x, x + 8), True) if middle else rim[i, at, :]
+                if not 0 <= x < TX:
+                    row = r % 16
+                    found.append(own + rim_in[2 * i + (x > 0), :, :].astype(F32)[row : row + 8])
+                    continue
+                turn, half = x // 32, x % 16
+                base = 16 + 34 * turn
+                beyond = rim_in[2 * i + x // 16 % 2, :, TY:].astype(F32)[half : half + 8]
+                theirs = mid_in[i, x - half : x - half + 16, :].astype(F32)[half : half + 8]
+                outer = jnp.where(lane < 16, pltpu.roll(beyond, 128 - base, 1), pltpu.roll(beyond, 96 - base, 1))
+                first = jnp.where(lane == 0, pltpu.roll(beyond, 95 - base, 1), theirs[:, 0:128])
+                last = jnp.where(lane == 127, pltpu.roll(beyond, 95 - base, 1), theirs[:, TY - 128 :])
+                theirs = jnp.concatenate([first, theirs[:, 128 : TY - 128], last, outer], 1)
+                if x in (0, TX - 8):
+                    end = rim_in[8].astype(F32)[2 * i + (x > 0) : 2 * i + (x > 0) + 1]
+                    row = lax.broadcasted_iota(jnp.int32, (8, LANES), 0)
+                    theirs = jnp.where(row == (0 if x == 0 else 7), end, theirs)
+                found.append(own + theirs)
             for k in range(4):
                 weight = jnp.where(level > float(k), 1.0 + 0.25 * k, 0.0)
                 found[0] = found[0] + weight * force[k, r + 4 : r + 12, :]
@@ -414,8 +498,8 @@
             lv[r + 8 : r + 16, :] = two[1, rr, :]
         inside = inside_of(sc[1], total, (8, LANES))
 
-        def step(_, carry):
-            for r in range(0, ROWS, 8):
+        def step(first, carry):
+            for r in range(first, ROWS - first, 8):
                 rr = slice(r, r + 8)
                 here = lv[r + 8 : r + 16, :]
                 dx = lv[r + 9 : r + 17, :] - lv[r + 7 : r + 15, :]
@@ -427,7 +511,7 @@
                 nb[rr, :] = n
                 fx[r + 8 : r + 16, :] = rel[rr, :] * e
                 fy[rr, :] = rel[rr, :] * n
-            for r in range(0, ROWS, 8):
+            for r in range(first, ROWS - first, 8):
                 rr = slice(r, r + 8)
                 dx = fx[r + 9 : r + 17, :] - fx[r + 7 : r + 15, :]
                 f = fy[rr, :]
@@ -435,7 +519,8 @@
                 lv[r + 8 : r + 16, :] = inside * (lv[r + 8 : r + 16, :] - (0.5 * sub_dt) * (dx + dy))
             return carry
 
-        lax.fori_loop(0, NSUB, step, 0)
+        lax.fori_loop(0, NSUB // 2, lambda _, carry: step(0, carry), 0)
+        lax.fori_loop(0, NSUB // 2, lambda _, carry: step(8, carry), 0)
         for q in range(0, TX, 16):
             r = q + HALO
             rr, at = slice(r, r + 16), slice(q, q + 16)
@@ -447,7 +532,7 @@
                 pieces = []
                 for p in (r, r + 8):
                     if RIM <= p < ROWS - RIM:
-                        pieces.append(mid[i, p - RIM : p - RIM + 8, :TY])
+                        pieces.append(ended(i, slice(p - HALO, p - HALO + 8), False))
                     else:
                         p = p if p < RIM else p - 48
                         pieces.append(rim[i, p : p + 8, :TY])
@@ -504,60 +589,74 @@
     return pl.CostEstimate(flops=int(us * 1e6), bytes_accessed=int(us * 3e6), transcendentals=0)
 
 
-def shifted(x, axis, by, ring):
+def shifted(x, axis, by):
     size = lax.axis_size(axis)
-    pairs = [(i, (i + by) % size) for i in range(size) if ring or 0 <= i + by < size]
-    return lax.ppermute(x, axis, pairs)
+    return lax.ppermute(x, axis, [(i, (i + by) % size) for i in range(size)])
 
 
 def local(u, v, b, wet_mask, bl, s, w_in, b_in, w_mid, b_mid, w_out):
     total = TY * lax.axis_size("lat")
     wide, half = pltpu.VMEM((2, 4, TX, 128), F32), sds((2, TX, 128), BF)
-    to_down, to_up = call(
+    made = [sds((192, 256), BF), sds((576, 256), BF), sds((192, 320), BF), sds((192, 128)), sds((192, 128))]
+    to_down, to_up, *weights = call(
         pack_lat,
         "pack_lat",
-        [half, half],
-        6,
-        [wide, wide, wide, pltpu.VMEM((2, TX, 128), jnp.int32), pltpu.VMEM((2, TX, 128), F32), pltpu.SemaphoreType.DMA((2, 5))],
-        in_specs=[pl.BlockSpec(memory_space=pltpu.HBM)] * 5,
+        [half, half] + made,
+        10,
+        [
+            wide,
+            wide,
+            wide,
+            pltpu.VMEM((2, TX, 128), jnp.int32),
+            pltpu.VMEM((2, TX, 128), F32),
+            pltpu.SemaphoreType.DMA((2, 5)),
+            pltpu.VMEM((9, 8, 32), BF),
+            pltpu.VMEM((1, 32), F32),
+            pltpu.VMEM((9, 32, 32), BF),
+            pltpu.VMEM((1, 32), F32),
+            pltpu.VMEM((9, 8, 32), BF),
+            pltpu.VMEM((8, 8, 384), F32),
+            pltpu.SemaphoreType.DMA((5,)),
+        ],
+        in_specs=[pl.BlockSpec(memory_space=pltpu.HBM)] * 10,
         room=60,
+    )(u, v, b, bl, s, w_in, b_in[None, :], w_mid, b_mid[None, :], jnp.swapaxes(w_out, 1, 2))
+    before = shifted(to_up, "lat", 1)
+    after = shifted(to_down, "lat", -1)
+
+    mid, mid_send, summed = call(
+        with_total(middle_sums, total),
+        "middle_sums",
+        [sds((6, TX, TY)), sds((4, TX, TY), BF), TOKEN],
+        5,
+        [pltpu.VMEM((4, TX + 16, TY), F32), pltpu.VMEM((TX + 16, TY), F32)],
+        cost=micros(1),
     )(u, v, b, bl, s)
-    before = shifted(to_up, "lat", 1, False)
-    after = shifted(to_down, "lat", -1, False)
-    vb = [sds((192, 256), BF), sds((576, 256), BF), sds((192, 320), BF), sds((192, 128)), sds((192, 128)), TOKEN]
-    *weights, ready = call(build_weights, "weights", vb, 5, [pltpu.VMEM((8, 8, 384), F32)], in_specs=[VMEM] * 5)(
-        w_in, b_in[None, :], w_mid, b_mid[None, :], w_out
-    )
+    mid_in = shifted(mid_send, "grp", 1)
 
     def rows(n, i, three):
         return [pl.BlockSpec((4, n, TY), lambda _: (0, i, 0))] * three + [pl.BlockSpec((n, TY), lambda _: (i, 0))] * (three - 1)
 
     out = sds((15, 16, LANES), BF)
     hal, down, up = call(
-        pack_lon,
+        with_total(pack_lon, total),
         "pack_lon",
         [sds((FIELDS, TX, 128)), out, out],
-        20,
+        19,
         [pltpu.VMEM((16, LANES), F32)],
         in_specs=[VMEM, VMEM, VMEM] + rows(16, 0, 3) + rows(16, 3, 3) + rows(8, 2, 2) + rows(8, 5, 2),
         grid=(1,),
-    )(ready, before, after, u, v, b, bl, s, u, v, b, bl, s, u, v, bl, u, v, bl)
-    low = shifted(up, "lon", 1, True)
-    high = shifted(down, "lon", -1, True)
-    mid, mid_send = call(
-        with_total(middle_sums, total),
-        "middle_sums",
-        [sds((6, 48, LANES)), sds((6, 48, LANES), BF)],
+    )(summed, before, after, u, v, b, bl, s, u, v, b, bl, s, u, v, bl, u, v, bl)
+    low = shifted(up, "lon", 1)
+    high = shifted(down, "lon", -1)
+    seam = call(
+        with_total(seam_sums, total),
+        "seam_sums",
+        sds((6, TX, 384)),
         5,
-        [
-            pltpu.VMEM((12, TX, LANES), F32),
-            pltpu.VMEM((TX, LANES), F32),
-            pltpu.VMEM((4, TX + 16, LANES), F32),
-            pltpu.VMEM((TX + 16, LANES), F32),
-        ],
-        cost=micros(2),
+        [pltpu.VMEM((13, TX, 384), F32), pltpu.VMEM((4, TX + 16, 384), F32), pltpu.VMEM((TX + 16, 384), F32)],
+        cost=micros(1),
     )(u, v, b, bl, hal)
-    mid_in = lax.ppermute(mid_send, "grp", [(1, 0)])
     inner, ready = call(
         with_total(interior, total),
         "interior",
@@ -574,12 +673,12 @@
     rim, rim_send, two, edge = call(
         with_total(rim_sums, total),
         "rim_sums",
-        [sds((6, 48, LANES)), sds((4, 48, LANES), BF), sds((2, ROWS, LANES)), sds((8, 64, LANES))],
-        9,
+        [sds((6, 48, LANES)), sds((9, 16, LANES), BF), sds((2, ROWS, LANES)), sds((8, 64, LANES))],
+        10,
         [pltpu.VMEM((13, 32, LANES), F32), pltpu.VMEM((4, 48, LANES), F32), pltpu.VMEM((48, LANES), F32)],
         cost=micros(2),
-    )(ready, u, v, b, bl, s, hal, low, high)
-    rim_in = lax.ppermute(rim_send, "grp", [(1, 0)])
+    )(ready, u, v, b, bl, s, hal, low, high, seam)
+    rim_in = shifted(rim_send, "grp", 1)
     force = call(
         with_total(edges, total),
         "edges",
@@ -595,11 +694,11 @@
         with_total(substeps, total),
         "substeps",
         [sds((2, TX, TY)), sds((4, TX, TY), BF)],
-        6,
+        7,
         [tall, tall] + [plane] * 9,
         cost=micros(5),
-    )(two, mid, rim, mid_in, rim_in, force)
-    fin_in = lax.ppermute(fin_send, "grp", [(0, 1)])
+    )(two, mid, seam, rim, mid_in, rim_in, force)
+    fin_in = shifted(fin_send, "grp", 1)
     own = call(
         with_total(own_part, total),
         "own_part",

time: 51.2 us -> 45.3 us (0.88)
  starting transfers between devices: 14 us -> 9.25 us
  local copies, waits for them, and re-layouts: 3.76 us -> 1.85 us
  waiting for transfers between devices: 11.3 us -> 12.3 us
    ppermute x7, starting transfers between devices: 14 us -> 9.25 us  [shifted(): return lax.ppermute(x, axis, [(i, (i + by) % size) for i in range(size)])]
    unnamed x19 -> x22, local copies, waits for them, and re-layouts: 3.76 us -> 1.85 us
    ppermute x7, waiting for transfers between devices: 11.3 us -> 12.3 us  [shifted(): return lax.ppermute(x, axis, [(i, (i + by) % size) for i in range(size)])]
    pallas_call x4, Pallas kernels: 3.78 us -> 4.71 us  [the longest x1 2.8 us: local(): call(pack_lat, 'pack_lat', [half, half] + made, 10, [wide, wide, wide, pl...]
  transfers between devices with their start and end apart: 7 -> 7, of which waited for: 3 -> 3; matrix products, arithmetic and copies ran while one was open for 2% -> 0% of each run, Pallas kernels for 27% -> 29%
where the time goes in v3:
time: 45.3 us; the launch traced here: 45.2 us
  Pallas kernels  20.9 us (46%)
  waiting for transfers between devices  12.3 us (27%)
  starting transfers between devices  9.25 us (20%)
  local copies, waits for them, and re-layouts  1.85 us (4%)
  between operations  0.85 us (2%)
    ppermute x7, waiting for transfers between devices, shifted(): return lax.ppermute(x, axis, [(i, (i + by) % size) for i in range(size)])  12.3 us
    ppermute x7, starting transfers between devices, shifted(): return lax.ppermute(x, axis, [(i, (i + by) % size) for i in range(size)])  9.25 us
    pallas_call x1, Pallas kernels, local(): call(with_total(interior, total), 'interior', [sds((8, FORCED, LANES)), T...  5.25 us
    pallas_call x1, Pallas kernels, local(): call(with_total(edges, total), 'edges', sds((8, FORCED, LANES)), 7, [pltp...  4.31 us
    pallas_call x1, Pallas kernels, local(): call(with_total(substeps, total), 'substeps', [sds((2, TX, TY)), sds((4,...  3.45 us
    pallas_call x1, Pallas kernels, local(): call(pack_lat, 'pack_lat', [half, half] + made, 10, [wide, wide, wide, pl...  2.8 us
    unnamed x22, local copies, waits for them, and re-layouts  1.85 us
    pallas_call x1, Pallas kernels, local(): call(finish, 'finish', [sds((4, TX, TY)), sds((4, TX, TY)), sds((TX, TY))...  1.1 us
  transfers between devices with their start and end apart: 7, of which 3 were waited for; matrix products, arithmetic and copies ran while one was open for 0% of the time, Pallas kernels for 29%

profile of v3, /device:TPU:1, one launch (start us, length us, event | category | flops | bytes accessed | tf_op | source)
XLA Modules:
  0.0 45.2 jit_solution(14823363283519017639)
XLA Ops:
  0.6 0.0 copy-start
  0.6 0.0 copy-start.1
  0.7 2.8 %pack_lat.1 = (bf16[2,64,128]{2,1,0:T(8,128)(2,1)}, bf16[2,64,128]{2,1,0:T(8,128)(2,1)}, bf16[192,256]{1,0:T(8,128)(2,1)}, bf16[576,256]{1,0:T(8,128)(2,1)}, bf1...) custom-call(f32[4,64,512]{2,1,0:T(8,128)} %refs_0_.10, f32[4,64,512]{2,1,0:T(8,128)} %refs_1_.11, ...), custom_call_target="tpu_custom_call" | custom-call | tf_op jit(solution)/shard_map/pack_lat/pallas_call | solution.py:601
  3.5 2.5 %collective-permute-start = (bf16[2,64,128]{2,1,0:T(8,128)(2,1)}, bf16[2,64,128]{2,1,0:T(8,128)(2,1)S(1)}, u32[]{:S(2)}, u32[]{:S(2)}) collective-permute-start(bf16[2,64,128]{2,1,0:T(8,128)(2,1)} %get-tuple-element.25), channel_id=1, source_target_pairs={{0,2},{2,4},{4,6},{6,0},{1,3},{3,5},{5,7},{7,1},{8,10},{10,12},{12... | collective-permute-start | bytes 98312 | tf_op jit(solution)/shard_map/ppermute | solution.py:594
  6.0 2.2 %collective-permute-start.1 = (bf16[2,64,128]{2,1,0:T(8,128)(2,1)}, bf16[2,64,128]{2,1,0:T(8,128)(2,1)S(1)}, u32[]{:S(2)}, u32[]{:S(2)}) collective-permute-start(bf16[2,64,128]{2,1,0:T(8,128)(2,1)} %get-tuple-element.26), channel_id=1, source_target_pairs={{0,6},{2,0},{4,2},{6,4},{1,7},{3,1},{5,3},{7,5},{8,14},{10,8},{12,... | collective-permute-start | bytes 98312 | tf_op jit(solution)/shard_map/ppermute | solution.py:594
  8.2 0.9 %copy-done.3 = s32[64,512]{1,0:T(8,128)S(1)} copy-done((s32[64,512]{1,0:T(8,128)S(1)}, s32[64,512]{1,0:T(8,128)}, u32[]{:S(2)}) %copy-start.3) | copy-done | bytes 131096
  9.1 0.9 %copy-done.5 = f32[64,512]{1,0:T(8,128)S(1)} copy-done((f32[64,512]{1,0:T(8,128)S(1)}, f32[64,512]{1,0:T(8,128)}, u32[]{:S(2)}) %copy-start.5) | copy-done | bytes 131096
  10.0 1.0 %middle_sums.1 = (f32[6,64,512]{2,1,0:T(8,128)S(1)}, bf16[4,64,512]{2,1,0:T(8,128)(2,1)S(1)}, f32[8,128]{1,0:T(8,128)S(1)}) custom-call(f32[4,64,512]{2,1,0:T(8,128)S(1)} %copy-done, f32[4,64,512]{2,1,0:T(8,128)S(1)} %copy-done.1, f32[4,64,512]{2,1,0:T(8,128)S(1)} %copy-done.2, s32[64,512]{1,0:T(8,128)S(1)} %copy-done.3, f32[64,512]{1,0:T(8,128)S(1)} %copy-done.5), custom_call_target="tpu_custom_call" | custom-call | flops 1000000 | bytes 3000000 | tf_op jit(solution)/shard_map/middle_sums/pallas_call | solution.py:627
  11.0 0.0 collective-permute-done.refs_1_
  11.0 0.0 collective-permute-done.1.refs_2_
  11.0 0.3 pack_lon.1
  11.3 0.0 copy-start.6
  11.3 0.0 copy-start.7
  11.3 0.0 copy-start.8
  11.4 3.8 %collective-permute-start.2 = (bf16[15,16,640]{2,1,0:T(8,128)(2,1)S(1)}, bf16[15,16,640]{2,1,0:T(8,128)(2,1)S(1)}, u32[]{:S(2)}, u32[]{:S(2)}) collective-permute-start(bf16[15,16,640]{2,1,0:T(8,128)(2,1)S(1)} %get-tuple-element.34), channel_id=1, source_target_pairs={{0,8},{8,16},{16,24},{24,32},{32,40},{40,48},{48,56},{56,64},{64,7... | collective-permute-start | bytes 921608 | tf_op jit(solution)/shard_map/ppermute | solution.py:594
  15.2 0.0 collective-permute-start.3
  15.2 0.4 collective-permute-start.4
  15.6 0.7 %seam_sums.1.refs_9_.refs_2_ = f32[6,64,384]{2,1,0:T(8,128)S(1)} custom-call(f32[4,64,512]{2,1,0:T(8,128)S(1)} %copy-done, f32[4,64,512]{2,1,0:T(8,128)S(1)} %copy-done.1, f32[4,64,512]{2,1,0:T(8,128)S(1)} %copy-done.2, s32[64,512]{1,0:T(8,128)S(1)} %copy-done.3, f32[14,64,128]{2,1,0:T(8,128)S(1)} %get-tuple-element.27.refs_3_.refs_4_.refs_6_), custom_call_target="tpu_custom_call" | custom-call | flops 1000000 | bytes 3000000 | tf_op jit(solution)/shard_map/seam_sums/pallas_call | solution.py:652
  16.3 5.3 %interior.1 = (f32[8,104,640]{2,1,0:T(8,128)S(1)}, f32[8,128]{1,0:T(8,128)S(1)}) custom-call(f32[4,64,512]{2,1,0:T(8,128)S(1)} %copy-done, f32[4,64,512]{2,1,0:T(8,128)S(1)} %copy-done.1, s32[64,512]{1,0:T(8,128)S(1)} %copy-done.3, f32[14,64,128]{2,1,0:T(8,128)S(1)} %get-tuple-element.27.refs_3_.refs_4_.refs_6_, bf16[192,256]{1,0:T(8,128)(2,1)S(1)} %copy-done.8, ...), custom_call_target="tpu_custom_call" | custom-call | flops 7000000 | bytes 21000000 | tf_op jit(solution)/shard_map/interior/pallas_call | solution.py:660
  21.6 1.4 %collective-permute-done.2.refs_7_.refs_5_ = bf16[15,16,640]{2,1,0:T(8,128)(2,1)S(1)} collective-permute-done((bf16[15,16,640]{2,1,0:T(8,128)(2,1)S(1)}, bf16[15,16,640]{2,1,0:T(8,128)(2,1)S(1)}, u32[]{:S(2)}, u32[]{:S(2)}) %collective-permute-start.2) | collective-permute-done | bytes 307232 | tf_op jit(solution)/shard_map/ppermute | solution.py:594
  22.9 4.7 %collective-permute-done.3.refs_8_.refs_6_ = bf16[15,16,640]{2,1,0:T(8,128)(2,1)S(1)} collective-permute-done((bf16[15,16,640]{2,1,0:T(8,128)(2,1)S(1)}, bf16[15,16,640]{2,1,0:T(8,128)(2,1)S(1)}, u32[]{:S(2)}, u32[]{:S(2)}) %collective-permute-start.3) | collective-permute-done | bytes 307232 | tf_op jit(solution)/shard_map/ppermute | solution.py:594
  27.7 1.1 %rim_sums.1 = (f32[6,48,640]{2,1,0:T(8,128)S(1)}, bf16[9,16,640]{2,1,0:T(8,128)(2,1)S(1)}, f32[2,96,640]{2,1,0:T(8,128)S(1)}, f32[8,64,640]{2,1,0:T(8,128)S(1)}) custom-call(f32[8,128]{1,0:T(8,128)S(1)} %get-tuple-element.33.refs_0_, f32[4,64,512]{2,1,0:T(8,128)S(1)} %copy-done, f32[4,64,512]{2,1,0:T(8,128)S(1)} %copy-done.1, f32[4,64,512]{2,1,0:T(8,128)S(1)} %copy-done.2, ...), custom_call_target="tpu_custom_call" | custom-call | flops 2000000 | bytes 6000000 | tf_op jit(solution)/shard_map/rim_sums/pallas_call | solution.py:673
  28.8 0.2 collective-permute-start.5
  29.0 4.3 %edges.1.refs_6_.refs_7_ = f32[8,104,640]{2,1,0:T(8,128)S(1)} custom-call(f32[8,64,640]{2,1,0:T(8,128)S(1)} %get-tuple-element.41.refs_0_, bf16[192,256]{1,0:T(8,128)(2,1)S(1)} %copy-done.8, bf16[576,256]{1,0:T(8,128)(2,1)S(1)} %copy-done.6, bf16[192,320]{1,0:T(8,128)(2,1)S(1)} %copy-done.7, ...), custom_call_target="tpu_custom_call", output_to_operand_aliasing={{}: (6, {})} | custom-call | flops 6000000 | bytes 18000000 | tf_op jit(solution)/shard_map/edges/pallas_call | solution.py:682
  33.3 0.0 collective-permute-done.4.refs_4_
  33.3 0.0 collective-permute-done.5.refs_5_
  33.3 3.5 %substeps.1 = (f32[2,64,512]{2,1,0:T(8,128)S(1)}, bf16[4,64,512]{2,1,0:T(8,128)(2,1)S(1)}) custom-call(f32[2,96,640]{2,1,0:T(8,128)S(1)} %get-tuple-element.36.refs_0_, f32[6,64,512]{2,1,0:T(8,128)S(1)} %get-tuple-element.37.refs_1_, f32[6,64,384]{2,1,0:T(8,128)S(1)} %seam_sums.1.refs_9_.refs_2_, f32[6,48,640]{2,1,0:T(8,128)S(1)} %get-tuple-element.38.refs_3_, ...), custom_call_target="tpu_custom_call" | custom-call | flops 5000000 | bytes 15000000 | tf_op jit(solution)/shard_map/substeps/pallas_call | solution.py:693
  36.8 0.1 collective-permute-start.6
  36.9 0.0 copy-done.4
  36.9 1.0 %own_part.1.refs_4_ = f32[8,64,512]{2,1,0:T(8,128)S(1)} custom-call(f32[4,64,512]{2,1,0:T(8,128)S(1)} %copy-done, f32[4,64,512]{2,1,0:T(8,128)S(1)} %copy-done.1, f32[4,64,512]{2,1,0:T(8,128)S(1)} %copy-done.2, s32[64,512]{1,0:T(8,128)S(1)} %copy-done.4, f32[14,64,128]{2,1,0:T(8,128)S(1)} %get-tuple-element.27.refs_3_.refs_4_.refs_6_, ...), custom_call_target="tpu_custom_call" | custom-call | flops 2000000 | bytes 6000000 | tf_op jit(solution)/shard_map/own_part/pallas_call | solution.py:702
  37.9 6.1 %collective-permute-done.6.refs_3_ = bf16[4,64,512]{2,1,0:T(8,128)(2,1)S(1)} collective-permute-done((bf16[4,64,512]{2,1,0:T(8,128)(2,1)S(1)}, bf16[4,64,512]{2,1,0:T(8,128)(2,1)S(1)}, u32[]{:S(2)}, u32[]{:S(2)}) %collective-permute-start.6) | collective-permute-done | bytes 262176 | tf_op jit(solution)/shard_map/ppermute | solution.py:594
  44.1 1.1 %finish.1 = (f32[4,64,512]{2,1,0:T(8,128)}, f32[4,64,512]{2,1,0:T(8,128)}, f32[64,512]{1,0:T(8,128)}) custom-call(s32[64,512]{1,0:T(8,128)S(1)} %copy-done.4, f32[2,64,512]{2,1,0:T(8,128)S(1)} %get-tuple-element.43.refs_1_, bf16[4,64,512]{2,1,0:T(8,128)(2,1)S(1)} %get-tuple-element.44.refs_2_, bf16[4,64,512]{2,1,0:T(8,128)(2,1)S(1)} %collective-permute-done.6.refs_3_, ...), custom_call_target="tpu_custom_call" | custom-call | flops 2000000 | bytes 6000000 | tf_op jit(solution)/shard_map/finish/pallas_call | solution.py:711
  (14 shorter events, 0.0 us)
Async XLA Ops:
  0.6 7.6 %copy-start = (f32[4,64,512]{2,1,0:T(8,128)S(1)}, f32[4,64,512]{2,1,0:T(8,128)}, u32[]{:S(2)}) copy-start(f32[4,64,512]{2,1,0:T(8,128)} %refs_0_.10) | copy-start | bytes 1572868
  0.6 7.6 %copy-start.1 = (f32[4,64,512]{2,1,0:T(8,128)S(1)}, f32[4,64,512]{2,1,0:T(8,128)}, u32[]{:S(2)}) copy-start(f32[4,64,512]{2,1,0:T(8,128)} %refs_1_.11) | copy-start | bytes 1572868
  0.7 7.6 %copy-start.2 = (f32[4,64,512]{2,1,0:T(8,128)S(1)}, f32[4,64,512]{2,1,0:T(8,128)}, u32[]{:S(2)}) copy-start(f32[4,64,512]{2,1,0:T(8,128)} %refs_2_.11) | copy-start | bytes 1572868
  3.5 7.5 %collective-permute-start = (bf16[2,64,128]{2,1,0:T(8,128)(2,1)}, bf16[2,64,128]{2,1,0:T(8,128)(2,1)S(1)}, u32[]{:S(2)}, u32[]{:S(2)}) collective-permute-start(bf16[2,64,128]{2,1,0:T(8,128)(2,1)} %get-tuple-element.25), channel_id=1, source_target_pairs={{0,2},{2,4},{4,6},{6,0},{1,3},{3,5},{5,7},{7,1},{8,10},{10,12},{12... | collective-permute-start | bytes 98312 | tf_op jit(solution)/shard_map/ppermute | solution.py:594
  6.0 5.0 %collective-permute-start.1 = (bf16[2,64,128]{2,1,0:T(8,128)(2,1)}, bf16[2,64,128]{2,1,0:T(8,128)(2,1)S(1)}, u32[]{:S(2)}, u32[]{:S(2)}) collective-permute-start(bf16[2,64,128]{2,1,0:T(8,128)(2,1)} %get-tuple-element.26), channel_id=1, source_target_pairs={{0,6},{2,0},{4,2},{6,4},{1,7},{3,1},{5,3},{7,5},{8,14},{10,8},{12,... | collective-permute-start | bytes 98312 | tf_op jit(solution)/shard_map/ppermute | solution.py:594
  8.2 0.9 %copy-start.3 = (s32[64,512]{1,0:T(8,128)S(1)}, s32[64,512]{1,0:T(8,128)}, u32[]{:S(2)}) copy-start(s32[64,512]{1,0:T(8,128)} %refs_0_.11) | copy-start | bytes 393220
  9.1 0.9 %copy-start.5 = (f32[64,512]{1,0:T(8,128)S(1)}, f32[64,512]{1,0:T(8,128)}, u32[]{:S(2)}) copy-start(f32[64,512]{1,0:T(8,128)} %refs_5_.5) | copy-start | bytes 393220
  11.3 5.0 %copy-start.6 = (bf16[576,256]{1,0:T(8,128)(2,1)S(1)}, bf16[576,256]{1,0:T(8,128)(2,1)}, u32[]{:S(2)}) copy-start(bf16[576,256]{1,0:T(8,128)(2,1)} %get-tuple-element.29.refs_5_.refs_2_) | copy-start | bytes 884740
  11.3 5.0 %copy-start.7 = (bf16[192,320]{1,0:T(8,128)(2,1)S(1)}, bf16[192,320]{1,0:T(8,128)(2,1)}, u32[]{:S(2)}) copy-start(bf16[192,320]{1,0:T(8,128)(2,1)} %get-tuple-element.30.refs_6_.refs_3_) | copy-start | bytes 368644
  11.3 5.0 %copy-start.8 = (bf16[192,256]{1,0:T(8,128)(2,1)S(1)}, bf16[192,256]{1,0:T(8,128)(2,1)}, u32[]{:S(2)}) copy-start(bf16[192,256]{1,0:T(8,128)(2,1)} %get-tuple-element.28.refs_4_.refs_1_) | copy-start | bytes 294916
  11.3 4.9 %copy-start.9 = (f32[192,128]{1,0:T(8,128)S(1)}, f32[192,128]{1,0:T(8,128)}, u32[]{:S(2)}) copy-start(f32[192,128]{1,0:T(8,128)} %get-tuple-element.31.refs_7_.refs_4_) | copy-start | bytes 294916
  11.3 4.9 %copy-start.10 = (f32[192,128]{1,0:T(8,128)S(1)}, f32[192,128]{1,0:T(8,128)}, u32[]{:S(2)}) copy-start(f32[192,128]{1,0:T(8,128)} %get-tuple-element.32.refs_8_.refs_5_) | copy-start | bytes 294916
  11.4 11.6 %collective-permute-start.2 = (bf16[15,16,640]{2,1,0:T(8,128)(2,1)S(1)}, bf16[15,16,640]{2,1,0:T(8,128)(2,1)S(1)}, u32[]{:S(2)}, u32[]{:S(2)}) collective-permute-start(bf16[15,16,640]{2,1,0:T(8,128)(2,1)S(1)} %get-tuple-element.34), channel_id=1, source_target_pairs={{0,8},{8,16},{16,24},{24,32},{32,40},{40,48},{48,56},{56,64},{64,7... | collective-permute-start | bytes 921608 | tf_op jit(solution)/shard_map/ppermute | solution.py:594
  15.2 12.5 %collective-permute-start.3 = (bf16[15,16,640]{2,1,0:T(8,128)(2,1)S(1)}, bf16[15,16,640]{2,1,0:T(8,128)(2,1)S(1)}, u32[]{:S(2)}, u32[]{:S(2)}) collective-permute-start(bf16[15,16,640]{2,1,0:T(8,128)(2,1)S(1)} %get-tuple-element.35), channel_id=1, source_target_pairs={{0,120},{8,0},{16,8},{24,16},{32,24},{40,32},{48,40},{56,48},{64,5... | collective-permute-start | bytes 921608 | tf_op jit(solution)/shard_map/ppermute | solution.py:594
  15.2 18.1 %collective-permute-start.4 = (bf16[4,64,512]{2,1,0:T(8,128)(2,1)S(1)}, bf16[4,64,512]{2,1,0:T(8,128)(2,1)S(1)}, u32[]{:S(2)}, u32[]{:S(2)}) collective-permute-start(bf16[4,64,512]{2,1,0:T(8,128)(2,1)S(1)} %get-tuple-element.39), channel_id=1, source_target_pairs={{0,1},{1,0},{2,3},{3,2},{4,5},{5,4},{6,7},{7,6},{8,9},{9,8},{10,11... | collective-permute-start | bytes 786440 | tf_op jit(solution)/shard_map/ppermute | solution.py:594
  28.8 4.5 %collective-permute-start.5 = (bf16[9,16,640]{2,1,0:T(8,128)(2,1)S(1)}, bf16[9,16,640]{2,1,0:T(8,128)(2,1)S(1)}, u32[]{:S(2)}, u32[]{:S(2)}) collective-permute-start(bf16[9,16,640]{2,1,0:T(8,128)(2,1)S(1)} %get-tuple-element.40), channel_id=1, source_target_pairs={{0,1},{1,0},{2,3},{3,2},{4,5},{5,4},{6,7},{7,6},{8,9},{9,8},{10,11... | collective-permute-start | bytes 552968 | tf_op jit(solution)/shard_map/ppermute | solution.py:594
  33.3 3.6 %copy-start.4 = (s32[64,512]{1,0:T(8,128)S(1)}, s32[64,512]{1,0:T(8,128)}, u32[]{:S(2)}) copy-start(s32[64,512]{1,0:T(8,128)} %refs_0_.11) | copy-start | bytes 393220
  36.8 7.3 %collective-permute-start.6 = (bf16[4,64,512]{2,1,0:T(8,128)(2,1)S(1)}, bf16[4,64,512]{2,1,0:T(8,128)(2,1)S(1)}, u32[]{:S(2)}, u32[]{:S(2)}) collective-permute-start(bf16[4,64,512]{2,1,0:T(8,128)(2,1)S(1)} %get-tuple-element.44.refs_2_), channel_id=1, source_target_pairs={{0,1},{1,0},{2,3},{3,2},{4,5},{5,4},{6,7},{7,6},{8,9},{9,8},{10,11... | collective-permute-start | bytes 786440 | tf_op jit(solution)/shard_map/ppermute | solution.py:594

commit v4 on v3

--- a/solution.py
+++ b/solution.py
@@ -90,7 +90,11 @@
     build_weights(*held, *made, spread)
 
 
-def pack_lon(total, sc, summed, before, after, *refs):
+def bring(sc, bl, s, done):
+    done[...] = bl[0:8, 0:128].astype(F32) + s[0:8, 0:128]
+
+
+def pack_lon(total, sc, near, before, after, *refs):
     tops, bots, extra_t, extra_b = refs[0:5], refs[5:10], refs[10:13], refs[13:16]
     hal, to_down, to_up, work = refs[16:]
     base = 4 * sc[0]
@@ -210,7 +214,7 @@
         closure(in0, act1, act2, (w1, w2, w3, b1, b2), inside_of(sc[1], total, (1, LANES)), [(0, 0, 0, 10, 10, 7)], store)
 
 
-def edges(total, sc, edge, w1, w2, w3, b1, b2, inner, out, in0, act1, act2):
+def edges(total, sc, edge, two, w1, w2, w3, b1, b2, inner, out, send, in0, act1, act2):
     @pl.when(sc[0] == 0)
     def _():
         for at, start in ((0, 6), (26, 33)):
@@ -225,6 +229,19 @@
 
         parts = [(0, 0, 5, 4, 4, 3), (26, 29, 0, 4, 4, 3)]
         closure(in0, act1, act2, (w1, w2, w3, b1, b2), inside_of(sc[1], total, (1, LANES)), parts, store)
+        for i in range(0, 48, 16):
+            halves = []
+            for p in (i, i + 8):
+                r = p if p < RIM else p + 48
+                level = two[0, r : r + 8, :]
+                rows = slice(r + 4, r + 12)
+                halves.append(forced(sc, level, out, rows, [slice(0, LANES)], ~inner_rows(r - HALO, level.shape)))
+            for n in range(2):
+                send[n, i : i + 16, :] = jnp.concatenate([halves[0][n], halves[1][n]], 0).astype(BF)
+
+    @pl.when(sc[0] != 0)
+    def _():
+        send[...] = jnp.zeros_like(send)
 
 
 def pressures(base, b_rows, pr, load, rows):
@@ -287,7 +304,25 @@
         ref[end - 8 : end, :] = jnp.zeros((8, ref.shape[1]), F32)
 
 
-def middle_sums(total, sc, u, v, b, bl, s, sums, send, done, pr, load):
+def forced(sc, level, force, rows, pieces, keep):
+    te = jnp.zeros(level.shape, F32)
+    tn = te
+    for k in range(4):
+        weight = jnp.where(level > float(k), 1.0 + 0.25 * k, 0.0)
+        fe = [force[k, rows, at] for at in pieces]
+        fn = [force[4 + k, rows, at] for at in pieces]
+        te = te + weight * (fe[0] if len(fe) == 1 else jnp.concatenate(fe, 1))
+        tn = tn + weight * (fn[0] if len(fn) == 1 else jnp.concatenate(fn, 1))
+    keep = keep & (jnp.zeros(level.shape, jnp.int32) + sc[0] == 0)
+    return jnp.where(keep, te, 0.0), jnp.where(keep, tn, 0.0)
+
+
+def inner_rows(r, shape):
+    x = r + lax.broadcasted_iota(jnp.int32, shape, 0)
+    return (x >= 4) & (x < 60)
+
+
+def middle_sums(total, sc, first, u, v, b, bl, s, force, sums, send, done, pr, load):
     done[...] = jnp.zeros_like(done)
     base = 4 * sc[0]
 
@@ -309,15 +344,18 @@
             found = sums_of(
                 sc, coriolis, level, lambda k: u[k, rr, :] * wet(k, rr), lambda k: v[k, rr, :] * wet(k, rr), pr, load, r, open_grads
             )
+            extra = forced(sc, level, force, slice(r + 20, r + 28), [slice(0, TY)], inner_rows(r, level.shape))
+            found = (found[0] + extra[0], found[1] + extra[1]) + found[2:]
             for i, a in enumerate(found):
                 sums[i, rr, :] = a
             halves.append(found)
         for i in range(4):
             a = jnp.concatenate([halves[0][i], halves[1][i]], 0)
             send[i, q : q + 16, :] = a.astype(BF)
-
-
-def seam_sums(total, sc, u, v, b, bl, hal, sums, ext, pr, load):
+        send[4, q : q + 16, :] = load[q + 8 : q + 24, :].astype(BF)
+
+
+def seam_sums(total, sc, u, v, b, bl, hal, force, sums, ext, pr, load):
     base = 4 * sc[0]
     last, first = slice(TY - 128, TY), slice(0, 128)
 
@@ -339,6 +377,9 @@
     for r in range(0, TX, 8):
         rr = slice(r, r + 8)
         found = sums_of(sc, coriolis, ext[12, rr, :], lambda k: ext[k, rr, :], lambda k: ext[4 + k, rr, :], pr, load, r)
+        pieces = [last, slice(TY, LANES), first]
+        extra = forced(sc, ext[12, rr, :], force, slice(r + 20, r + 28), pieces, inner_rows(r, (8, 384)))
+        found = (found[0] + extra[0], found[1] + extra[1]) + found[2:] + (load[r + 8 : r + 16, :],)
         for i, a in enumerate(found):
             sums[i, rr, :] = a
 
@@ -346,6 +387,7 @@
 def rim_sums(total, sc, ready, u, v, b, bl, s, hal, low, high, seam, sums, send, two, edge, ext, pr, load):
     base = 4 * sc[0]
     tall = 32
+    loads = []
     for side, halo in ((0, low), (1, high)):
         own = slice(0, 16) if side == 0 else slice(TX - 16, TX)
         hr, orr = (slice(0, 16), slice(16, 32)) if side == 0 else (slice(16, 32), slice(0, 16))
@@ -364,6 +406,7 @@
                 ref[0:8, :] = jnp.zeros((8, LANES), F32)
             else:
                 ref[40:48, :] = jnp.zeros((8, LANES), F32)
+        loads.append(load[23:24, :] if side == 0 else load[24:25, :])
         coriolis = coriolis_of(sc[1], total, (8, LANES))
         for j in range(3):
             r = 8 * j + 8 * side
@@ -401,13 +444,17 @@
                 packed = jnp.where((lane >= base + 16) & (lane < base + 32), pltpu.roll(outer, base + 32, 1), packed)
                 packed = jnp.where(lane == base + 32, pltpu.roll(before, base + 33, 1), packed)
                 packed = jnp.where(lane == base + 33, pltpu.roll(after, base + 33, 1), packed)
+                if i == 0:
+                    load_at = seam[6, own, 128:256]
+                    packed = jnp.where(lane == 84 + 2 * turn, pltpu.roll(load_at, 84 + 2 * turn, 1), packed)
+                    packed = jnp.where(lane == 85 + 2 * turn, pltpu.roll(load_at, 86 + 2 * turn, 1), packed)
             send[2 * i + side, :, :TY] = sums[i, at, :TY].astype(BF)
             send[2 * i + side, :, TY:] = packed.astype(BF)
     ends = [sums[i, row : row + 1, :] for i in range(4) for row in (16, 31)]
-    send[8] = jnp.concatenate(ends + [jnp.zeros((8, LANES), F32)], 0).astype(BF)
-
-
-def own_part(total, sc, u, v, b, bl, hal, low, high, force, out, pr, load):
+    send[8] = jnp.concatenate(ends + loads + [jnp.zeros((6, LANES), F32)], 0).astype(BF)
+
+
+def own_part(total, sc, u, v, b, bl, hal, low, high, force, mid_in, rim_in, out, pr, load):
     base = 4 * sc[0]
     upper = jnp.where(sc[0] == 0, step_dt, 0.0)
 
@@ -421,6 +468,20 @@
         return jnp.concatenate([b[k, at, :] * wet, hal[8 + k, at, :]], 1)
 
     pressures(base, b_rows, pr, load, TX + 16)
+    lane = lax.broadcasted_iota(jnp.int32, (16, 128), 1)
+    for x in range(0, TX, 16):
+        turn = x // 32
+        beyond = rim_in[x // 16 % 2, :, TY:].astype(F32)
+        outer = jnp.where(lane < 64, pltpu.roll(beyond, 44 - 2 * turn, 1), pltpu.roll(beyond, 42 - 2 * turn, 1))
+        above = jnp.concatenate([mid_in[4, x : x + 16, :].astype(F32), outer], 1)
+        above = jnp.where(upper > 0.0, 0.0, above)
+        for k in range(4):
+            pr[k, x + 16 : x + 32, :] = pr[k, x + 16 : x + 32, :] + above
+    ends = rim_in[8].astype(F32)
+    for at, row in ((8, 15), (9, TX + 16)):
+        above = jnp.where(upper > 0.0, 0.0, ends[at : at + 1, :])
+        for k in range(4):
+            pr[k, row : row + 1, :] = pr[k, row : row + 1, :] + above
     coriolis = coriolis_of(sc[1], total, (8, LANES))[:, :TY]
     for r in range(0, TX, 8):
         rr = slice(r, r + 8)
@@ -440,125 +501,100 @@
             out[4 + k, rr, :] = wet * (north + step_dt * (tn + fn))
 
 
-def substeps(total, sc, two, mid, seam, rim, mid_in, rim_in, force, fin, send, lv, fx, fy, eb, nb, ae, an, es, ns, rel, c2):
-    @pl.when(sc[0] == 0)
-    def _():
-        zero8 = jnp.zeros((8, LANES), F32)
-        lane = lax.broadcasted_iota(jnp.int32, (8, 128), 1)
-
-        def ended(i, at, outer):
-            first = jnp.where(lane == 0, seam[i, at, 256:384], mid[i, at, 0:128])
-            last = jnp.where(lane == 127, seam[i, at, 0:128], mid[i, at, TY - 128 :])
-            pieces = [first, mid[i, at, 128 : TY - 128], last]
-            return jnp.concatenate(pieces + [seam[i, at, 128:256]] if outer else pieces, 1)
-
-        for ref in (lv, fx):
-            ref[0:8, :] = zero8
-            ref[ROWS + 8 : ROWS + 16, :] = zero8
-        for r in range(0, ROWS, 8):
+def substeps(total, sc, two, mid, seam, rim, mid_in, rim_in, force, force_in, own, east_out, north_out, surface_out, lv, fx, fy, eb, nb, ae, an, es, ns, rel, c2):
+    zero8 = jnp.zeros((8, LANES), F32)
+    lower = jnp.zeros((8, LANES), jnp.int32) + sc[0] > 0
+    lane = lax.broadcasted_iota(jnp.int32, (8, 128), 1)
+
+    def ended(i, at, outer):
+        first = jnp.where(lane == 0, seam[i, at, 256:384], mid[i, at, 0:128])
+        last = jnp.where(lane == 127, seam[i, at, 0:128], mid[i, at, TY - 128 :])
+        pieces = [first, mid[i, at, 128 : TY - 128], last]
+        return jnp.concatenate(pieces + [seam[i, at, 128:256]] if outer else pieces, 1)
+
+    for ref in (lv, fx):
+        ref[0:8, :] = zero8
+        ref[ROWS + 8 : ROWS + 16, :] = zero8
+    for r in range(0, ROWS, 8):
+        rr = slice(r, r + 8)
+        level = two[0, rr, :]
+        depth = level + 0.125 * level * (level - 1.0)
+        over = 1.0 / jnp.maximum(depth, 1.0)
+        rel[rr, :] = depth * (1.0 / TOTAL_DEPTH)
+        c2[rr, :] = jnp.where(level > 0.0, 0.5 * sub_dt * gravity, 0.0)
+        middle = RIM <= r < ROWS - RIM
+        at = r - RIM if middle else (r if r < RIM else r - 48)
+        at = slice(at, at + 8)
+        x = r - HALO
+        found = []
+        for i in range(4):
+            here = ended(i, slice(x, x + 8), True) if middle else rim[i, at, :]
+            if not 0 <= x < TX:
+                row = r % 16
+                found.append(here + rim_in[2 * i + (x > 0), :, :].astype(F32)[row : row + 8])
+                continue
+            turn, half = x // 32, x % 16
+            base = 16 + 34 * turn
+            beyond = rim_in[2 * i + x // 16 % 2, :, TY:].astype(F32)[half : half + 8]
+            theirs = mid_in[i, x - half : x - half + 16, :].astype(F32)[half : half + 8]
+            outer = jnp.where(lane < 16, pltpu.roll(beyond, 128 - base, 1), pltpu.roll(beyond, 96 - base, 1))
+            first = jnp.where(lane == 0, pltpu.roll(beyond, 95 - base, 1), theirs[:, 0:128])
+            last = jnp.where(lane == 127, pltpu.roll(beyond, 95 - base, 1), theirs[:, TY - 128 :])
+            theirs = jnp.concatenate([first, theirs[:, 128 : TY - 128], last, outer], 1)
+            if x in (0, TX - 8):
+                end = rim_in[8].astype(F32)[2 * i + (x > 0) : 2 * i + (x > 0) + 1]
+                row = lax.broadcasted_iota(jnp.int32, (8, LANES), 0)
+                theirs = jnp.where(row == (0 if x == 0 else 7), end, theirs)
+            found.append(here + theirs)
+        if not middle:
+            everywhere = level == level
+            mine = forced(sc, level, force, slice(r + 4, r + 12), [slice(0, LANES)], everywhere)
+            pair, half = at.start // 16 * 16, at.start % 16
+            for n in range(2):
+                theirs = force_in[n, pair : pair + 16, :].astype(F32)[half : half + 8]
+                found[n] = found[n] + jnp.where(lower, theirs, mine[n])
+        ae[rr, :] = sub_dt * found[0] * over
+        an[rr, :] = sub_dt * found[1] * over
+        e, n = found[2] * over, found[3] * over
+        es[rr, :], ns[rr, :] = e, n
+        eb[rr, :], nb[rr, :] = e, n
+        lv[r + 8 : r + 16, :] = two[1, rr, :]
+    inside = inside_of(sc[1], total, (8, LANES))
+
+    def step(first, carry):
+        for r in range(first, ROWS - first, 8):
             rr = slice(r, r + 8)
-            level = two[0, rr, :]
-            depth = level + 0.125 * level * (level - 1.0)
-            over = 1.0 / jnp.maximum(depth, 1.0)
-            rel[rr, :] = depth * (1.0 / TOTAL_DEPTH)
-            c2[rr, :] = jnp.where(level > 0.0, 0.5 * sub_dt * gravity, 0.0)
-            middle = RIM <= r < ROWS - RIM
-            at = r - RIM if middle else (r if r < RIM else r - 48)
-            at = slice(at, at + 8)
-            x = r - HALO
-            found = []
-            for i in range(4):
-                own = ended(i, slice(x, x + 8), True) if middle else rim[i, at, :]
-                if not 0 <= x < TX:
-                    row = r % 16
-                    found.append(own + rim_in[2 * i + (x > 0), :, :].astype(F32)[row : row + 8])
-                    continue
-                turn, half = x // 32, x % 16
-                base = 16 + 34 * turn
-                beyond = rim_in[2 * i + x // 16 % 2, :, TY:].astype(F32)[half : half + 8]
-                theirs = mid_in[i, x - half : x - half + 16, :].astype(F32)[half : half + 8]
-                outer = jnp.where(lane < 16, pltpu.roll(beyond, 128 - base, 1), pltpu.roll(beyond, 96 - base, 1))
-                first = jnp.where(lane == 0, pltpu.roll(beyond, 95 - base, 1), theirs[:, 0:128])
-                last = jnp.where(lane == 127, pltpu.roll(beyond, 95 - base, 1), theirs[:, TY - 128 :])
-                theirs = jnp.concatenate([first, theirs[:, 128 : TY - 128], last, outer], 1)
-                if x in (0, TX - 8):
-                    end = rim_in[8].astype(F32)[2 * i + (x > 0) : 2 * i + (x > 0) + 1]
-                    row = lax.broadcasted_iota(jnp.int32, (8, LANES), 0)
-                    theirs = jnp.where(row == (0 if x == 0 else 7), end, theirs)
-                found.append(own + theirs)
-            for k in range(4):
-                weight = jnp.where(level > float(k), 1.0 + 0.25 * k, 0.0)
-                found[0] = found[0] + weight * force[k, r + 4 : r + 12, :]
-                found[1] = found[1] + weight * force[4 + k, r + 4 : r + 12, :]
-            ae[rr, :] = sub_dt * found[0] * over
-            an[rr, :] = sub_dt * found[1] * over
-            e, n = found[2] * over, found[3] * over
-            es[rr, :], ns[rr, :] = e, n
-            eb[rr, :], nb[rr, :] = e, n
-            lv[r + 8 : r + 16, :] = two[1, rr, :]
-        inside = inside_of(sc[1], total, (8, LANES))
-
-        def step(first, carry):
-            for r in range(first, ROWS - first, 8):
-                rr = slice(r, r + 8)
-                here = lv[r + 8 : r + 16, :]
-                dx = lv[r + 9 : r + 17, :] - lv[r + 7 : r + 15, :]
-                dy = pltpu.roll(here, LANES - 1, 1) - pltpu.roll(here, 1, 1)
-                c = c2[rr, :]
-                e = eb[rr, :] + (ae[rr, :] - c * dx)
-                n = nb[rr, :] + (an[rr, :] - c * dy)
-                eb[rr, :] = e
-                nb[rr, :] = n
-                fx[r + 8 : r + 16, :] = rel[rr, :] * e
-                fy[rr, :] = rel[rr, :] * n
-            for r in range(first, ROWS - first, 8):
-                rr = slice(r, r + 8)
-                dx = fx[r + 9 : r + 17, :] - fx[r + 7 : r + 15, :]
-                f = fy[rr, :]
-                dy = pltpu.roll(f, LANES - 1, 1) - pltpu.roll(f, 1, 1)
-                lv[r + 8 : r + 16, :] = inside * (lv[r + 8 : r + 16, :] - (0.5 * sub_dt) * (dx + dy))
-            return carry
-
-        lax.fori_loop(0, NSUB // 2, lambda _, carry: step(0, carry), 0)
-        lax.fori_loop(0, NSUB // 2, lambda _, carry: step(8, carry), 0)
-        for q in range(0, TX, 16):
-            r = q + HALO
-            rr, at = slice(r, r + 16), slice(q, q + 16)
-            fe = eb[rr, :TY] - es[rr, :TY] - (step_dt / sub_dt) * ae[rr, :TY]
-            fn = nb[rr, :TY] - ns[rr, :TY] - (step_dt / sub_dt) * an[rr, :TY]
-            fin[0, at, :], fin[1, at, :] = fe, fn
-            slopes = []
-            for i in (4, 5):
-                pieces = []
-                for p in (r, r + 8):
-                    if RIM <= p < ROWS - RIM:
-                        pieces.append(ended(i, slice(p - HALO, p - HALO + 8), False))
-                    else:
-                        p = p if p < RIM else p - 48
-                        pieces.append(rim[i, p : p + 8, :TY])
-                slopes.append(jnp.concatenate(pieces, 0))
-            send[0, at, :] = (fe - (step_dt * press_coef) * slopes[0]).astype(BF)
-            send[1, at, :] = (fn - (step_dt * press_coef) * slopes[1]).astype(BF)
-            level = lv[r + 8 : r + 24, :TY]
-            high = level.astype(BF)
-            send[2, at, :] = high
-            send[3, at, :] = (level - high.astype(F32)).astype(BF)
-
-
-def finish(sc, bl, fin, mine, theirs, own, east_out, north_out, surface_out):
+            here = lv[r + 8 : r + 16, :]
+            dx = lv[r + 9 : r + 17, :] - lv[r + 7 : r + 15, :]
+            dy = pltpu.roll(here, LANES - 1, 1) - pltpu.roll(here, 1, 1)
+            c = c2[rr, :]
+            e = eb[rr, :] + (ae[rr, :] - c * dx)
+            n = nb[rr, :] + (an[rr, :] - c * dy)
+            eb[rr, :] = e
+            nb[rr, :] = n
+            fx[r + 8 : r + 16, :] = rel[rr, :] * e
+            fy[rr, :] = rel[rr, :] * n
+        for r in range(first, ROWS - first, 8):
+            rr = slice(r, r + 8)
+            dx = fx[r + 9 : r + 17, :] - fx[r + 7 : r + 15, :]
+            f = fy[rr, :]
+            dy = pltpu.roll(f, LANES - 1, 1) - pltpu.roll(f, 1, 1)
+            lv[r + 8 : r + 16, :] = inside * (lv[r + 8 : r + 16, :] - (0.5 * sub_dt) * (dx + dy))
+        return carry
+
+    lax.fori_loop(0, NSUB // 2, lambda _, carry: step(0, carry), 0)
+    lax.fori_loop(0, NSUB // 2, lambda _, carry: step(8, carry), 0)
     base = 4 * sc[0]
-    upper = jnp.where(sc[0] == 0, 1.0, 0.0) > 0.0
-    for r in range(0, TX, 16):
-        rr = slice(r, r + 16)
-        level = bl[rr, :].astype(F32)
-        fe = jnp.where(upper, fin[0, rr, :], theirs[0, rr, :].astype(F32))
-        fn = jnp.where(upper, fin[1, rr, :], theirs[1, rr, :].astype(F32))
+    for q in range(0, TX, 8):
+        rr, at = slice(q + HALO, q + HALO + 8), slice(q, q + 8)
+        level = two[0, rr, :TY]
+        fe = eb[rr, :TY] - es[rr, :TY] - (step_dt / sub_dt) * ae[rr, :TY]
+        fn = nb[rr, :TY] - ns[rr, :TY] - (step_dt / sub_dt) * an[rr, :TY]
         for k in range(4):
             wet = wet_of(level, (base + k).astype(F32))
-            east_out[k, rr, :] = own[k, rr, :] + wet * fe
-            north_out[k, rr, :] = own[4 + k, rr, :] + wet * fn
-        parts = [jnp.where(upper, mine[i, rr, :].astype(F32), theirs[i, rr, :].astype(F32)) for i in (2, 3)]
-        surface_out[rr, :] = parts[0] + parts[1]
+            east_out[k, at, :] = own[k, at, :] + wet * fe
+            north_out[k, at, :] = own[4 + k, at, :] + wet * fn
+        surface_out[at, :] = lv[q + HALO + 8 : q + HALO + 16, :TY]
 
 
 def call(kernel, name, out_shape, n_in, scratch=(), in_specs=None, cost=None, grid=(), aliases=None, room=28):
@@ -624,15 +660,7 @@
     before = shifted(to_up, "lat", 1)
     after = shifted(to_down, "lat", -1)
 
-    mid, mid_send, summed = call(
-        with_total(middle_sums, total),
-        "middle_sums",
-        [sds((6, TX, TY)), sds((4, TX, TY), BF), TOKEN],
-        5,
-        [pltpu.VMEM((4, TX + 16, TY), F32), pltpu.VMEM((TX + 16, TY), F32)],
-        cost=micros(1),
-    )(u, v, b, bl, s)
-    mid_in = shifted(mid_send, "grp", 1)
+    near = call(bring, "bring", TOKEN, 2, cost=micros(1))(bl, s)
 
     def rows(n, i, three):
         return [pl.BlockSpec((4, n, TY), lambda _: (0, i, 0))] * three + [pl.BlockSpec((n, TY), lambda _: (i, 0))] * (three - 1)
@@ -646,17 +674,9 @@
         [pltpu.VMEM((16, LANES), F32)],
         in_specs=[VMEM, VMEM, VMEM] + rows(16, 0, 3) + rows(16, 3, 3) + rows(8, 2, 2) + rows(8, 5, 2),
         grid=(1,),
-    )(summed, before, after, u, v, b, bl, s, u, v, b, bl, s, u, v, bl, u, v, bl)
+    )(near, before, after, u, v, b, bl, s, u, v, b, bl, s, u, v, bl, u, v, bl)
     low = shifted(up, "lon", 1)
     high = shifted(down, "lon", -1)
-    seam = call(
-        with_total(seam_sums, total),
-        "seam_sums",
-        sds((6, TX, 384)),
-        5,
-        [pltpu.VMEM((13, TX, 384), F32), pltpu.VMEM((4, TX + 16, 384), F32), pltpu.VMEM((TX + 16, 384), F32)],
-        cost=micros(1),
-    )(u, v, b, bl, hal)
     inner, ready = call(
         with_total(interior, total),
         "interior",
@@ -670,6 +690,23 @@
         ],
         cost=micros(7),
     )(u, v, bl, hal, *weights)
+    mid, mid_send, summed = call(
+        with_total(middle_sums, total),
+        "middle_sums",
+        [sds((6, TX, TY)), sds((5, TX, TY), BF), TOKEN],
+        7,
+        [pltpu.VMEM((4, TX + 16, TY), F32), pltpu.VMEM((TX + 16, TY), F32)],
+        cost=micros(1),
+    )(ready, u, v, b, bl, s, inner)
+    mid_in = shifted(mid_send, "grp", 1)
+    seam = call(
+        with_total(seam_sums, total),
+        "seam_sums",
+        sds((7, TX, 384)),
+        6,
+        [pltpu.VMEM((13, TX, 384), F32), pltpu.VMEM((4, TX + 16, 384), F32), pltpu.VMEM((TX + 16, 384), F32)],
+        cost=micros(1),
+    )(u, v, b, bl, hal, inner)
     rim, rim_send, two, edge = call(
         with_total(rim_sums, total),
         "rim_sums",
@@ -677,40 +714,37 @@
         10,
         [pltpu.VMEM((13, 32, LANES), F32), pltpu.VMEM((4, 48, LANES), F32), pltpu.VMEM((48, LANES), F32)],
         cost=micros(2),
-    )(ready, u, v, b, bl, s, hal, low, high, seam)
+    )(summed, u, v, b, bl, s, hal, low, high, seam)
     rim_in = shifted(rim_send, "grp", 1)
-    force = call(
+    force, force_send = call(
         with_total(edges, total),
         "edges",
-        sds((8, FORCED, LANES)),
-        7,
+        [sds((8, FORCED, LANES)), sds((2, 48, LANES), BF)],
+        8,
         [pltpu.VMEM((52 * 32, LANES), BF), pltpu.VMEM((52 * 32, LANES), BF), pltpu.VMEM((55 * 32, LANES), BF)],
         cost=micros(6),
-        aliases={6: 0},
-    )(edge, *weights, inner)
-    plane = pltpu.VMEM((ROWS, LANES), F32)
-    tall = pltpu.VMEM((ROWS + 16, LANES), F32)
-    fin, fin_send = call(
-        with_total(substeps, total),
-        "substeps",
-        [sds((2, TX, TY)), sds((4, TX, TY), BF)],
-        7,
-        [tall, tall] + [plane] * 9,
-        cost=micros(5),
-    )(two, mid, seam, rim, mid_in, rim_in, force)
-    fin_in = shifted(fin_send, "grp", 1)
+        aliases={7: 0},
+    )(edge, two, *weights, inner)
+    force_in = shifted(force_send, "grp", 1)
     own = call(
         with_total(own_part, total),
         "own_part",
         sds((8, TX, TY)),
-        8,
+        10,
         [pltpu.VMEM((4, 96, LANES), F32), pltpu.VMEM((96, LANES), F32)],
         cost=micros(2),
-    )(u, v, b, bl, hal, low, high, force)
+    )(u, v, b, bl, hal, low, high, force, mid_in, rim_in)
+    plane = pltpu.VMEM((ROWS, LANES), F32)
+    tall = pltpu.VMEM((ROWS + 16, LANES), F32)
     return tuple(
-        call(finish, "finish", [sds((4, TX, TY)), sds((4, TX, TY)), sds((TX, TY))], 5, cost=micros(2))(
-            bl, fin, fin_send, fin_in, own
-        )
+        call(
+            with_total(substeps, total),
+            "substeps",
+            [sds((4, TX, TY)), sds((4, TX, TY)), sds((TX, TY))],
+            9,
+            [tall, tall] + [plane] * 9,
+            cost=micros(5),
+        )(two, mid, seam, rim, mid_in, rim_in, force, force_in, own)
     )
 
 

time: 45.3 us -> 41.8 us (0.923)
  the two profiles are of different devices: /device:TPU:1 before, /device:TPU:0 now
where the time goes in v4:
time: 41.8 us; the launch traced here: 41 us
  Pallas kernels  21.6 us (52%)
  starting transfers between devices  12 us (29%)
  waiting for transfers between devices  4.8 us (11%)
  local copies, waits for them, and re-layouts  1.84 us (4%)
  between operations  0.8 us (2%)
    ppermute x7, starting transfers between devices, shifted(): return lax.ppermute(x, axis, [(i, (i + by) % size) for i in range(size)])  12 us
    pallas_call x1, Pallas kernels, local(): call(with_total(interior, total), 'interior', [sds((8, FORCED, LANES)), T...  5.52 us
    ppermute x7, waiting for transfers between devices, shifted(): return lax.ppermute(x, axis, [(i, (i + by) % size) for i in range(size)])  4.8 us
    pallas_call x1, Pallas kernels, local(): call(with_total(edges, total), 'edges', [sds((8, FORCED, LANES)), sds((2,...  4.61 us
    pallas_call x1, Pallas kernels, local(): call(with_total(substeps, total), 'substeps', [sds((4, TX, TY)), sds((4,...  4.18 us
    pallas_call x1, Pallas kernels, local(): call(pack_lat, 'pack_lat', [half, half] + made, 10, [wide, wide, wide, pl...  2.8 us
    unnamed x22, local copies, waits for them, and re-layouts  1.84 us
    pallas_call x1, Pallas kernels, local(): call(with_total(middle_sums, total), 'middle_sums', [sds((6, TX, TY)), sd...  1.19 us
  transfers between devices with their start and end apart: 7, of which 4 were waited for; matrix products, arithmetic and copies ran while one was open for 0% of the time, Pallas kernels for 35%

profile of v4, /device:TPU:0, one launch (start us, length us, event | category | flops | bytes accessed | tf_op | source)
XLA Modules:
  0.0 41.0 jit_solution(6813917568017259570)
XLA Ops:
  0.6 0.0 copy-start
  0.6 0.0 copy-start.1
  0.7 2.8 %pack_lat.1 = (bf16[2,64,128]{2,1,0:T(8,128)(2,1)}, bf16[2,64,128]{2,1,0:T(8,128)(2,1)}, bf16[192,256]{1,0:T(8,128)(2,1)}, bf16[576,256]{1,0:T(8,128)(2,1)}, bf1...) custom-call(f32[4,64,512]{2,1,0:T(8,128)} %refs_0_.9, f32[4,64,512]{2,1,0:T(8,128)} %refs_1_.13, ...), custom_call_target="tpu_custom_call" | custom-call | tf_op jit(solution)/shard_map/pack_lat/pallas_call | solution.py:637
  3.5 2.1 %collective-permute-start = (bf16[2,64,128]{2,1,0:T(8,128)(2,1)}, bf16[2,64,128]{2,1,0:T(8,128)(2,1)S(1)}, u32[]{:S(2)}, u32[]{:S(2)}) collective-permute-start(bf16[2,64,128]{2,1,0:T(8,128)(2,1)} %get-tuple-element.24), channel_id=1, source_target_pairs={{0,2},{2,4},{4,6},{6,0},{1,3},{3,5},{5,7},{7,1},{8,10},{10,12},{12... | collective-permute-start | bytes 98312 | tf_op jit(solution)/shard_map/ppermute | solution.py:630
  5.5 2.2 %collective-permute-start.1 = (bf16[2,64,128]{2,1,0:T(8,128)(2,1)}, bf16[2,64,128]{2,1,0:T(8,128)(2,1)S(1)}, u32[]{:S(2)}, u32[]{:S(2)}) collective-permute-start(bf16[2,64,128]{2,1,0:T(8,128)(2,1)} %get-tuple-element.25), channel_id=1, source_target_pairs={{0,6},{2,0},{4,2},{6,4},{1,7},{3,1},{5,3},{7,5},{8,14},{10,8},{12,... | collective-permute-start | bytes 98312 | tf_op jit(solution)/shard_map/ppermute | solution.py:630
  7.7 0.9 %copy-done.3 = s32[64,512]{1,0:T(8,128)S(1)} copy-done((s32[64,512]{1,0:T(8,128)S(1)}, s32[64,512]{1,0:T(8,128)}, u32[]{:S(2)}) %copy-start.3) | copy-done | bytes 131096
  8.7 0.9 %copy-done.5 = f32[64,512]{1,0:T(8,128)S(1)} copy-done((f32[64,512]{1,0:T(8,128)S(1)}, f32[64,512]{1,0:T(8,128)}, u32[]{:S(2)}) %copy-start.5) | copy-done | bytes 131096
  9.6 0.0 copy-start.9
  9.6 0.0 copy-start.10
  9.6 0.2 collective-permute-done.refs_1_
  9.8 0.0 collective-permute-done.1.refs_2_
  9.8 0.0 copy-done.2
  9.8 0.3 pack_lon.1
  10.1 0.1 collective-permute-start.2
  10.1 5.3 %collective-permute-start.3 = (bf16[15,16,640]{2,1,0:T(8,128)(2,1)S(1)}, bf16[15,16,640]{2,1,0:T(8,128)(2,1)S(1)}, u32[]{:S(2)}, u32[]{:S(2)}) collective-permute-start(bf16[15,16,640]{2,1,0:T(8,128)(2,1)S(1)} %get-tuple-element.36), channel_id=1, source_target_pairs={{0,120},{8,0},{16,8},{24,16},{32,24},{40,32},{48,40},{56,48},{64,5... | collective-permute-start | bytes 921608 | tf_op jit(solution)/shard_map/ppermute | solution.py:630
  15.5 0.0 copy-done.7
  15.5 0.0 copy-done.9
  15.5 5.5 %interior.1 = (f32[8,104,640]{2,1,0:T(8,128)S(1)}, f32[8,128]{1,0:T(8,128)S(1)}) custom-call(f32[4,64,512]{2,1,0:T(8,128)S(1)} %copy-done, f32[4,64,512]{2,1,0:T(8,128)S(1)} %copy-done.1, s32[64,512]{1,0:T(8,128)S(1)} %copy-done.3, f32[14,64,128]{2,1,0:T(8,128)S(1)} %get-tuple-element.26.refs_3_.refs_4_.refs_6_, bf16[192,256]{1,0:T(8,128)(2,1)S(1)} %copy-done.8, ...), custom_call_target="tpu_custom_call" | custom-call | flops 7000000 | bytes 21000000 | tf_op jit(solution)/shard_map/interior/pallas_call | solution.py:680
  21.0 1.2 %middle_sums.1 = (f32[6,64,512]{2,1,0:T(8,128)S(1)}, bf16[5,64,512]{2,1,0:T(8,128)(2,1)S(1)}, f32[8,128]{1,0:T(8,128)S(1)}) custom-call(f32[8,128]{1,0:T(8,128)S(1)} %get-tuple-element.32.refs_0_, f32[4,64,512]{2,1,0:T(8,128)S(1)} %copy-done, f32[4,64,512]{2,1,0:T(8,128)S(1)} %copy-done.1, f32[4,64,512]{2,1,0:T(8,128)S(1)} %copy-done.2, ...), custom_call_target="tpu_custom_call" | custom-call | flops 1000000 | bytes 3000000 | tf_op jit(solution)/shard_map/middle_sums/pallas_call | solution.py:693
  22.2 0.1 collective-permute-start.4
  22.3 0.8 %seam_sums.1.refs_9_.refs_2_ = f32[7,64,384]{2,1,0:T(8,128)S(1)} custom-call(f32[4,64,512]{2,1,0:T(8,128)S(1)} %copy-done, f32[4,64,512]{2,1,0:T(8,128)S(1)} %copy-done.1, f32[4,64,512]{2,1,0:T(8,128)S(1)} %copy-done.2, s32[64,512]{1,0:T(8,128)S(1)} %copy-done.3, f32[14,64,128]{2,1,0:T(8,128)S(1)} %get-tuple-element.26.refs_3_.refs_4_.refs_6_, ...), custom_call_target="tpu_custom_call" | custom-call | flops 1000000 | bytes 3000000 | tf_op jit(solution)/shard_map/seam_sums/pallas_call | solution.py:702
  23.2 0.0 collective-permute-done.2.refs_7_.refs_5_
  23.2 0.0 collective-permute-done.3.refs_8_.refs_6_
  23.2 1.1 %rim_sums.1 = (f32[6,48,640]{2,1,0:T(8,128)S(1)}, bf16[9,16,640]{2,1,0:T(8,128)(2,1)S(1)}, f32[2,96,640]{2,1,0:T(8,128)S(1)}, f32[8,64,640]{2,1,0:T(8,128)S(1)}) custom-call(f32[8,128]{1,0:T(8,128)S(1)} %get-tuple-element.34.refs_0_, f32[4,64,512]{2,1,0:T(8,128)S(1)} %copy-done, f32[4,64,512]{2,1,0:T(8,128)S(1)} %copy-done.1, f32[4,64,512]{2,1,0:T(8,128)S(1)} %copy-done.2, ...), custom_call_target="tpu_custom_call" | custom-call | flops 2000000 | bytes 6000000 | tf_op jit(solution)/shard_map/rim_sums/pallas_call | solution.py:710
  24.3 2.1 %collective-permute-start.5 = (bf16[9,16,640]{2,1,0:T(8,128)(2,1)S(1)}, bf16[9,16,640]{2,1,0:T(8,128)(2,1)S(1)}, u32[]{:S(2)}, u32[]{:S(2)}) collective-permute-start(bf16[9,16,640]{2,1,0:T(8,128)(2,1)S(1)} %get-tuple-element.41), channel_id=1, source_target_pairs={{0,1},{1,0},{2,3},{3,2},{4,5},{5,4},{6,7},{7,6},{8,9},{9,8},{10,11... | collective-permute-start | bytes 552968 | tf_op jit(solution)/shard_map/ppermute | solution.py:630
  26.4 4.6 %edges.1 = (f32[8,104,640]{2,1,0:T(8,128)S(1)}, bf16[2,48,640]{2,1,0:T(8,128)(2,1)S(1)}) custom-call(f32[8,64,640]{2,1,0:T(8,128)S(1)} %get-tuple-element.42.refs_0_, f32[2,96,640]{2,1,0:T(8,128)S(1)} %get-tuple-element.37.refs_1_.refs_0_, bf16[192,256]{1,0:T(8,128)(2,1)S(1)} %copy-done.8, ...), custom_call_target="tpu_custom_call", output_to_operand_aliasing={{0}: (7, {})} | custom-call | flops 6000000 | bytes 18000000 | tf_op jit(solution)/shard_map/edges/pallas_call | solution.py:719
  31.0 0.1 collective-permute-start.6
  31.1 0.6 %collective-permute-done.4.refs_8_.refs_4_ = bf16[5,64,512]{2,1,0:T(8,128)(2,1)S(1)} collective-permute-done((bf16[5,64,512]{2,1,0:T(8,128)(2,1)S(1)}, bf16[5,64,512]{2,1,0:T(8,128)(2,1)S(1)}, u32[]{:S(2)}, u32[]{:S(2)}) %collective-permute-start.4) | collective-permute-done | bytes 327712 | tf_op jit(solution)/shard_map/ppermute | solution.py:630
  31.7 2.2 %collective-permute-done.5.refs_9_.refs_5_ = bf16[9,16,640]{2,1,0:T(8,128)(2,1)S(1)} collective-permute-done((bf16[9,16,640]{2,1,0:T(8,128)(2,1)S(1)}, bf16[9,16,640]{2,1,0:T(8,128)(2,1)S(1)}, u32[]{:S(2)}, u32[]{:S(2)}) %collective-permute-start.5) | collective-permute-done | bytes 184352 | tf_op jit(solution)/shard_map/ppermute | solution.py:630
  33.9 1.1 %own_part.1.refs_8_ = f32[8,64,512]{2,1,0:T(8,128)S(1)} custom-call(f32[4,64,512]{2,1,0:T(8,128)S(1)} %copy-done, f32[4,64,512]{2,1,0:T(8,128)S(1)} %copy-done.1, f32[4,64,512]{2,1,0:T(8,128)S(1)} %copy-done.2, s32[64,512]{1,0:T(8,128)S(1)} %copy-done.4, f32[14,64,128]{2,1,0:T(8,128)S(1)} %get-tuple-element.26.refs_3_.refs_4_.refs_6_, ...), custom_call_target="tpu_custom_call" | custom-call | flops 2000000 | bytes 6000000 | tf_op jit(solution)/shard_map/own_part/pallas_call | solution.py:729
  35.0 1.9 %collective-permute-done.6.refs_7_ = bf16[2,48,640]{2,1,0:T(8,128)(2,1)S(1)} collective-permute-done((bf16[2,48,640]{2,1,0:T(8,128)(2,1)S(1)}, bf16[2,48,640]{2,1,0:T(8,128)(2,1)S(1)}, u32[]{:S(2)}, u32[]{:S(2)}) %collective-permute-start.6) | collective-permute-done | bytes 122912 | tf_op jit(solution)/shard_map/ppermute | solution.py:630
  36.8 4.2 %substeps.1 = (f32[4,64,512]{2,1,0:T(8,128)}, f32[4,64,512]{2,1,0:T(8,128)}, f32[64,512]{1,0:T(8,128)}) custom-call(f32[2,96,640]{2,1,0:T(8,128)S(1)} %get-tuple-element.37.refs_1_.refs_0_, f32[6,64,512]{2,1,0:T(8,128)S(1)} %get-tuple-element.38.refs_1_, f32[7,64,384]{2,1,0:T(8,128)S(1)} %seam_sums.1.refs_9_.refs_2_, ...), custom_call_target="tpu_custom_call" | custom-call | flops 5000000 | bytes 15000000 | tf_op jit(solution)/shard_map/substeps/pallas_call | solution.py:740
  (14 shorter events, 0.0 us)
Async XLA Ops:
  0.6 9.1 %copy-start = (f32[4,64,512]{2,1,0:T(8,128)S(1)}, f32[4,64,512]{2,1,0:T(8,128)}, u32[]{:S(2)}) copy-start(f32[4,64,512]{2,1,0:T(8,128)} %refs_0_.9) | copy-start | bytes 1572868
  0.6 9.1 %copy-start.1 = (f32[4,64,512]{2,1,0:T(8,128)S(1)}, f32[4,64,512]{2,1,0:T(8,128)}, u32[]{:S(2)}) copy-start(f32[4,64,512]{2,1,0:T(8,128)} %refs_1_.13) | copy-start | bytes 1572868
  0.7 9.1 %copy-start.2 = (f32[4,64,512]{2,1,0:T(8,128)S(1)}, f32[4,64,512]{2,1,0:T(8,128)}, u32[]{:S(2)}) copy-start(f32[4,64,512]{2,1,0:T(8,128)} %refs_2_.11) | copy-start | bytes 1572868
  3.5 6.3 %collective-permute-start = (bf16[2,64,128]{2,1,0:T(8,128)(2,1)}, bf16[2,64,128]{2,1,0:T(8,128)(2,1)S(1)}, u32[]{:S(2)}, u32[]{:S(2)}) collective-permute-start(bf16[2,64,128]{2,1,0:T(8,128)(2,1)} %get-tuple-element.24), channel_id=1, source_target_pairs={{0,2},{2,4},{4,6},{6,0},{1,3},{3,5},{5,7},{7,1},{8,10},{10,12},{12... | collective-permute-start | bytes 98312 | tf_op jit(solution)/shard_map/ppermute | solution.py:630
  5.5 4.2 %collective-permute-start.1 = (bf16[2,64,128]{2,1,0:T(8,128)(2,1)}, bf16[2,64,128]{2,1,0:T(8,128)(2,1)S(1)}, u32[]{:S(2)}, u32[]{:S(2)}) collective-permute-start(bf16[2,64,128]{2,1,0:T(8,128)(2,1)} %get-tuple-element.25), channel_id=1, source_target_pairs={{0,6},{2,0},{4,2},{6,4},{1,7},{3,1},{5,3},{7,5},{8,14},{10,8},{12,... | collective-permute-start | bytes 98312 | tf_op jit(solution)/shard_map/ppermute | solution.py:630
  7.7 0.9 %copy-start.3 = (s32[64,512]{1,0:T(8,128)S(1)}, s32[64,512]{1,0:T(8,128)}, u32[]{:S(2)}) copy-start(s32[64,512]{1,0:T(8,128)} %refs_3_.11) | copy-start | bytes 393220
  8.6 0.9 %copy-start.5 = (f32[64,512]{1,0:T(8,128)S(1)}, f32[64,512]{1,0:T(8,128)}, u32[]{:S(2)}) copy-start(f32[64,512]{1,0:T(8,128)} %refs_5_.7) | copy-start | bytes 393220
  9.6 5.9 %copy-start.6 = (bf16[576,256]{1,0:T(8,128)(2,1)S(1)}, bf16[576,256]{1,0:T(8,128)(2,1)}, u32[]{:S(2)}) copy-start(bf16[576,256]{1,0:T(8,128)(2,1)} %get-tuple-element.28.refs_5_.refs_3_) | copy-start | bytes 884740
  9.6 5.9 %copy-start.7 = (bf16[192,320]{1,0:T(8,128)(2,1)S(1)}, bf16[192,320]{1,0:T(8,128)(2,1)}, u32[]{:S(2)}) copy-start(bf16[192,320]{1,0:T(8,128)(2,1)} %get-tuple-element.29.refs_6_.refs_4_) | copy-start | bytes 368644
  9.6 5.9 %copy-start.8 = (bf16[192,256]{1,0:T(8,128)(2,1)S(1)}, bf16[192,256]{1,0:T(8,128)(2,1)}, u32[]{:S(2)}) copy-start(bf16[192,256]{1,0:T(8,128)(2,1)} %get-tuple-element.27.refs_4_.refs_2_) | copy-start | bytes 294916
  9.6 5.9 %copy-start.9 = (f32[192,128]{1,0:T(8,128)S(1)}, f32[192,128]{1,0:T(8,128)}, u32[]{:S(2)}) copy-start(f32[192,128]{1,0:T(8,128)} %get-tuple-element.30.refs_7_.refs_5_) | copy-start | bytes 294916
  9.6 5.9 %copy-start.10 = (f32[192,128]{1,0:T(8,128)S(1)}, f32[192,128]{1,0:T(8,128)}, u32[]{:S(2)}) copy-start(f32[192,128]{1,0:T(8,128)} %get-tuple-element.31.refs_8_.refs_6_) | copy-start | bytes 294916
  10.1 13.1 %collective-permute-start.2 = (bf16[15,16,640]{2,1,0:T(8,128)(2,1)S(1)}, bf16[15,16,640]{2,1,0:T(8,128)(2,1)S(1)}, u32[]{:S(2)}, u32[]{:S(2)}) collective-permute-start(bf16[15,16,640]{2,1,0:T(8,128)(2,1)S(1)} %get-tuple-element.35), channel_id=1, source_target_pairs={{0,8},{8,16},{16,24},{24,32},{32,40},{40,48},{48,56},{56,64},{64,7... | collective-permute-start | bytes 921608 | tf_op jit(solution)/shard_map/ppermute | solution.py:630
  10.1 13.1 %collective-permute-start.3 = (bf16[15,16,640]{2,1,0:T(8,128)(2,1)S(1)}, bf16[15,16,640]{2,1,0:T(8,128)(2,1)S(1)}, u32[]{:S(2)}, u32[]{:S(2)}) collective-permute-start(bf16[15,16,640]{2,1,0:T(8,128)(2,1)S(1)} %get-tuple-element.36), channel_id=1, source_target_pairs={{0,120},{8,0},{16,8},{24,16},{32,24},{40,32},{48,40},{56,48},{64,5... | collective-permute-start | bytes 921608 | tf_op jit(solution)/shard_map/ppermute | solution.py:630
  22.2 9.4 %collective-permute-start.4 = (bf16[5,64,512]{2,1,0:T(8,128)(2,1)S(1)}, bf16[5,64,512]{2,1,0:T(8,128)(2,1)S(1)}, u32[]{:S(2)}, u32[]{:S(2)}) collective-permute-start(bf16[5,64,512]{2,1,0:T(8,128)(2,1)S(1)} %get-tuple-element.40), channel_id=1, source_target_pairs={{0,1},{1,0},{2,3},{3,2},{4,5},{5,4},{6,7},{7,6},{8,9},{9,8},{10,11... | collective-permute-start | bytes 983048 | tf_op jit(solution)/shard_map/ppermute | solution.py:630
  24.3 9.5 %collective-permute-start.5 = (bf16[9,16,640]{2,1,0:T(8,128)(2,1)S(1)}, bf16[9,16,640]{2,1,0:T(8,128)(2,1)S(1)}, u32[]{:S(2)}, u32[]{:S(2)}) collective-permute-start(bf16[9,16,640]{2,1,0:T(8,128)(2,1)S(1)} %get-tuple-element.41), channel_id=1, source_target_pairs={{0,1},{1,0},{2,3},{3,2},{4,5},{5,4},{6,7},{7,6},{8,9},{9,8},{10,11... | collective-permute-start | bytes 552968 | tf_op jit(solution)/shard_map/ppermute | solution.py:630
  26.4 7.4 %copy-start.4 = (s32[64,512]{1,0:T(8,128)S(1)}, s32[64,512]{1,0:T(8,128)}, u32[]{:S(2)}) copy-start(s32[64,512]{1,0:T(8,128)} %refs_3_.11) | copy-start | bytes 393220
  31.0 5.8 %collective-permute-start.6 = (bf16[2,48,640]{2,1,0:T(8,128)(2,1)S(1)}, bf16[2,48,640]{2,1,0:T(8,128)(2,1)S(1)}, u32[]{:S(2)}, u32[]{:S(2)}) collective-permute-start(bf16[2,48,640]{2,1,0:T(8,128)(2,1)S(1)} %get-tuple-element.44), channel_id=1, source_target_pairs={{0,1},{1,0},{2,3},{3,2},{4,5},{5,4},{6,7},{7,6},{8,9},{9,8},{10,11... | collective-permute-start | bytes 368648 | tf_op jit(solution)/shard_map/ppermute | solution.py:630

commit v5 on v4

--- a/solution.py
+++ b/solution.py
@@ -31,6 +31,30 @@
 VMEM = pl.BlockSpec(memory_space=pltpu.VMEM)
 
 
+def placed(n, *spots):
+    return [(src, n, block, at) for src, (block, at) in zip((0, 128 - n), spots)]
+
+
+SPOTS = (
+    [placed(EDGE, (1 + i // 3, 36 * (i % 3)), (1 + i // 3, 36 * (i % 3) + 18)) for i in range(8)]
+    + [placed(16, (0, 32 * k), (0, 32 * k + 16)) for k in range(4)]
+    + [placed(16, (3, 72), (3, 88)), placed(16, (2, 108), (3, 104)), placed(4, (1, 108), (1, 112))]
+)
+
+
+def outer_lanes(halo, i):
+    lane = lax.broadcasted_iota(jnp.int32, (16, 128), 1)
+    found = jnp.zeros((16, 128), F32)
+    for src, n, block, at in SPOTS[i]:
+        moved = pltpu.roll(halo[15, :, 128 * block : 128 * block + 128].astype(F32), (src - at) % 128, 1)
+        found = jnp.where((lane >= src) & (lane < src + n), moved, found)
+    return found
+
+
+def sent_rows(halo, i):
+    return jnp.concatenate([halo[i].astype(F32), outer_lanes(halo, i)], 1)
+
+
 def sds(shape, dtype=F32):
     return jax.ShapeDtypeStruct(shape, dtype)
 
@@ -50,32 +74,32 @@
 
 
 def pack_lat(sc, u, v, b, l, s, *refs):
-    raw, to_down, to_up, made = refs[:5], refs[5], refs[6], refs[7:12]
-    ub, vb, bb, lb, sb, sem = refs[12:18]
-    held, spread, weight_sem = refs[18:23], refs[23], refs[24]
+    raw, to_down, to_up, flat, made = refs[:5], refs[5], refs[6], refs[7], refs[8:13]
+    ub, vb, bb, lb, sb, sem = refs[13:19]
+    held, spread, weight_sem = refs[19:24], refs[24], refs[25]
     base = 4 * sc[0]
     lane = lax.broadcasted_iota(jnp.int32, (TX, 128), 1)
     copies = []
     for side, at in enumerate((0, TY - 128)):
         for n, (src, dst) in enumerate(((u, ub), (v, vb), (b, bb))):
             copies.append(pltpu.make_async_copy(src.at[:, :, at : at + 128], dst.at[side], sem.at[side, n]))
-        for n, (src, dst) in enumerate(((l, lb), (s, sb))):
-            copies.append(pltpu.make_async_copy(src.at[:, at : at + 128], dst.at[side], sem.at[side, 3 + n]))
+    copies = [pltpu.make_async_copy(l, lb, sem.at[0, 3]), pltpu.make_async_copy(s, sb, sem.at[0, 4])] + copies
     more = [pltpu.make_async_copy(src, dst, weight_sem.at[n]) for n, (src, dst) in enumerate(zip(raw, held))]
     for copy in copies + more:
         copy.start()
 
     def fields(side):
-        bl = lb[side].astype(F32)
+        at = slice(0, 128) if side == 0 else slice(TY - 128, TY)
+        bl = lb[:, at].astype(F32)
         wets = [wet_of(bl, (base + k).astype(F32)) for k in range(4)]
         for a in (ub, vb, bb):
             for k in range(4):
                 yield a[side, k] * wets[k]
         yield bl
-        yield sb[side]
+        yield sb[:, at]
 
     for side, (out, origin) in enumerate(((to_down, 0), (to_up, 128 - EDGE))):
-        for copy in copies[5 * side : 5 * side + 5]:
+        for copy in copies[:5] if side == 0 else copies[5:]:
             copy.wait()
         for i, field in enumerate(fields(side)):
             tile, place = divmod(i, 7)
@@ -85,18 +109,19 @@
             acc = jnp.where((lane >= EDGE * place) & (lane < EDGE * (place + 1)), moved, acc)
             if place == 6:
                 out[tile] = acc.astype(BF)
+    flat[0] = lb[...].astype(F32)
+    flat[1] = sb[...]
     for copy in more:
         copy.wait()
     build_weights(*held, *made, spread)
 
 
-def bring(sc, bl, s, done):
-    done[...] = bl[0:8, 0:128].astype(F32) + s[0:8, 0:128]
-
-
-def pack_lon(total, sc, near, before, after, *refs):
-    tops, bots, extra_t, extra_b = refs[0:5], refs[5:10], refs[10:13], refs[13:16]
-    hal, to_down, to_up, work = refs[16:]
+def bring(sc, flat, done):
+    done[...] = flat[0, 0:8, 0:128] + flat[1, 0:8, 0:128]
+
+
+def pack_lon(total, sc, near, before, after, u, v, b, flat, hal, to_down, to_up, work):
+    bl, s = flat.at[0], flat.at[1]
     base = 4 * sc[0]
     lane = lax.broadcasted_iota(jnp.int32, (TX, 128), 1)
     low_from = jnp.where(sc[1] > 0, 128 - EDGE, 128)
@@ -104,28 +129,37 @@
     for tile in range(2):
         low, high = before[tile].astype(F32), after[tile].astype(F32)
         for place in range(7):
-            a = pltpu.roll(high, (-EDGE * place) % 128, 1)
-            b = pltpu.roll(low, (128 - EDGE - EDGE * place) % 128, 1)
-            hal[tile * 7 + place] = jnp.where(lane < high_to, a, jnp.where(lane >= low_from, b, 0.0))
-    for out, (u, v, b, l, s), row in ((to_down, tops, 0), (to_up, bots, TX - 16)):
-        bl = l[...].astype(F32)
+            beyond = pltpu.roll(high, (-EDGE * place) % 128, 1)
+            short = pltpu.roll(low, (128 - EDGE - EDGE * place) % 128, 1)
+            hal[tile * 7 + place] = jnp.where(lane < high_to, beyond, jnp.where(lane >= low_from, short, 0.0))
+    for out, row in ((to_down, 0), (to_up, TX - 16)):
+        rr = slice(row, row + 16)
+        level = bl[rr, :]
         for k in range(4):
-            wet = wet_of(bl, (base + k).astype(F32))
+            wet = wet_of(level, (base + k).astype(F32))
             for n, a in enumerate((u, v, b)):
-                out[4 * n + k, :, :TY] = (a[k] * wet).astype(BF)
-        out[12, :, :TY] = bl.astype(BF)
-        out[13, :, :TY] = s[...].astype(BF)
-        for i in range(FIELDS):
-            out[i, :, TY:] = hal[i, row : row + 16, :].astype(BF)
-    for out, (u, v, l), first, row in ((to_down, extra_t, 0, 16), (to_up, extra_b, 6, 46)):
-        bl = l[first : first + 2, :].astype(F32)
+                out[4 * n + k] = (a[k, rr, :] * wet).astype(BF)
+        out[12] = level.astype(BF)
+        out[13] = s[rr, :].astype(BF)
+    for out, row in ((to_down, 16), (to_up, 46)):
+        rr = slice(row, row + 2)
+        level = bl[rr, :]
         for k in range(4):
-            wet = wet_of(bl, (base + k).astype(F32))
+            wet = wet_of(level, (base + k).astype(F32))
             for n, a in enumerate((u, v)):
-                work[2 * (4 * n + k) : 2 * (4 * n + k) + 2, :TY] = a[k, first : first + 2, :] * wet
+                work[2 * (4 * n + k) : 2 * (4 * n + k) + 2, :TY] = a[k, rr, :] * wet
         for i in range(8):
             work[2 * i : 2 * i + 2, TY:] = hal[i, row : row + 2, :]
-        out[14] = work[...].astype(BF)
+        out[14] = work[:, :TY].astype(BF)
+        near = 0 if row == 16 else TX - 16
+        column = lax.broadcasted_iota(jnp.int32, (16, 128), 1)
+        blocks = [jnp.zeros((16, 128), F32)] * 4
+        for i in range(FIELDS + 1):
+            field = hal[i, near : near + 16, :] if i < FIELDS else work[:, TY:]
+            for src, n, block, at in SPOTS[i]:
+                moved = pltpu.roll(field, (at - src) % 128, 1)
+                blocks[block] = jnp.where((column >= at) & (column < at + n), moved, blocks[block])
+        out[15] = jnp.concatenate(blocks, 1).astype(BF)
 
 
 def build_weights(w_in, b_in, w_mid, b_mid, w_out, w1, w2, w3, b1, b2, spread):
@@ -193,12 +227,12 @@
             store(part, j, (closure_coef * o).astype(BF).astype(F32).reshape(8, 8, LANES))
 
 
-def interior(total, sc, u, v, bl, hal, w1, w2, w3, b1, b2, out, done, up, in0, act1, act2):
+def interior(total, sc, u, v, flat, hal, w1, w2, w3, b1, b2, out, done, up, in0, act1, act2):
     done[...] = jnp.zeros_like(done)
 
     @pl.when(sc[0] == 0)
     def _():
-        level = bl[...].astype(F32)
+        level = flat[0]
         for k in range(4):
             wet = wet_of(level, float(k))
             up[k, :, :TY] = u[k] * wet
@@ -229,15 +263,16 @@
 
         parts = [(0, 0, 5, 4, 4, 3), (26, 29, 0, 4, 4, 3)]
         closure(in0, act1, act2, (w1, w2, w3, b1, b2), inside_of(sc[1], total, (1, LANES)), parts, store)
-        for i in range(0, 48, 16):
-            halves = []
-            for p in (i, i + 8):
-                r = p if p < RIM else p + 48
-                level = two[0, r : r + 8, :]
-                rows = slice(r + 4, r + 12)
-                halves.append(forced(sc, level, out, rows, [slice(0, LANES)], ~inner_rows(r - HALO, level.shape)))
+        def extra(r):
+            level = two[0, r : r + 8, :]
+            return forced(sc, level, out, slice(r + 4, r + 12), [slice(0, LANES)], ~inner_rows(r - HALO, level.shape))
+
+        for side, r in enumerate((0, 80)):
+            halves = extra(r), extra(r + 8)
             for n in range(2):
-                send[n, i : i + 16, :] = jnp.concatenate([halves[0][n], halves[1][n]], 0).astype(BF)
+                send[2 * n + side] = jnp.concatenate([halves[0][n], halves[1][n]], 0).astype(BF)
+        halves = extra(16), extra(72)
+        send[4] = jnp.concatenate([halves[0][n] + halves[1][n] for n in range(2)], 0).astype(BF)
 
     @pl.when(sc[0] != 0)
     def _():
@@ -322,9 +357,10 @@
     return (x >= 4) & (x < 60)
 
 
-def middle_sums(total, sc, first, u, v, b, bl, s, force, sums, send, done, pr, load):
+def middle_sums(total, sc, first, u, v, b, flat, force, sums, send, done, pr, load):
     done[...] = jnp.zeros_like(done)
     base = 4 * sc[0]
+    bl, s = flat.at[0], flat.at[1]
 
     def wet(k, rr):
         return wet_of(bl[rr, :].astype(F32), (base + k).astype(F32))
@@ -355,8 +391,9 @@
         send[4, q : q + 16, :] = load[q + 8 : q + 24, :].astype(BF)
 
 
-def seam_sums(total, sc, u, v, b, bl, hal, force, sums, ext, pr, load):
+def seam_sums(total, sc, u, v, b, flat, hal, force, sums, ext, pr, load):
     base = 4 * sc[0]
+    bl, s = flat.at[0], flat.at[1]
     last, first = slice(TY - 128, TY), slice(0, 128)
 
     def three(a, outer, b):
@@ -384,8 +421,9 @@
             sums[i, rr, :] = a
 
 
-def rim_sums(total, sc, ready, u, v, b, bl, s, hal, low, high, seam, sums, send, two, edge, ext, pr, load):
+def rim_sums(total, sc, ready, u, v, b, flat, hal, low, high, seam, sums, send, two, edge, ext, pr, load):
     base = 4 * sc[0]
+    bl, s = flat.at[0], flat.at[1]
     tall = 32
     loads = []
     for side, halo in ((0, low), (1, high)):
@@ -393,7 +431,7 @@
         hr, orr = (slice(0, 16), slice(16, 32)) if side == 0 else (slice(16, 32), slice(0, 16))
         level = bl[own, :].astype(F32)
         for i in range(13):
-            ext[i, hr, :] = halo[i].astype(F32)
+            ext[i, hr, :] = sent_rows(halo, i)
             ext[i, orr, TY:] = hal[i, own, :]
         for k in range(4):
             wet = wet_of(level, (base + k).astype(F32))
@@ -414,7 +452,7 @@
             found = sums_of(sc, coriolis, ext[12, rr, :], lambda k: ext[k, rr, :], lambda k: ext[4 + k, rr, :], pr, load, r)
             for i, a in enumerate(found):
                 sums[i, RIM * side + 8 * j : RIM * side + 8 * j + 8, :] = a
-        more = halo[14].astype(F32)
+        more = sent_rows(halo, 14)
         for i in range(8):
             if side == 0:
                 edge[i, 0:8, :] = jnp.zeros((8, LANES), F32)
@@ -425,8 +463,8 @@
                 edge[i, 56:64, :] = jnp.zeros((8, LANES), F32)
                 edge[i, 56:58, :] = more[2 * i : 2 * i + 2, :]
         at = slice(0, 16) if side == 0 else slice(80, 96)
-        two[0, at, :] = halo[12].astype(F32)
-        two[1, at, :] = halo[13].astype(F32)
+        two[0, at, :] = sent_rows(halo, 12)
+        two[1, at, :] = sent_rows(halo, 13)
     two[0, 16:80, :TY] = bl[...].astype(F32)
     two[1, 16:80, :TY] = s[...]
     for i in range(2):
@@ -454,34 +492,22 @@
     send[8] = jnp.concatenate(ends + loads + [jnp.zeros((6, LANES), F32)], 0).astype(BF)
 
 
-def own_part(total, sc, u, v, b, bl, hal, low, high, force, mid_in, rim_in, out, pr, load):
+def own_part(total, sc, u, v, b, flat, hal, low, high, force, out, done, pr, load):
+    done[...] = jnp.zeros_like(done)
     base = 4 * sc[0]
+    bl, s = flat.at[0], flat.at[1]
     upper = jnp.where(sc[0] == 0, step_dt, 0.0)
 
     def b_rows(k, r):
         if r == 0:
-            return low[8 + k].astype(F32)[8:16]
+            return sent_rows(low, 8 + k)[8:16]
         if r == TX + 8:
-            return high[8 + k].astype(F32)[0:8]
+            return sent_rows(high, 8 + k)[0:8]
         at = slice(r - 8, r)
         wet = wet_of(bl[at, :].astype(F32), (base + k).astype(F32))
         return jnp.concatenate([b[k, at, :] * wet, hal[8 + k, at, :]], 1)
 
     pressures(base, b_rows, pr, load, TX + 16)
-    lane = lax.broadcasted_iota(jnp.int32, (16, 128), 1)
-    for x in range(0, TX, 16):
-        turn = x // 32
-        beyond = rim_in[x // 16 % 2, :, TY:].astype(F32)
-        outer = jnp.where(lane < 64, pltpu.roll(beyond, 44 - 2 * turn, 1), pltpu.roll(beyond, 42 - 2 * turn, 1))
-        above = jnp.concatenate([mid_in[4, x : x + 16, :].astype(F32), outer], 1)
-        above = jnp.where(upper > 0.0, 0.0, above)
-        for k in range(4):
-            pr[k, x + 16 : x + 32, :] = pr[k, x + 16 : x + 32, :] + above
-    ends = rim_in[8].astype(F32)
-    for at, row in ((8, 15), (9, TX + 16)):
-        above = jnp.where(upper > 0.0, 0.0, ends[at : at + 1, :])
-        for k in range(4):
-            pr[k, row : row + 1, :] = pr[k, row : row + 1, :] + above
     coriolis = coriolis_of(sc[1], total, (8, LANES))[:, :TY]
     for r in range(0, TX, 8):
         rr = slice(r, r + 8)
@@ -501,9 +527,8 @@
             out[4 + k, rr, :] = wet * (north + step_dt * (tn + fn))
 
 
-def substeps(total, sc, two, mid, seam, rim, mid_in, rim_in, force, force_in, own, east_out, north_out, surface_out, lv, fx, fy, eb, nb, ae, an, es, ns, rel, c2):
+def prepare(total, sc, ready, two, mid, seam, rim, mid_in, rim_in, force, ae, an, es, ns, rel, c2, off, above):
     zero8 = jnp.zeros((8, LANES), F32)
-    lower = jnp.zeros((8, LANES), jnp.int32) + sc[0] > 0
     lane = lax.broadcasted_iota(jnp.int32, (8, 128), 1)
 
     def ended(i, at, outer):
@@ -512,9 +537,6 @@
         pieces = [first, mid[i, at, 128 : TY - 128], last]
         return jnp.concatenate(pieces + [seam[i, at, 128:256]] if outer else pieces, 1)
 
-    for ref in (lv, fx):
-        ref[0:8, :] = zero8
-        ref[ROWS + 8 : ROWS + 16, :] = zero8
     for r in range(0, ROWS, 8):
         rr = slice(r, r + 8)
         level = two[0, rr, :]
@@ -549,16 +571,59 @@
         if not middle:
             everywhere = level == level
             mine = forced(sc, level, force, slice(r + 4, r + 12), [slice(0, LANES)], everywhere)
-            pair, half = at.start // 16 * 16, at.start % 16
-            for n in range(2):
-                theirs = force_in[n, pair : pair + 16, :].astype(F32)[half : half + 8]
-                found[n] = found[n] + jnp.where(lower, theirs, mine[n])
+            found[:2] = [found[n] + mine[n] for n in range(2)]
         ae[rr, :] = sub_dt * found[0] * over
         an[rr, :] = sub_dt * found[1] * over
         e, n = found[2] * over, found[3] * over
         es[rr, :], ns[rr, :] = e, n
-        eb[rr, :], nb[rr, :] = e, n
+
+    @pl.when(sc[0] == 0)
+    def _():
+        off[0] = es[HALO : HALO + TX, :TY]
+        off[1] = ns[HALO : HALO + TX, :TY]
+
+    @pl.when(sc[0] != 0)
+    def _():
+        lane = lax.broadcasted_iota(jnp.int32, (16, 128), 1)
+        for x in range(0, TX, 16):
+            turn = x // 32
+            beyond = rim_in[x // 16 % 2, :, TY:].astype(F32)
+            outer = jnp.where(lane < 64, pltpu.roll(beyond, 44 - 2 * turn, 1), pltpu.roll(beyond, 42 - 2 * turn, 1))
+            above[x + 8 : x + 24, :TY] = mid_in[4, x : x + 16, :].astype(F32)
+            above[x + 8 : x + 24, TY:] = outer
+        ends = rim_in[8].astype(F32)
+        above[7:8, :], above[TX + 8 : TX + 9, :] = ends[8:9, :], ends[9:10, :]
+        for r in range(0, TX, 8):
+            gx, gy = grads(above, r)
+            at = slice(r + HALO, r + HALO + 8)
+            off[0, r : r + 8, :] = es[at, :TY] + (step_dt * press_coef) * gx[:, :TY]
+            off[1, r : r + 8, :] = ns[at, :TY] + (step_dt * press_coef) * gy[:, :TY]
+
+
+def substeps(total, sc, two, ae_in, an_in, es, ns, rel, c2, off, force_in, own, east_out, north_out, surface_out, lv, fx, fy, eb, nb, ae, an):
+    zero8 = jnp.zeros((8, LANES), F32)
+    for ref in (lv, fx):
+        ref[0:8, :] = zero8
+        ref[ROWS + 8 : ROWS + 16, :] = zero8
+    share = jnp.where(sc[0] > 0, sub_dt, 0.0)
+    for r in range(0, ROWS, 8):
+        rr = slice(r, r + 8)
+        eb[rr, :], nb[rr, :] = es[rr, :], ns[rr, :]
         lv[r + 8 : r + 16, :] = two[1, rr, :]
+        if RIM <= r < ROWS - RIM:
+            ae[rr, :], an[rr, :] = ae_in[rr, :], an_in[rr, :]
+            continue
+        level = two[0, rr, :]
+        over = share / jnp.maximum(level + 0.125 * level * (level - 1.0), 1.0)
+        row = lax.broadcasted_iota(jnp.int32, (8, LANES), 0)
+        for n, (old, new) in enumerate(((ae_in, ae), (an_in, an))):
+            if HALO <= r < ROWS - HALO:
+                theirs = force_in[4].astype(F32)[8 * n : 8 * n + 8]
+                theirs = jnp.where((row < 4) if r < RIM else (row >= 4), theirs, 0.0)
+            else:
+                half = r % 16
+                theirs = force_in[2 * n + (r > RIM), :, :].astype(F32)[half : half + 8]
+            new[rr, :] = old[rr, :] + over * theirs
     inside = inside_of(sc[1], total, (8, LANES))
 
     def step(first, carry):
@@ -588,8 +653,8 @@
     for q in range(0, TX, 8):
         rr, at = slice(q + HALO, q + HALO + 8), slice(q, q + 8)
         level = two[0, rr, :TY]
-        fe = eb[rr, :TY] - es[rr, :TY] - (step_dt / sub_dt) * ae[rr, :TY]
-        fn = nb[rr, :TY] - ns[rr, :TY] - (step_dt / sub_dt) * an[rr, :TY]
+        fe = eb[rr, :TY] - off[0, at, :] - (step_dt / sub_dt) * ae[rr, :TY]
+        fn = nb[rr, :TY] - off[1, at, :] - (step_dt / sub_dt) * an[rr, :TY]
         for k in range(4):
             wet = wet_of(level, (base + k).astype(F32))
             east_out[k, at, :] = own[k, at, :] + wet * fe
@@ -597,14 +662,14 @@
         surface_out[at, :] = lv[q + HALO + 8 : q + HALO + 16, :TY]
 
 
-def call(kernel, name, out_shape, n_in, scratch=(), in_specs=None, cost=None, grid=(), aliases=None, room=28):
+def call(kernel, name, out_shape, n_in, scratch=(), in_specs=None, cost=None, grid=(), aliases=None, room=20):
     single = not isinstance(out_shape, (list, tuple))
 
-    def placed(*refs):
+    def body(*refs):
         kernel((lax.axis_index("grp"), lax.axis_index("lat")), *refs)
 
     return pl.pallas_call(
-        placed,
+        body,
         name=name,
         grid=grid,
         out_shape=out_shape,
@@ -634,17 +699,17 @@
     total = TY * lax.axis_size("lat")
     wide, half = pltpu.VMEM((2, 4, TX, 128), F32), sds((2, TX, 128), BF)
     made = [sds((192, 256), BF), sds((576, 256), BF), sds((192, 320), BF), sds((192, 128)), sds((192, 128))]
-    to_down, to_up, *weights = call(
+    to_down, to_up, flat, *weights = call(
         pack_lat,
         "pack_lat",
-        [half, half] + made,
+        [half, half, sds((2, TX, TY))] + made,
         10,
         [
             wide,
             wide,
             wide,
-            pltpu.VMEM((2, TX, 128), jnp.int32),
-            pltpu.VMEM((2, TX, 128), F32),
+            pltpu.VMEM((TX, TY), jnp.int32),
+            pltpu.VMEM((TX, TY), F32),
             pltpu.SemaphoreType.DMA((2, 5)),
             pltpu.VMEM((9, 8, 32), BF),
             pltpu.VMEM((1, 32), F32),
@@ -660,21 +725,16 @@
     before = shifted(to_up, "lat", 1)
     after = shifted(to_down, "lat", -1)
 
-    near = call(bring, "bring", TOKEN, 2, cost=micros(1))(bl, s)
-
-    def rows(n, i, three):
-        return [pl.BlockSpec((4, n, TY), lambda _: (0, i, 0))] * three + [pl.BlockSpec((n, TY), lambda _: (i, 0))] * (three - 1)
-
-    out = sds((15, 16, LANES), BF)
+    near = call(bring, "bring", TOKEN, 1, cost=micros(1))(flat)
+
+    out = sds((16, 16, TY), BF)
     hal, down, up = call(
         with_total(pack_lon, total),
         "pack_lon",
         [sds((FIELDS, TX, 128)), out, out],
-        19,
+        7,
         [pltpu.VMEM((16, LANES), F32)],
-        in_specs=[VMEM, VMEM, VMEM] + rows(16, 0, 3) + rows(16, 3, 3) + rows(8, 2, 2) + rows(8, 5, 2),
-        grid=(1,),
-    )(near, before, after, u, v, b, bl, s, u, v, b, bl, s, u, v, bl, u, v, bl)
+    )(near, before, after, u, v, b, flat)
     low = shifted(up, "lon", 1)
     high = shifted(down, "lon", -1)
     inner, ready = call(
@@ -689,15 +749,15 @@
             pltpu.VMEM((60 * 32, LANES), BF),
         ],
         cost=micros(7),
-    )(u, v, bl, hal, *weights)
+    )(u, v, flat, hal, *weights)
     mid, mid_send, summed = call(
         with_total(middle_sums, total),
         "middle_sums",
         [sds((6, TX, TY)), sds((5, TX, TY), BF), TOKEN],
-        7,
+        6,
         [pltpu.VMEM((4, TX + 16, TY), F32), pltpu.VMEM((TX + 16, TY), F32)],
         cost=micros(1),
-    )(ready, u, v, b, bl, s, inner)
+    )(ready, u, v, b, flat, inner)
     mid_in = shifted(mid_send, "grp", 1)
     seam = call(
         with_total(seam_sums, total),
@@ -706,34 +766,42 @@
         6,
         [pltpu.VMEM((13, TX, 384), F32), pltpu.VMEM((4, TX + 16, 384), F32), pltpu.VMEM((TX + 16, 384), F32)],
         cost=micros(1),
-    )(u, v, b, bl, hal, inner)
+    )(u, v, b, flat, hal, inner)
     rim, rim_send, two, edge = call(
         with_total(rim_sums, total),
         "rim_sums",
         [sds((6, 48, LANES)), sds((9, 16, LANES), BF), sds((2, ROWS, LANES)), sds((8, 64, LANES))],
-        10,
+        9,
         [pltpu.VMEM((13, 32, LANES), F32), pltpu.VMEM((4, 48, LANES), F32), pltpu.VMEM((48, LANES), F32)],
         cost=micros(2),
-    )(summed, u, v, b, bl, s, hal, low, high, seam)
+    )(summed, u, v, b, flat, hal, low, high, seam)
     rim_in = shifted(rim_send, "grp", 1)
     force, force_send = call(
         with_total(edges, total),
         "edges",
-        [sds((8, FORCED, LANES)), sds((2, 48, LANES), BF)],
+        [sds((8, FORCED, LANES)), sds((5, 16, LANES), BF)],
         8,
         [pltpu.VMEM((52 * 32, LANES), BF), pltpu.VMEM((52 * 32, LANES), BF), pltpu.VMEM((55 * 32, LANES), BF)],
         cost=micros(6),
         aliases={7: 0},
     )(edge, two, *weights, inner)
     force_in = shifted(force_send, "grp", 1)
-    own = call(
+    own, owned = call(
         with_total(own_part, total),
         "own_part",
-        sds((8, TX, TY)),
-        10,
+        [sds((8, TX, TY)), TOKEN],
+        8,
         [pltpu.VMEM((4, 96, LANES), F32), pltpu.VMEM((96, LANES), F32)],
         cost=micros(2),
-    )(u, v, b, bl, hal, low, high, force, mid_in, rim_in)
+    )(u, v, b, flat, hal, low, high, force)
+    start = call(
+        with_total(prepare, total),
+        "prepare",
+        [sds((ROWS, LANES))] * 6 + [sds((2, TX, TY))],
+        8,
+        [pltpu.VMEM((TX + 16, LANES), F32)],
+        cost=micros(1),
+    )(owned, two, mid, seam, rim, mid_in, rim_in, force)
     plane = pltpu.VMEM((ROWS, LANES), F32)
     tall = pltpu.VMEM((ROWS + 16, LANES), F32)
     return tuple(
@@ -741,10 +809,10 @@
             with_total(substeps, total),
             "substeps",
             [sds((4, TX, TY)), sds((4, TX, TY)), sds((TX, TY))],
-            9,
-            [tall, tall] + [plane] * 9,
+            10,
+            [tall, tall] + [plane] * 5,
             cost=micros(5),
-        )(two, mid, seam, rim, mid_in, rim_in, force, force_in, own)
+        )(two, *start, force_in, own)
     )
 
 

time: 41.8 us -> 40.4 us (0.967); the launches traced: 41 us -> 40.3 us
  local copies, waits for them, and re-layouts: 1.84 us -> 0.98 us
  Pallas kernels: 21.6 us -> 22.2 us
  waiting for transfers between devices: 4.8 us -> 4.32 us
    unnamed x22 -> x20, local copies, waits for them, and re-layouts: 1.84 us -> 0.98 us
    pallas_call x4 -> x5, Pallas kernels: 8.51 us -> 9.1 us  [the longest x1 4.61 us: local(): call(with_total(edges, total), 'edges', [sds((8, FORCED, LANES)), sds((5,...]
    ppermute x7, waiting for transfers between devices: 4.8 us -> 4.32 us  [shifted(): return lax.ppermute(x, axis, [(i, (i + by) % size) for i in range(size)])]
  transfers between devices with their start and end apart: 7 -> 7, of which waited for: 4 -> 3; matrix products, arithmetic and copies ran while one was open for 0% -> 0% of each run, Pallas kernels for 35% -> 37%
where the time goes in v5:
time: 40.4 us; the launch traced here: 40.3 us
  Pallas kernels  22.2 us (55%)
  starting transfers between devices  12 us (30%)
  waiting for transfers between devices  4.32 us (11%)
  local copies, waits for them, and re-layouts  0.98 us (2%)
  between operations  0.81 us (2%)
    ppermute x7, starting transfers between devices, shifted(): return lax.ppermute(x, axis, [(i, (i + by) % size) for i in range(size)])  12 us
    pallas_call x1, Pallas kernels, local(): call(with_total(interior, total), 'interior', [sds((8, FORCED, LANES)), T...  5.55 us
    pallas_call x1, Pallas kernels, local(): call(with_total(edges, total), 'edges', [sds((8, FORCED, LANES)), sds((5,...  4.61 us
    ppermute x7, waiting for transfers between devices, shifted(): return lax.ppermute(x, axis, [(i, (i + by) % size) for i in range(size)])  4.32 us
    pallas_call x1, Pallas kernels, local(): call(with_total(substeps, total), 'substeps', [sds((4, TX, TY)), sds((4,...  4.06 us
    pallas_call x1, Pallas kernels, local(): call(pack_lat, 'pack_lat', [half, half, sds((2, TX, TY))] + made, 10, [wi...  2.9 us
    pallas_call x1, Pallas kernels, local(): call(with_total(middle_sums, total), 'middle_sums', [sds((6, TX, TY)), sd...  1.18 us
    pallas_call x1, Pallas kernels, local(): call(with_total(rim_sums, total), 'rim_sums', [sds((6, 48, LANES)), sds((...  1.16 us
  transfers between devices with their start and end apart: 7, of which 3 were waited for; matrix products, arithmetic and copies ran while one was open for 0% of the time, Pallas kernels for 37%

profile of v5, /device:TPU:0, one launch (start us, length us, event | category | flops | bytes accessed | tf_op | source)
XLA Modules:
  0.0 40.3 jit_solution(17337778046124947097)
XLA Ops:
  0.6 0.0 copy-start.1
  0.6 0.0 copy-start
  0.7 0.0 copy-start.2
  0.7 2.9 %pack_lat.1 = (bf16[2,64,128]{2,1,0:T(8,128)(2,1)}, bf16[2,64,128]{2,1,0:T(8,128)(2,1)}, f32[2,64,512]{2,1,0:T(8,128)}, bf16[192,256]{1,0:T(8,128)(2,1)}, bf16[5...) custom-call(f32[4,64,512]{2,1,0:T(8,128)} %refs_0_.7, ...), custom_call_target="tpu_custom_call" | custom-call | tf_op jit(solution)/shard_map/pack_lat/pallas_call | solution.py:702
  3.6 2.1 %collective-permute-start = (bf16[2,64,128]{2,1,0:T(8,128)(2,1)}, bf16[2,64,128]{2,1,0:T(8,128)(2,1)S(1)}, u32[]{:S(2)}, u32[]{:S(2)}) collective-permute-start(bf16[2,64,128]{2,1,0:T(8,128)(2,1)} %get-tuple-element.35), channel_id=1, source_target_pairs={{0,2},{2,4},{4,6},{6,0},{1,3},{3,5},{5,7},{7,1},{8,10},{10,12},{12... | collective-permute-start | bytes 98312 | tf_op jit(solution)/shard_map/ppermute | solution.py:695
  5.6 2.2 %collective-permute-start.1 = (bf16[2,64,128]{2,1,0:T(8,128)(2,1)}, bf16[2,64,128]{2,1,0:T(8,128)(2,1)S(1)}, u32[]{:S(2)}, u32[]{:S(2)}) collective-permute-start(bf16[2,64,128]{2,1,0:T(8,128)(2,1)} %get-tuple-element.36), channel_id=1, source_target_pairs={{0,6},{2,0},{4,2},{6,4},{1,7},{3,1},{5,3},{7,5},{8,14},{10,8},{12,... | collective-permute-start | bytes 98312 | tf_op jit(solution)/shard_map/ppermute | solution.py:695
  7.8 0.9 %copy-done.3 = f32[2,64,512]{2,1,0:T(8,128)S(1)} copy-done((f32[2,64,512]{2,1,0:T(8,128)S(1)}, f32[2,64,512]{2,1,0:T(8,128)}, u32[]{:S(2)}) %copy-start.3) | copy-done | bytes 262168
  8.8 0.0 copy-start.9
  8.8 1.0 %collective-permute-done.refs_1_ = bf16[2,64,128]{2,1,0:T(8,128)(2,1)S(1)} collective-permute-done((bf16[2,64,128]{2,1,0:T(8,128)(2,1)}, bf16[2,64,128]{2,1,0:T(8,128)(2,1)S(1)}, u32[]{:S(2)}, u32[]{:S(2)}) %collective-permute-start) | collective-permute-done | bytes 32800 | tf_op jit(solution)/shard_map/ppermute | solution.py:695
  9.9 0.0 collective-permute-done.1.refs_2_
  9.9 0.0 copy-done.1
  9.9 0.0 copy-done
  9.9 0.0 copy-done.2
  9.9 0.3 pack_lon.1
  10.2 0.1 collective-permute-start.2
  10.3 5.3 %collective-permute-start.3 = (bf16[16,16,512]{2,1,0:T(8,128)(2,1)S(1)}, bf16[16,16,512]{2,1,0:T(8,128)(2,1)S(1)}, u32[]{:S(2)}, u32[]{:S(2)}) collective-permute-start(bf16[16,16,512]{2,1,0:T(8,128)(2,1)S(1)} %get-tuple-element.47), channel_id=1, source_target_pairs={{0,120},{8,0},{16,8},{24,16},{32,24},{40,32},{48,40},{56,48},{64,5... | collective-permute-start | bytes 786440 | tf_op jit(solution)/shard_map/ppermute | solution.py:695
  15.7 5.5 %interior.1 = (f32[8,104,640]{2,1,0:T(8,128)S(1)}, f32[8,128]{1,0:T(8,128)S(1)}) custom-call(f32[4,64,512]{2,1,0:T(8,128)S(1)} %copy-done, f32[4,64,512]{2,1,0:T(8,128)S(1)} %copy-done.1, f32[2,64,512]{2,1,0:T(8,128)S(1)} %copy-done.3, f32[14,64,128]{2,1,0:T(8,128)S(1)} %get-tuple-element.37.refs_3_.refs_4_.refs_5_, bf16[192,256]{1,0:T(8,128)(2,1)S(1)} %copy-done.7, ...), custom_call_target="tpu_custom_call" | custom-call | flops 7000000 | bytes 21000000 | tf_op jit(solution)/shard_map/interior/pallas_call | solution.py:740
  21.2 1.2 %middle_sums.1 = (f32[6,64,512]{2,1,0:T(8,128)S(1)}, bf16[5,64,512]{2,1,0:T(8,128)(2,1)S(1)}, f32[8,128]{1,0:T(8,128)S(1)}) custom-call(f32[8,128]{1,0:T(8,128)S(1)} %get-tuple-element.43.refs_0_, f32[4,64,512]{2,1,0:T(8,128)S(1)} %copy-done, f32[4,64,512]{2,1,0:T(8,128)S(1)} %copy-done.1, f32[4,64,512]{2,1,0:T(8,128)S(1)} %copy-done.2, ...), custom_call_target="tpu_custom_call" | custom-call | flops 1000000 | bytes 3000000 | tf_op jit(solution)/shard_map/middle_sums/pallas_call | solution.py:753
  22.4 0.1 collective-permute-start.4
  22.5 0.8 %seam_sums.1.refs_8_.refs_3_ = f32[7,64,384]{2,1,0:T(8,128)S(1)} custom-call(f32[4,64,512]{2,1,0:T(8,128)S(1)} %copy-done, f32[4,64,512]{2,1,0:T(8,128)S(1)} %copy-done.1, f32[4,64,512]{2,1,0:T(8,128)S(1)} %copy-done.2, f32[2,64,512]{2,1,0:T(8,128)S(1)} %copy-done.3, f32[14,64,128]{2,1,0:T(8,128)S(1)} %get-tuple-element.37.refs_3_.refs_4_.refs_5_, ...), custom_call_target="tpu_custom_call" | custom-call | flops 1000000 | bytes 3000000 | tf_op jit(solution)/shard_map/seam_sums/pallas_call | solution.py:762
  23.3 0.0 collective-permute-done.2.refs_6_.refs_5_
  23.4 0.0 collective-permute-done.3.refs_7_.refs_6_
  23.4 1.2 %rim_sums.1 = (f32[6,48,640]{2,1,0:T(8,128)S(1)}, bf16[9,16,640]{2,1,0:T(8,128)(2,1)S(1)}, f32[2,96,640]{2,1,0:T(8,128)S(1)}, f32[8,64,640]{2,1,0:T(8,128)S(1)}) custom-call(f32[8,128]{1,0:T(8,128)S(1)} %get-tuple-element.45.refs_0_, f32[4,64,512]{2,1,0:T(8,128)S(1)} %copy-done, f32[4,64,512]{2,1,0:T(8,128)S(1)} %copy-done.1, f32[4,64,512]{2,1,0:T(8,128)S(1)} %copy-done.2, ...), custom_call_target="tpu_custom_call" | custom-call | flops 2000000 | bytes 6000000 | tf_op jit(solution)/shard_map/rim_sums/pallas_call | solution.py:770
  24.5 2.1 %collective-permute-start.5 = (bf16[9,16,640]{2,1,0:T(8,128)(2,1)S(1)}, bf16[9,16,640]{2,1,0:T(8,128)(2,1)S(1)}, u32[]{:S(2)}, u32[]{:S(2)}) collective-permute-start(bf16[9,16,640]{2,1,0:T(8,128)(2,1)S(1)} %get-tuple-element.55), channel_id=1, source_target_pairs={{0,1},{1,0},{2,3},{3,2},{4,5},{5,4},{6,7},{7,6},{8,9},{9,8},{10,11... | collective-permute-start | bytes 552968 | tf_op jit(solution)/shard_map/ppermute | solution.py:695
  26.6 4.6 %edges.1 = (f32[8,104,640]{2,1,0:T(8,128)S(1)}, bf16[5,16,640]{2,1,0:T(8,128)(2,1)S(1)}) custom-call(f32[8,64,640]{2,1,0:T(8,128)S(1)} %get-tuple-element.49.refs_0_, f32[2,96,640]{2,1,0:T(8,128)S(1)} %get-tuple-element.48.refs_1_.refs_0_, bf16[192,256]{1,0:T(8,128)(2,1)S(1)} %copy-done.7, ...), custom_call_target="tpu_custom_call", output_to_operand_aliasing={{0}: (7, {})} | custom-call | flops 6000000 | bytes 18000000 | tf_op jit(solution)/shard_map/edges/pallas_call | solution.py:779
  31.2 0.1 collective-permute-start.6
  31.3 1.0 %own_part.1 = (f32[8,64,512]{2,1,0:T(8,128)S(1)}, f32[8,128]{1,0:T(8,128)S(1)}) custom-call(f32[4,64,512]{2,1,0:T(8,128)S(1)} %copy-done, f32[4,64,512]{2,1,0:T(8,128)S(1)} %copy-done.1, f32[4,64,512]{2,1,0:T(8,128)S(1)} %copy-done.2, f32[2,64,512]{2,1,0:T(8,128)S(1)} %copy-done.4, f32[14,64,128]{2,1,0:T(8,128)S(1)} %get-tuple-element.37.refs_3_.refs_4_.refs_5_, ...), custom_call_target="tpu_custom_call" | custom-call | flops 2000000 | bytes 6000000 | tf_op jit(solution)/shard_map/own_part/pallas_call | solution.py:789
  32.4 0.0 collective-permute-done.4.refs_5_
  32.4 2.7 %collective-permute-done.5.refs_6_ = bf16[9,16,640]{2,1,0:T(8,128)(2,1)S(1)} collective-permute-done((bf16[9,16,640]{2,1,0:T(8,128)(2,1)S(1)}, bf16[9,16,640]{2,1,0:T(8,128)(2,1)S(1)}, u32[]{:S(2)}, u32[]{:S(2)}) %collective-permute-start.5) | collective-permute-done | bytes 184352 | tf_op jit(solution)/shard_map/ppermute | solution.py:695
  35.1 0.5 %prepare.1 = (f32[96,640]{1,0:T(8,128)S(1)}, f32[96,640]{1,0:T(8,128)S(1)}, f32[96,640]{1,0:T(8,128)S(1)}, f32[96,640]{1,0:T(8,128)S(1)}, f32[96,640]{1,0:T(8,12...) custom-call(f32[8,128]{1,0:T(8,128)S(1)} %get-tuple-element.51.refs_0_, ...), custom_call_target="tpu_custom_call" | custom-call | flops 1000000 | bytes 3000000 | tf_op jit(solution)/shard_map/prepare/pallas_call | solution.py:797
  35.7 0.6 %collective-permute-done.6.refs_8_ = bf16[5,16,640]{2,1,0:T(8,128)(2,1)S(1)} collective-permute-done((bf16[5,16,640]{2,1,0:T(8,128)(2,1)S(1)}, bf16[5,16,640]{2,1,0:T(8,128)(2,1)S(1)}, u32[]{:S(2)}, u32[]{:S(2)}) %collective-permute-start.6) | collective-permute-done | bytes 102432 | tf_op jit(solution)/shard_map/ppermute | solution.py:695
  36.2 4.1 %substeps.1 = (f32[4,64,512]{2,1,0:T(8,128)}, f32[4,64,512]{2,1,0:T(8,128)}, f32[64,512]{1,0:T(8,128)}) custom-call(f32[2,96,640]{2,1,0:T(8,128)S(1)} %get-tuple-element.48.refs_1_.refs_0_, f32[96,640]{1,0:T(8,128)S(1)} %get-tuple-element.56.refs_1_, f32[96,640]{1,0:T(8,128)S(1)} %get-tuple-element.57.refs_2_, f32[96,640]{1,0:T(8,128)S(1)} %get-tuple-element.58.refs_3_, ...), custom_call_target="tpu_custom_call" | custom-call | flops 5000000 | bytes 15000000 | tf_op jit(solution)/shard_map/substeps/pallas_call | solution.py:808
  (13 shorter events, 0.0 us)
Async XLA Ops:
  0.6 9.2 %copy-start.1 = (f32[4,64,512]{2,1,0:T(8,128)S(1)}, f32[4,64,512]{2,1,0:T(8,128)}, u32[]{:S(2)}) copy-start(f32[4,64,512]{2,1,0:T(8,128)} %refs_1_.11) | copy-start | bytes 1572868
  0.6 9.2 %copy-start = (f32[4,64,512]{2,1,0:T(8,128)S(1)}, f32[4,64,512]{2,1,0:T(8,128)}, u32[]{:S(2)}) copy-start(f32[4,64,512]{2,1,0:T(8,128)} %refs_0_.7) | copy-start | bytes 1572868
  0.7 9.2 %copy-start.2 = (f32[4,64,512]{2,1,0:T(8,128)S(1)}, f32[4,64,512]{2,1,0:T(8,128)}, u32[]{:S(2)}) copy-start(f32[4,64,512]{2,1,0:T(8,128)} %refs_2_.9) | copy-start | bytes 1572868
  3.6 6.3 %collective-permute-start = (bf16[2,64,128]{2,1,0:T(8,128)(2,1)}, bf16[2,64,128]{2,1,0:T(8,128)(2,1)S(1)}, u32[]{:S(2)}, u32[]{:S(2)}) collective-permute-start(bf16[2,64,128]{2,1,0:T(8,128)(2,1)} %get-tuple-element.35), channel_id=1, source_target_pairs={{0,2},{2,4},{4,6},{6,0},{1,3},{3,5},{5,7},{7,1},{8,10},{10,12},{12... | collective-permute-start | bytes 98312 | tf_op jit(solution)/shard_map/ppermute | solution.py:695
  5.6 4.2 %collective-permute-start.1 = (bf16[2,64,128]{2,1,0:T(8,128)(2,1)}, bf16[2,64,128]{2,1,0:T(8,128)(2,1)S(1)}, u32[]{:S(2)}, u32[]{:S(2)}) collective-permute-start(bf16[2,64,128]{2,1,0:T(8,128)(2,1)} %get-tuple-element.36), channel_id=1, source_target_pairs={{0,6},{2,0},{4,2},{6,4},{1,7},{3,1},{5,3},{7,5},{8,14},{10,8},{12,... | collective-permute-start | bytes 98312 | tf_op jit(solution)/shard_map/ppermute | solution.py:695
  7.8 0.9 %copy-start.3 = (f32[2,64,512]{2,1,0:T(8,128)S(1)}, f32[2,64,512]{2,1,0:T(8,128)}, u32[]{:S(2)}) copy-start(f32[2,64,512]{2,1,0:T(8,128)} %get-tuple-element.34.refs_0_.refs_6_.refs_2_.refs_4_.refs_3_) | copy-start | bytes 786436
  8.8 6.9 %copy-start.5 = (bf16[576,256]{1,0:T(8,128)(2,1)S(1)}, bf16[576,256]{1,0:T(8,128)(2,1)}, u32[]{:S(2)}) copy-start(bf16[576,256]{1,0:T(8,128)(2,1)} %get-tuple-element.39.refs_5_.refs_3_) | copy-start | bytes 884740
  8.8 6.9 %copy-start.6 = (bf16[192,320]{1,0:T(8,128)(2,1)S(1)}, bf16[192,320]{1,0:T(8,128)(2,1)}, u32[]{:S(2)}) copy-start(bf16[192,320]{1,0:T(8,128)(2,1)} %get-tuple-element.40.refs_6_.refs_4_) | copy-start | bytes 368644
  8.8 6.9 %copy-start.7 = (bf16[192,256]{1,0:T(8,128)(2,1)S(1)}, bf16[192,256]{1,0:T(8,128)(2,1)}, u32[]{:S(2)}) copy-start(bf16[192,256]{1,0:T(8,128)(2,1)} %get-tuple-element.38.refs_4_.refs_2_) | copy-start | bytes 294916
  8.8 6.9 %copy-start.8 = (f32[192,128]{1,0:T(8,128)S(1)}, f32[192,128]{1,0:T(8,128)}, u32[]{:S(2)}) copy-start(f32[192,128]{1,0:T(8,128)} %get-tuple-element.41.refs_7_.refs_5_) | copy-start | bytes 294916
  8.8 6.9 %copy-start.9 = (f32[192,128]{1,0:T(8,128)S(1)}, f32[192,128]{1,0:T(8,128)}, u32[]{:S(2)}) copy-start(f32[192,128]{1,0:T(8,128)} %get-tuple-element.42.refs_8_.refs_6_) | copy-start | bytes 294916
  10.2 13.1 %collective-permute-start.2 = (bf16[16,16,512]{2,1,0:T(8,128)(2,1)S(1)}, bf16[16,16,512]{2,1,0:T(8,128)(2,1)S(1)}, u32[]{:S(2)}, u32[]{:S(2)}) collective-permute-start(bf16[16,16,512]{2,1,0:T(8,128)(2,1)S(1)} %get-tuple-element.46), channel_id=1, source_target_pairs={{0,8},{8,16},{16,24},{24,32},{32,40},{40,48},{48,56},{56,64},{64,7... | collective-permute-start | bytes 786440 | tf_op jit(solution)/shard_map/ppermute | solution.py:695
  10.3 13.1 %collective-permute-start.3 = (bf16[16,16,512]{2,1,0:T(8,128)(2,1)S(1)}, bf16[16,16,512]{2,1,0:T(8,128)(2,1)S(1)}, u32[]{:S(2)}, u32[]{:S(2)}) collective-permute-start(bf16[16,16,512]{2,1,0:T(8,128)(2,1)S(1)} %get-tuple-element.47), channel_id=1, source_target_pairs={{0,120},{8,0},{16,8},{24,16},{32,24},{40,32},{48,40},{56,48},{64,5... | collective-permute-start | bytes 786440 | tf_op jit(solution)/shard_map/ppermute | solution.py:695
  22.4 10.0 %collective-permute-start.4 = (bf16[5,64,512]{2,1,0:T(8,128)(2,1)S(1)}, bf16[5,64,512]{2,1,0:T(8,128)(2,1)S(1)}, u32[]{:S(2)}, u32[]{:S(2)}) collective-permute-start(bf16[5,64,512]{2,1,0:T(8,128)(2,1)S(1)} %get-tuple-element.54), channel_id=1, source_target_pairs={{0,1},{1,0},{2,3},{3,2},{4,5},{5,4},{6,7},{7,6},{8,9},{9,8},{10,11... | collective-permute-start | bytes 983048 | tf_op jit(solution)/shard_map/ppermute | solution.py:695
  24.5 10.6 %collective-permute-start.5 = (bf16[9,16,640]{2,1,0:T(8,128)(2,1)S(1)}, bf16[9,16,640]{2,1,0:T(8,128)(2,1)S(1)}, u32[]{:S(2)}, u32[]{:S(2)}) collective-permute-start(bf16[9,16,640]{2,1,0:T(8,128)(2,1)S(1)} %get-tuple-element.55), channel_id=1, source_target_pairs={{0,1},{1,0},{2,3},{3,2},{4,5},{5,4},{6,7},{7,6},{8,9},{9,8},{10,11... | collective-permute-start | bytes 552968 | tf_op jit(solution)/shard_map/ppermute | solution.py:695
  26.6 4.7 %copy-start.4 = (f32[2,64,512]{2,1,0:T(8,128)S(1)}, f32[2,64,512]{2,1,0:T(8,128)}, u32[]{:S(2)}) copy-start(f32[2,64,512]{2,1,0:T(8,128)} %get-tuple-element.34.refs_0_.refs_6_.refs_2_.refs_4_.refs_3_) | copy-start | bytes 786436
  31.2 5.0 %collective-permute-start.6 = (bf16[5,16,640]{2,1,0:T(8,128)(2,1)S(1)}, bf16[5,16,640]{2,1,0:T(8,128)(2,1)S(1)}, u32[]{:S(2)}, u32[]{:S(2)}) collective-permute-start(bf16[5,16,640]{2,1,0:T(8,128)(2,1)S(1)} %get-tuple-element.63), channel_id=1, source_target_pairs={{0,1},{1,0},{2,3},{3,2},{4,5},{5,4},{6,7},{7,6},{8,9},{9,8},{10,11... | collective-permute-start | bytes 307208 | tf_op jit(solution)/shard_map/ppermute | solution.py:695

commit v6 on v5

--- a/solution.py
+++ b/solution.py
@@ -647,8 +647,8 @@
             lv[r + 8 : r + 16, :] = inside * (lv[r + 8 : r + 16, :] - (0.5 * sub_dt) * (dx + dy))
         return carry
 
-    lax.fori_loop(0, NSUB // 2, lambda _, carry: step(0, carry), 0)
-    lax.fori_loop(0, NSUB // 2, lambda _, carry: step(8, carry), 0)
+    lax.fori_loop(0, NSUB // 2, lambda _, carry: step(0, carry), 0, unroll=4)
+    lax.fori_loop(0, NSUB // 2, lambda _, carry: step(8, carry), 0, unroll=4)
     base = 4 * sc[0]
     for q in range(0, TX, 8):
         rr, at = slice(q + HALO, q + HALO + 8), slice(q, q + 8)

time: 40.4 us -> 40.1 us (level)
  no operation moved by 1% of the time
where the time goes in v6:
time: 40.1 us; the launch traced here: 39.9 us
  Pallas kernels  21.8 us (54%)
  starting transfers between devices  12 us (30%)
  waiting for transfers between devices  4.32 us (11%)
  local copies, waits for them, and re-layouts  0.98 us (2%)
  between operations  0.81 us (2%)
    ppermute x7, starting transfers between devices, shifted(): return lax.ppermute(x, axis, [(i, (i + by) % size) for i in range(size)])  12 us
    pallas_call x1, Pallas kernels, local(): call(with_total(interior, total), 'interior', [sds((8, FORCED, LANES)), T...  5.55 us
    pallas_call x1, Pallas kernels, local(): call(with_total(edges, total), 'edges', [sds((8, FORCED, LANES)), sds((5,...  4.61 us
    ppermute x7, waiting for transfers between devices, shifted(): return lax.ppermute(x, axis, [(i, (i + by) % size) for i in range(size)])  4.32 us
    pallas_call x1, Pallas kernels, local(): call(with_total(substeps, total), 'substeps', [sds((4, TX, TY)), sds((4,...  3.68 us
    pallas_call x1, Pallas kernels, local(): call(pack_lat, 'pack_lat', [half, half, sds((2, TX, TY))] + made, 10, [wi...  2.9 us
    pallas_call x1, Pallas kernels, local(): call(with_total(middle_sums, total), 'middle_sums', [sds((6, TX, TY)), sd...  1.18 us
    pallas_call x1, Pallas kernels, local(): call(with_total(rim_sums, total), 'rim_sums', [sds((6, 48, LANES)), sds((...  1.16 us
  transfers between devices with their start and end apart: 7, of which 3 were waited for; matrix products, arithmetic and copies ran while one was open for 0% of the time, Pallas kernels for 37%

profile of v6, /device:TPU:0, one launch (start us, length us, event | category | flops | bytes accessed | tf_op | source)
XLA Modules:
  0.0 39.9 jit_solution(6369173631153837444)
XLA Ops:
  0.6 0.0 copy-start.1
  0.6 0.0 copy-start
  0.7 0.0 copy-start.2
  0.7 2.9 %pack_lat.1 = (bf16[2,64,128]{2,1,0:T(8,128)(2,1)}, bf16[2,64,128]{2,1,0:T(8,128)(2,1)}, f32[2,64,512]{2,1,0:T(8,128)}, bf16[192,256]{1,0:T(8,128)(2,1)}, bf16[5...) custom-call(f32[4,64,512]{2,1,0:T(8,128)} %refs_0_.7, ...), custom_call_target="tpu_custom_call" | custom-call | tf_op jit(solution)/shard_map/pack_lat/pallas_call | solution.py:702
  3.6 2.1 %collective-permute-start = (bf16[2,64,128]{2,1,0:T(8,128)(2,1)}, bf16[2,64,128]{2,1,0:T(8,128)(2,1)S(1)}, u32[]{:S(2)}, u32[]{:S(2)}) collective-permute-start(bf16[2,64,128]{2,1,0:T(8,128)(2,1)} %get-tuple-element.35), channel_id=1, source_target_pairs={{0,2},{2,4},{4,6},{6,0},{1,3},{3,5},{5,7},{7,1},{8,10},{10,12},{12... | collective-permute-start | bytes 98312 | tf_op jit(solution)/shard_map/ppermute | solution.py:695
  5.6 2.2 %collective-permute-start.1 = (bf16[2,64,128]{2,1,0:T(8,128)(2,1)}, bf16[2,64,128]{2,1,0:T(8,128)(2,1)S(1)}, u32[]{:S(2)}, u32[]{:S(2)}) collective-permute-start(bf16[2,64,128]{2,1,0:T(8,128)(2,1)} %get-tuple-element.36), channel_id=1, source_target_pairs={{0,6},{2,0},{4,2},{6,4},{1,7},{3,1},{5,3},{7,5},{8,14},{10,8},{12,... | collective-permute-start | bytes 98312 | tf_op jit(solution)/shard_map/ppermute | solution.py:695
  7.8 0.9 %copy-done.3 = f32[2,64,512]{2,1,0:T(8,128)S(1)} copy-done((f32[2,64,512]{2,1,0:T(8,128)S(1)}, f32[2,64,512]{2,1,0:T(8,128)}, u32[]{:S(2)}) %copy-start.3) | copy-done | bytes 262168
  8.8 0.0 copy-start.9
  8.8 1.0 %collective-permute-done.refs_1_ = bf16[2,64,128]{2,1,0:T(8,128)(2,1)S(1)} collective-permute-done((bf16[2,64,128]{2,1,0:T(8,128)(2,1)}, bf16[2,64,128]{2,1,0:T(8,128)(2,1)S(1)}, u32[]{:S(2)}, u32[]{:S(2)}) %collective-permute-start) | collective-permute-done | bytes 32800 | tf_op jit(solution)/shard_map/ppermute | solution.py:695
  9.9 0.0 collective-permute-done.1.refs_2_
  9.9 0.0 copy-done
  9.9 0.3 pack_lon.1
  10.2 0.1 collective-permute-start.2
  10.3 5.3 %collective-permute-start.3 = (bf16[16,16,512]{2,1,0:T(8,128)(2,1)S(1)}, bf16[16,16,512]{2,1,0:T(8,128)(2,1)S(1)}, u32[]{:S(2)}, u32[]{:S(2)}) collective-permute-start(bf16[16,16,512]{2,1,0:T(8,128)(2,1)S(1)} %get-tuple-element.47), channel_id=1, source_target_pairs={{0,120},{8,0},{16,8},{24,16},{32,24},{40,32},{48,40},{56,48},{64,5... | collective-permute-start | bytes 786440 | tf_op jit(solution)/shard_map/ppermute | solution.py:695
  15.6 0.0 copy-done.6
  15.7 0.0 copy-done.8
  15.7 5.5 %interior.1 = (f32[8,104,640]{2,1,0:T(8,128)S(1)}, f32[8,128]{1,0:T(8,128)S(1)}) custom-call(f32[4,64,512]{2,1,0:T(8,128)S(1)} %copy-done, f32[4,64,512]{2,1,0:T(8,128)S(1)} %copy-done.1, f32[2,64,512]{2,1,0:T(8,128)S(1)} %copy-done.3, f32[14,64,128]{2,1,0:T(8,128)S(1)} %get-tuple-element.37.refs_3_.refs_4_.refs_5_, bf16[192,256]{1,0:T(8,128)(2,1)S(1)} %copy-done.7, ...), custom_call_target="tpu_custom_call" | custom-call | flops 7000000 | bytes 21000000 | tf_op jit(solution)/shard_map/interior/pallas_call | solution.py:740
  21.2 1.2 %middle_sums.1 = (f32[6,64,512]{2,1,0:T(8,128)S(1)}, bf16[5,64,512]{2,1,0:T(8,128)(2,1)S(1)}, f32[8,128]{1,0:T(8,128)S(1)}) custom-call(f32[8,128]{1,0:T(8,128)S(1)} %get-tuple-element.43.refs_0_, f32[4,64,512]{2,1,0:T(8,128)S(1)} %copy-done, f32[4,64,512]{2,1,0:T(8,128)S(1)} %copy-done.1, f32[4,64,512]{2,1,0:T(8,128)S(1)} %copy-done.2, ...), custom_call_target="tpu_custom_call" | custom-call | flops 1000000 | bytes 3000000 | tf_op jit(solution)/shard_map/middle_sums/pallas_call | solution.py:753
  22.4 0.1 collective-permute-start.4
  22.5 0.8 %seam_sums.1.refs_8_.refs_3_ = f32[7,64,384]{2,1,0:T(8,128)S(1)} custom-call(f32[4,64,512]{2,1,0:T(8,128)S(1)} %copy-done, f32[4,64,512]{2,1,0:T(8,128)S(1)} %copy-done.1, f32[4,64,512]{2,1,0:T(8,128)S(1)} %copy-done.2, f32[2,64,512]{2,1,0:T(8,128)S(1)} %copy-done.3, f32[14,64,128]{2,1,0:T(8,128)S(1)} %get-tuple-element.37.refs_3_.refs_4_.refs_5_, ...), custom_call_target="tpu_custom_call" | custom-call | flops 1000000 | bytes 3000000 | tf_op jit(solution)/shard_map/seam_sums/pallas_call | solution.py:762
  23.3 0.0 collective-permute-done.2.refs_6_.refs_5_
  23.4 0.0 collective-permute-done.3.refs_7_.refs_6_
  23.4 1.2 %rim_sums.1 = (f32[6,48,640]{2,1,0:T(8,128)S(1)}, bf16[9,16,640]{2,1,0:T(8,128)(2,1)S(1)}, f32[2,96,640]{2,1,0:T(8,128)S(1)}, f32[8,64,640]{2,1,0:T(8,128)S(1)}) custom-call(f32[8,128]{1,0:T(8,128)S(1)} %get-tuple-element.45.refs_0_, f32[4,64,512]{2,1,0:T(8,128)S(1)} %copy-done, f32[4,64,512]{2,1,0:T(8,128)S(1)} %copy-done.1, f32[4,64,512]{2,1,0:T(8,128)S(1)} %copy-done.2, ...), custom_call_target="tpu_custom_call" | custom-call | flops 2000000 | bytes 6000000 | tf_op jit(solution)/shard_map/rim_sums/pallas_call | solution.py:770
  24.5 2.1 %collective-permute-start.5 = (bf16[9,16,640]{2,1,0:T(8,128)(2,1)S(1)}, bf16[9,16,640]{2,1,0:T(8,128)(2,1)S(1)}, u32[]{:S(2)}, u32[]{:S(2)}) collective-permute-start(bf16[9,16,640]{2,1,0:T(8,128)(2,1)S(1)} %get-tuple-element.55), channel_id=1, source_target_pairs={{0,1},{1,0},{2,3},{3,2},{4,5},{5,4},{6,7},{7,6},{8,9},{9,8},{10,11... | collective-permute-start | bytes 552968 | tf_op jit(solution)/shard_map/ppermute | solution.py:695
  26.6 4.6 %edges.1 = (f32[8,104,640]{2,1,0:T(8,128)S(1)}, bf16[5,16,640]{2,1,0:T(8,128)(2,1)S(1)}) custom-call(f32[8,64,640]{2,1,0:T(8,128)S(1)} %get-tuple-element.49.refs_0_, f32[2,96,640]{2,1,0:T(8,128)S(1)} %get-tuple-element.48.refs_1_.refs_0_, bf16[192,256]{1,0:T(8,128)(2,1)S(1)} %copy-done.7, ...), custom_call_target="tpu_custom_call", output_to_operand_aliasing={{0}: (7, {})} | custom-call | flops 6000000 | bytes 18000000 | tf_op jit(solution)/shard_map/edges/pallas_call | solution.py:779
  31.2 0.1 collective-permute-start.6
  31.3 1.0 %own_part.1 = (f32[8,64,512]{2,1,0:T(8,128)S(1)}, f32[8,128]{1,0:T(8,128)S(1)}) custom-call(f32[4,64,512]{2,1,0:T(8,128)S(1)} %copy-done, f32[4,64,512]{2,1,0:T(8,128)S(1)} %copy-done.1, f32[4,64,512]{2,1,0:T(8,128)S(1)} %copy-done.2, f32[2,64,512]{2,1,0:T(8,128)S(1)} %copy-done.4, f32[14,64,128]{2,1,0:T(8,128)S(1)} %get-tuple-element.37.refs_3_.refs_4_.refs_5_, ...), custom_call_target="tpu_custom_call" | custom-call | flops 2000000 | bytes 6000000 | tf_op jit(solution)/shard_map/own_part/pallas_call | solution.py:789
  32.4 0.0 collective-permute-done.4.refs_5_
  32.4 2.7 %collective-permute-done.5.refs_6_ = bf16[9,16,640]{2,1,0:T(8,128)(2,1)S(1)} collective-permute-done((bf16[9,16,640]{2,1,0:T(8,128)(2,1)S(1)}, bf16[9,16,640]{2,1,0:T(8,128)(2,1)S(1)}, u32[]{:S(2)}, u32[]{:S(2)}) %collective-permute-start.5) | collective-permute-done | bytes 184352 | tf_op jit(solution)/shard_map/ppermute | solution.py:695
  35.1 0.5 %prepare.1 = (f32[96,640]{1,0:T(8,128)S(1)}, f32[96,640]{1,0:T(8,128)S(1)}, f32[96,640]{1,0:T(8,128)S(1)}, f32[96,640]{1,0:T(8,128)S(1)}, f32[96,640]{1,0:T(8,12...) custom-call(f32[8,128]{1,0:T(8,128)S(1)} %get-tuple-element.51.refs_0_, ...), custom_call_target="tpu_custom_call" | custom-call | flops 1000000 | bytes 3000000 | tf_op jit(solution)/shard_map/prepare/pallas_call | solution.py:797
  35.7 0.6 %collective-permute-done.6.refs_8_ = bf16[5,16,640]{2,1,0:T(8,128)(2,1)S(1)} collective-permute-done((bf16[5,16,640]{2,1,0:T(8,128)(2,1)S(1)}, bf16[5,16,640]{2,1,0:T(8,128)(2,1)S(1)}, u32[]{:S(2)}, u32[]{:S(2)}) %collective-permute-start.6) | collective-permute-done | bytes 102432 | tf_op jit(solution)/shard_map/ppermute | solution.py:695
  36.2 3.7 %substeps.1 = (f32[4,64,512]{2,1,0:T(8,128)}, f32[4,64,512]{2,1,0:T(8,128)}, f32[64,512]{1,0:T(8,128)}) custom-call(f32[2,96,640]{2,1,0:T(8,128)S(1)} %get-tuple-element.48.refs_1_.refs_0_, f32[96,640]{1,0:T(8,128)S(1)} %get-tuple-element.56.refs_1_, f32[96,640]{1,0:T(8,128)S(1)} %get-tuple-element.57.refs_2_, f32[96,640]{1,0:T(8,128)S(1)} %get-tuple-element.58.refs_3_, ...), custom_call_target="tpu_custom_call" | custom-call | flops 5000000 | bytes 15000000 | tf_op jit(solution)/shard_map/substeps/pallas_call | solution.py:808
  (13 shorter events, 0.0 us)
Async XLA Ops:
  0.6 9.2 %copy-start.1 = (f32[4,64,512]{2,1,0:T(8,128)S(1)}, f32[4,64,512]{2,1,0:T(8,128)}, u32[]{:S(2)}) copy-start(f32[4,64,512]{2,1,0:T(8,128)} %refs_1_.11) | copy-start | bytes 1572868
  0.6 9.2 %copy-start = (f32[4,64,512]{2,1,0:T(8,128)S(1)}, f32[4,64,512]{2,1,0:T(8,128)}, u32[]{:S(2)}) copy-start(f32[4,64,512]{2,1,0:T(8,128)} %refs_0_.7) | copy-start | bytes 1572868
  0.7 9.2 %copy-start.2 = (f32[4,64,512]{2,1,0:T(8,128)S(1)}, f32[4,64,512]{2,1,0:T(8,128)}, u32[]{:S(2)}) copy-start(f32[4,64,512]{2,1,0:T(8,128)} %refs_2_.9) | copy-start | bytes 1572868
  3.6 6.3 %collective-permute-start = (bf16[2,64,128]{2,1,0:T(8,128)(2,1)}, bf16[2,64,128]{2,1,0:T(8,128)(2,1)S(1)}, u32[]{:S(2)}, u32[]{:S(2)}) collective-permute-start(bf16[2,64,128]{2,1,0:T(8,128)(2,1)} %get-tuple-element.35), channel_id=1, source_target_pairs={{0,2},{2,4},{4,6},{6,0},{1,3},{3,5},{5,7},{7,1},{8,10},{10,12},{12... | collective-permute-start | bytes 98312 | tf_op jit(solution)/shard_map/ppermute | solution.py:695
  5.6 4.2 %collective-permute-start.1 = (bf16[2,64,128]{2,1,0:T(8,128)(2,1)}, bf16[2,64,128]{2,1,0:T(8,128)(2,1)S(1)}, u32[]{:S(2)}, u32[]{:S(2)}) collective-permute-start(bf16[2,64,128]{2,1,0:T(8,128)(2,1)} %get-tuple-element.36), channel_id=1, source_target_pairs={{0,6},{2,0},{4,2},{6,4},{1,7},{3,1},{5,3},{7,5},{8,14},{10,8},{12,... | collective-permute-start | bytes 98312 | tf_op jit(solution)/shard_map/ppermute | solution.py:695
  7.8 0.9 %copy-start.3 = (f32[2,64,512]{2,1,0:T(8,128)S(1)}, f32[2,64,512]{2,1,0:T(8,128)}, u32[]{:S(2)}) copy-start(f32[2,64,512]{2,1,0:T(8,128)} %get-tuple-element.34.refs_0_.refs_6_.refs_2_.refs_4_.refs_3_) | copy-start | bytes 786436
  8.8 6.9 %copy-start.5 = (bf16[576,256]{1,0:T(8,128)(2,1)S(1)}, bf16[576,256]{1,0:T(8,128)(2,1)}, u32[]{:S(2)}) copy-start(bf16[576,256]{1,0:T(8,128)(2,1)} %get-tuple-element.39.refs_5_.refs_3_) | copy-start | bytes 884740
  8.8 6.9 %copy-start.6 = (bf16[192,320]{1,0:T(8,128)(2,1)S(1)}, bf16[192,320]{1,0:T(8,128)(2,1)}, u32[]{:S(2)}) copy-start(bf16[192,320]{1,0:T(8,128)(2,1)} %get-tuple-element.40.refs_6_.refs_4_) | copy-start | bytes 368644
  8.8 6.9 %copy-start.7 = (bf16[192,256]{1,0:T(8,128)(2,1)S(1)}, bf16[192,256]{1,0:T(8,128)(2,1)}, u32[]{:S(2)}) copy-start(bf16[192,256]{1,0:T(8,128)(2,1)} %get-tuple-element.38.refs_4_.refs_2_) | copy-start | bytes 294916
  8.8 6.9 %copy-start.8 = (f32[192,128]{1,0:T(8,128)S(1)}, f32[192,128]{1,0:T(8,128)}, u32[]{:S(2)}) copy-start(f32[192,128]{1,0:T(8,128)} %get-tuple-element.41.refs_7_.refs_5_) | copy-start | bytes 294916
  8.8 6.9 %copy-start.9 = (f32[192,128]{1,0:T(8,128)S(1)}, f32[192,128]{1,0:T(8,128)}, u32[]{:S(2)}) copy-start(f32[192,128]{1,0:T(8,128)} %get-tuple-element.42.refs_8_.refs_6_) | copy-start | bytes 294916
  10.2 13.1 %collective-permute-start.2 = (bf16[16,16,512]{2,1,0:T(8,128)(2,1)S(1)}, bf16[16,16,512]{2,1,0:T(8,128)(2,1)S(1)}, u32[]{:S(2)}, u32[]{:S(2)}) collective-permute-start(bf16[16,16,512]{2,1,0:T(8,128)(2,1)S(1)} %get-tuple-element.46), channel_id=1, source_target_pairs={{0,8},{8,16},{16,24},{24,32},{32,40},{40,48},{48,56},{56,64},{64,7... | collective-permute-start | bytes 786440 | tf_op jit(solution)/shard_map/ppermute | solution.py:695
  10.3 13.1 %collective-permute-start.3 = (bf16[16,16,512]{2,1,0:T(8,128)(2,1)S(1)}, bf16[16,16,512]{2,1,0:T(8,128)(2,1)S(1)}, u32[]{:S(2)}, u32[]{:S(2)}) collective-permute-start(bf16[16,16,512]{2,1,0:T(8,128)(2,1)S(1)} %get-tuple-element.47), channel_id=1, source_target_pairs={{0,120},{8,0},{16,8},{24,16},{32,24},{40,32},{48,40},{56,48},{64,5... | collective-permute-start | bytes 786440 | tf_op jit(solution)/shard_map/ppermute | solution.py:695
  22.4 10.0 %collective-permute-start.4 = (bf16[5,64,512]{2,1,0:T(8,128)(2,1)S(1)}, bf16[5,64,512]{2,1,0:T(8,128)(2,1)S(1)}, u32[]{:S(2)}, u32[]{:S(2)}) collective-permute-start(bf16[5,64,512]{2,1,0:T(8,128)(2,1)S(1)} %get-tuple-element.54), channel_id=1, source_target_pairs={{0,1},{1,0},{2,3},{3,2},{4,5},{5,4},{6,7},{7,6},{8,9},{9,8},{10,11... | collective-permute-start | bytes 983048 | tf_op jit(solution)/shard_map/ppermute | solution.py:695
  24.5 10.6 %collective-permute-start.5 = (bf16[9,16,640]{2,1,0:T(8,128)(2,1)S(1)}, bf16[9,16,640]{2,1,0:T(8,128)(2,1)S(1)}, u32[]{:S(2)}, u32[]{:S(2)}) collective-permute-start(bf16[9,16,640]{2,1,0:T(8,128)(2,1)S(1)} %get-tuple-element.55), channel_id=1, source_target_pairs={{0,1},{1,0},{2,3},{3,2},{4,5},{5,4},{6,7},{7,6},{8,9},{9,8},{10,11... | collective-permute-start | bytes 552968 | tf_op jit(solution)/shard_map/ppermute | solution.py:695
  26.6 4.7 %copy-start.4 = (f32[2,64,512]{2,1,0:T(8,128)S(1)}, f32[2,64,512]{2,1,0:T(8,128)}, u32[]{:S(2)}) copy-start(f32[2,64,512]{2,1,0:T(8,128)} %get-tuple-element.34.refs_0_.refs_6_.refs_2_.refs_4_.refs_3_) | copy-start | bytes 786436
  31.2 5.0 %collective-permute-start.6 = (bf16[5,16,640]{2,1,0:T(8,128)(2,1)S(1)}, bf16[5,16,640]{2,1,0:T(8,128)(2,1)S(1)}, u32[]{:S(2)}, u32[]{:S(2)}) collective-permute-start(bf16[5,16,640]{2,1,0:T(8,128)(2,1)S(1)} %get-tuple-element.63), channel_id=1, source_target_pairs={{0,1},{1,0},{2,3},{3,2},{4,5},{5,4},{6,7},{7,6},{8,9},{9,8},{10,11... | collective-permute-start | bytes 307208 | tf_op jit(solution)/shard_map/ppermute | solution.py:695

commit v7 on v6

--- a/solution.py
+++ b/solution.py
@@ -191,8 +191,7 @@
     eye = lax.broadcasted_iota(jnp.int32, (32, 32), 0) == lax.broadcasted_iota(jnp.int32, (32, 32), 1)
     for src, dst in ((b_in, b1), (b_mid, b2)):
         column = jnp.sum(jnp.where(eye, src[...], 0.0), 1, keepdims=True)
-        for p in range(6):
-            dst[32 * p : 32 * p + 32, :] = jnp.broadcast_to(column, (32, 128))
+        dst[...] = jnp.broadcast_to(column, (32, 128))
 
 
 def load_slots(up, start, count, in0, at):
@@ -205,7 +204,7 @@
 
 def closure(in0, act1, act2, weights, inside, parts, store):
     w1, w2, w3, b1, b2 = weights
-    bias1, bias2 = b1[:, :1], b2[:, :1]
+    bias1, bias2 = (jnp.concatenate([b[:, :1]] * 6, 0) for b in (b1, b2))
 
     def combined(o, m):
         return pltpu.roll(o[:m], 1, 1) + o[m : 2 * m] + pltpu.roll(o[2 * m :], LANES - 1, 1)
@@ -698,7 +697,7 @@
 def local(u, v, b, wet_mask, bl, s, w_in, b_in, w_mid, b_mid, w_out):
     total = TY * lax.axis_size("lat")
     wide, half = pltpu.VMEM((2, 4, TX, 128), F32), sds((2, TX, 128), BF)
-    made = [sds((192, 256), BF), sds((576, 256), BF), sds((192, 320), BF), sds((192, 128)), sds((192, 128))]
+    made = [sds((192, 256), BF), sds((576, 256), BF), sds((192, 320), BF), sds((32, 128)), sds((32, 128))]
     to_down, to_up, flat, *weights = call(
         pack_lat,
         "pack_lat",

time: 40.1 us -> 39.9 us (level)
  no operation moved by 1% of the time
where the time goes in v7:
time: 39.9 us; the launch traced here: 39.7 us
  Pallas kernels  21.6 us (54%)
  starting transfers between devices  12 us (30%)
  waiting for transfers between devices  4.4 us (11%)
  local copies, waits for them, and re-layouts  0.98 us (2%)
  between operations  0.81 us (2%)
    ppermute x7, starting transfers between devices, shifted(): return lax.ppermute(x, axis, [(i, (i + by) % size) for i in range(size)])  12 us
    pallas_call x1, Pallas kernels, local(): call(with_total(interior, total), 'interior', [sds((8, FORCED, LANES)), T...  5.41 us
    pallas_call x1, Pallas kernels, local(): call(with_total(edges, total), 'edges', [sds((8, FORCED, LANES)), sds((5,...  4.54 us
    ppermute x7, waiting for transfers between devices, shifted(): return lax.ppermute(x, axis, [(i, (i + by) % size) for i in range(size)])  4.4 us
    pallas_call x1, Pallas kernels, local(): call(with_total(substeps, total), 'substeps', [sds((4, TX, TY)), sds((4,...  3.68 us
    pallas_call x1, Pallas kernels, local(): call(pack_lat, 'pack_lat', [half, half, sds((2, TX, TY))] + made, 10, [wi...  2.84 us
    pallas_call x1, Pallas kernels, local(): call(with_total(middle_sums, total), 'middle_sums', [sds((6, TX, TY)), sd...  1.18 us
    pallas_call x1, Pallas kernels, local(): call(with_total(rim_sums, total), 'rim_sums', [sds((6, 48, LANES)), sds((...  1.16 us
  transfers between devices with their start and end apart: 7, of which 3 were waited for; matrix products, arithmetic and copies ran while one was open for 0% of the time, Pallas kernels for 37%

profile of v7, /device:TPU:0, one launch (start us, length us, event | category | flops | bytes accessed | tf_op | source)
XLA Modules:
  0.0 39.7 jit_solution(2303173770019701731)
XLA Ops:
  0.6 0.0 copy-start.1
  0.6 0.0 copy-start
  0.7 0.0 copy-start.2
  0.7 2.8 %pack_lat.1 = (bf16[2,64,128]{2,1,0:T(8,128)(2,1)}, bf16[2,64,128]{2,1,0:T(8,128)(2,1)}, f32[2,64,512]{2,1,0:T(8,128)}, bf16[192,256]{1,0:T(8,128)(2,1)}, bf16[5...) custom-call(f32[4,64,512]{2,1,0:T(8,128)} %refs_0_.7, ...), custom_call_target="tpu_custom_call" | custom-call | tf_op jit(solution)/shard_map/pack_lat/pallas_call | solution.py:701
  3.5 2.1 %collective-permute-start = (bf16[2,64,128]{2,1,0:T(8,128)(2,1)}, bf16[2,64,128]{2,1,0:T(8,128)(2,1)S(1)}, u32[]{:S(2)}, u32[]{:S(2)}) collective-permute-start(bf16[2,64,128]{2,1,0:T(8,128)(2,1)} %get-tuple-element.35), channel_id=1, source_target_pairs={{0,2},{2,4},{4,6},{6,0},{1,3},{3,5},{5,7},{7,1},{8,10},{10,12},{12... | collective-permute-start | bytes 98312 | tf_op jit(solution)/shard_map/ppermute | solution.py:694
  5.6 2.2 %collective-permute-start.1 = (bf16[2,64,128]{2,1,0:T(8,128)(2,1)}, bf16[2,64,128]{2,1,0:T(8,128)(2,1)S(1)}, u32[]{:S(2)}, u32[]{:S(2)}) collective-permute-start(bf16[2,64,128]{2,1,0:T(8,128)(2,1)} %get-tuple-element.36), channel_id=1, source_target_pairs={{0,6},{2,0},{4,2},{6,4},{1,7},{3,1},{5,3},{7,5},{8,14},{10,8},{12,... | collective-permute-start | bytes 98312 | tf_op jit(solution)/shard_map/ppermute | solution.py:694
  7.8 0.9 %copy-done.3 = f32[2,64,512]{2,1,0:T(8,128)S(1)} copy-done((f32[2,64,512]{2,1,0:T(8,128)S(1)}, f32[2,64,512]{2,1,0:T(8,128)}, u32[]{:S(2)}) %copy-start.3) | copy-done | bytes 262168
  8.8 1.0 %collective-permute-done.refs_1_ = bf16[2,64,128]{2,1,0:T(8,128)(2,1)S(1)} collective-permute-done((bf16[2,64,128]{2,1,0:T(8,128)(2,1)}, bf16[2,64,128]{2,1,0:T(8,128)(2,1)S(1)}, u32[]{:S(2)}, u32[]{:S(2)}) %collective-permute-start) | collective-permute-done | bytes 32800 | tf_op jit(solution)/shard_map/ppermute | solution.py:694
  9.8 0.0 collective-permute-done.1.refs_2_
  9.8 0.0 copy-done
  9.8 0.0 copy-done.2
  9.8 0.3 pack_lon.1
  10.2 0.1 collective-permute-start.2
  10.2 5.3 %collective-permute-start.3 = (bf16[16,16,512]{2,1,0:T(8,128)(2,1)S(1)}, bf16[16,16,512]{2,1,0:T(8,128)(2,1)S(1)}, u32[]{:S(2)}, u32[]{:S(2)}) collective-permute-start(bf16[16,16,512]{2,1,0:T(8,128)(2,1)S(1)} %get-tuple-element.47), channel_id=1, source_target_pairs={{0,120},{8,0},{16,8},{24,16},{32,24},{40,32},{48,40},{56,48},{64,5... | collective-permute-start | bytes 786440 | tf_op jit(solution)/shard_map/ppermute | solution.py:694
  15.6 0.0 copy-done.8
  15.6 0.0 copy-done.9
  15.6 5.4 %interior.1 = (f32[8,104,640]{2,1,0:T(8,128)S(1)}, f32[8,128]{1,0:T(8,128)S(1)}) custom-call(f32[4,64,512]{2,1,0:T(8,128)S(1)} %copy-done, f32[4,64,512]{2,1,0:T(8,128)S(1)} %copy-done.1, f32[2,64,512]{2,1,0:T(8,128)S(1)} %copy-done.3, f32[14,64,128]{2,1,0:T(8,128)S(1)} %get-tuple-element.37.refs_3_.refs_4_.refs_5_, bf16[192,256]{1,0:T(8,128)(2,1)S(1)} %copy-done.7, ...), custom_call_target="tpu_custom_call" | custom-call | flops 7000000 | bytes 21000000 | tf_op jit(solution)/shard_map/interior/pallas_call | solution.py:739
  21.0 1.2 %middle_sums.1 = (f32[6,64,512]{2,1,0:T(8,128)S(1)}, bf16[5,64,512]{2,1,0:T(8,128)(2,1)S(1)}, f32[8,128]{1,0:T(8,128)S(1)}) custom-call(f32[8,128]{1,0:T(8,128)S(1)} %get-tuple-element.43.refs_0_, f32[4,64,512]{2,1,0:T(8,128)S(1)} %copy-done, f32[4,64,512]{2,1,0:T(8,128)S(1)} %copy-done.1, f32[4,64,512]{2,1,0:T(8,128)S(1)} %copy-done.2, ...), custom_call_target="tpu_custom_call" | custom-call | flops 1000000 | bytes 3000000 | tf_op jit(solution)/shard_map/middle_sums/pallas_call | solution.py:752
  22.2 0.1 collective-permute-start.4
  22.3 0.8 %seam_sums.1.refs_8_.refs_3_ = f32[7,64,384]{2,1,0:T(8,128)S(1)} custom-call(f32[4,64,512]{2,1,0:T(8,128)S(1)} %copy-done, f32[4,64,512]{2,1,0:T(8,128)S(1)} %copy-done.1, f32[4,64,512]{2,1,0:T(8,128)S(1)} %copy-done.2, f32[2,64,512]{2,1,0:T(8,128)S(1)} %copy-done.3, f32[14,64,128]{2,1,0:T(8,128)S(1)} %get-tuple-element.37.refs_3_.refs_4_.refs_5_, ...), custom_call_target="tpu_custom_call" | custom-call | flops 1000000 | bytes 3000000 | tf_op jit(solution)/shard_map/seam_sums/pallas_call | solution.py:761
  23.2 0.0 collective-permute-done.2.refs_6_.refs_5_
  23.2 0.0 collective-permute-done.3.refs_7_.refs_6_
  23.2 1.2 %rim_sums.1 = (f32[6,48,640]{2,1,0:T(8,128)S(1)}, bf16[9,16,640]{2,1,0:T(8,128)(2,1)S(1)}, f32[2,96,640]{2,1,0:T(8,128)S(1)}, f32[8,64,640]{2,1,0:T(8,128)S(1)}) custom-call(f32[8,128]{1,0:T(8,128)S(1)} %get-tuple-element.45.refs_0_, f32[4,64,512]{2,1,0:T(8,128)S(1)} %copy-done, f32[4,64,512]{2,1,0:T(8,128)S(1)} %copy-done.1, f32[4,64,512]{2,1,0:T(8,128)S(1)} %copy-done.2, ...), custom_call_target="tpu_custom_call" | custom-call | flops 2000000 | bytes 6000000 | tf_op jit(solution)/shard_map/rim_sums/pallas_call | solution.py:769
  24.3 2.1 %collective-permute-start.5 = (bf16[9,16,640]{2,1,0:T(8,128)(2,1)S(1)}, bf16[9,16,640]{2,1,0:T(8,128)(2,1)S(1)}, u32[]{:S(2)}, u32[]{:S(2)}) collective-permute-start(bf16[9,16,640]{2,1,0:T(8,128)(2,1)S(1)} %get-tuple-element.55), channel_id=1, source_target_pairs={{0,1},{1,0},{2,3},{3,2},{4,5},{5,4},{6,7},{7,6},{8,9},{9,8},{10,11... | collective-permute-start | bytes 552968 | tf_op jit(solution)/shard_map/ppermute | solution.py:694
  26.4 4.5 %edges.1 = (f32[8,104,640]{2,1,0:T(8,128)S(1)}, bf16[5,16,640]{2,1,0:T(8,128)(2,1)S(1)}) custom-call(f32[8,64,640]{2,1,0:T(8,128)S(1)} %get-tuple-element.49.refs_0_, f32[2,96,640]{2,1,0:T(8,128)S(1)} %get-tuple-element.48.refs_1_.refs_0_, bf16[192,256]{1,0:T(8,128)(2,1)S(1)} %copy-done.7, ...), custom_call_target="tpu_custom_call", output_to_operand_aliasing={{0}: (7, {})} | custom-call | flops 6000000 | bytes 18000000 | tf_op jit(solution)/shard_map/edges/pallas_call | solution.py:778
  31.0 0.1 collective-permute-start.6
  31.1 1.0 %own_part.1 = (f32[8,64,512]{2,1,0:T(8,128)S(1)}, f32[8,128]{1,0:T(8,128)S(1)}) custom-call(f32[4,64,512]{2,1,0:T(8,128)S(1)} %copy-done, f32[4,64,512]{2,1,0:T(8,128)S(1)} %copy-done.1, f32[4,64,512]{2,1,0:T(8,128)S(1)} %copy-done.2, f32[2,64,512]{2,1,0:T(8,128)S(1)} %copy-done.4, f32[14,64,128]{2,1,0:T(8,128)S(1)} %get-tuple-element.37.refs_3_.refs_4_.refs_5_, ...), custom_call_target="tpu_custom_call" | custom-call | flops 2000000 | bytes 6000000 | tf_op jit(solution)/shard_map/own_part/pallas_call | solution.py:788
  32.1 0.0 collective-permute-done.4.refs_5_
  32.1 2.8 %collective-permute-done.5.refs_6_ = bf16[9,16,640]{2,1,0:T(8,128)(2,1)S(1)} collective-permute-done((bf16[9,16,640]{2,1,0:T(8,128)(2,1)S(1)}, bf16[9,16,640]{2,1,0:T(8,128)(2,1)S(1)}, u32[]{:S(2)}, u32[]{:S(2)}) %collective-permute-start.5) | collective-permute-done | bytes 184352 | tf_op jit(solution)/shard_map/ppermute | solution.py:694
  34.9 0.5 %prepare.1 = (f32[96,640]{1,0:T(8,128)S(1)}, f32[96,640]{1,0:T(8,128)S(1)}, f32[96,640]{1,0:T(8,128)S(1)}, f32[96,640]{1,0:T(8,128)S(1)}, f32[96,640]{1,0:T(8,12...) custom-call(f32[8,128]{1,0:T(8,128)S(1)} %get-tuple-element.51.refs_0_, ...), custom_call_target="tpu_custom_call" | custom-call | flops 1000000 | bytes 3000000 | tf_op jit(solution)/shard_map/prepare/pallas_call | solution.py:796
  35.5 0.6 %collective-permute-done.6.refs_8_ = bf16[5,16,640]{2,1,0:T(8,128)(2,1)S(1)} collective-permute-done((bf16[5,16,640]{2,1,0:T(8,128)(2,1)S(1)}, bf16[5,16,640]{2,1,0:T(8,128)(2,1)S(1)}, u32[]{:S(2)}, u32[]{:S(2)}) %collective-permute-start.6) | collective-permute-done | bytes 102432 | tf_op jit(solution)/shard_map/ppermute | solution.py:694
  36.0 3.7 %substeps.1 = (f32[4,64,512]{2,1,0:T(8,128)}, f32[4,64,512]{2,1,0:T(8,128)}, f32[64,512]{1,0:T(8,128)}) custom-call(f32[2,96,640]{2,1,0:T(8,128)S(1)} %get-tuple-element.48.refs_1_.refs_0_, f32[96,640]{1,0:T(8,128)S(1)} %get-tuple-element.56.refs_1_, f32[96,640]{1,0:T(8,128)S(1)} %get-tuple-element.57.refs_2_, f32[96,640]{1,0:T(8,128)S(1)} %get-tuple-element.58.refs_3_, ...), custom_call_target="tpu_custom_call" | custom-call | flops 5000000 | bytes 15000000 | tf_op jit(solution)/shard_map/substeps/pallas_call | solution.py:807
  (13 shorter events, 0.0 us)
Async XLA Ops:
  0.6 9.2 %copy-start.1 = (f32[4,64,512]{2,1,0:T(8,128)S(1)}, f32[4,64,512]{2,1,0:T(8,128)}, u32[]{:S(2)}) copy-start(f32[4,64,512]{2,1,0:T(8,128)} %refs_1_.11) | copy-start | bytes 1572868
  0.6 9.2 %copy-start = (f32[4,64,512]{2,1,0:T(8,128)S(1)}, f32[4,64,512]{2,1,0:T(8,128)}, u32[]{:S(2)}) copy-start(f32[4,64,512]{2,1,0:T(8,128)} %refs_0_.7) | copy-start | bytes 1572868
  0.7 9.2 %copy-start.2 = (f32[4,64,512]{2,1,0:T(8,128)S(1)}, f32[4,64,512]{2,1,0:T(8,128)}, u32[]{:S(2)}) copy-start(f32[4,64,512]{2,1,0:T(8,128)} %refs_2_.9) | copy-start | bytes 1572868
  3.5 6.3 %collective-permute-start = (bf16[2,64,128]{2,1,0:T(8,128)(2,1)}, bf16[2,64,128]{2,1,0:T(8,128)(2,1)S(1)}, u32[]{:S(2)}, u32[]{:S(2)}) collective-permute-start(bf16[2,64,128]{2,1,0:T(8,128)(2,1)} %get-tuple-element.35), channel_id=1, source_target_pairs={{0,2},{2,4},{4,6},{6,0},{1,3},{3,5},{5,7},{7,1},{8,10},{10,12},{12... | collective-permute-start | bytes 98312 | tf_op jit(solution)/shard_map/ppermute | solution.py:694
  5.6 4.2 %collective-permute-start.1 = (bf16[2,64,128]{2,1,0:T(8,128)(2,1)}, bf16[2,64,128]{2,1,0:T(8,128)(2,1)S(1)}, u32[]{:S(2)}, u32[]{:S(2)}) collective-permute-start(bf16[2,64,128]{2,1,0:T(8,128)(2,1)} %get-tuple-element.36), channel_id=1, source_target_pairs={{0,6},{2,0},{4,2},{6,4},{1,7},{3,1},{5,3},{7,5},{8,14},{10,8},{12,... | collective-permute-start | bytes 98312 | tf_op jit(solution)/shard_map/ppermute | solution.py:694
  7.8 0.9 %copy-start.3 = (f32[2,64,512]{2,1,0:T(8,128)S(1)}, f32[2,64,512]{2,1,0:T(8,128)}, u32[]{:S(2)}) copy-start(f32[2,64,512]{2,1,0:T(8,128)} %get-tuple-element.34.refs_0_.refs_6_.refs_2_.refs_4_.refs_3_) | copy-start | bytes 786436
  8.7 6.9 %copy-start.5 = (bf16[576,256]{1,0:T(8,128)(2,1)S(1)}, bf16[576,256]{1,0:T(8,128)(2,1)}, u32[]{:S(2)}) copy-start(bf16[576,256]{1,0:T(8,128)(2,1)} %get-tuple-element.39.refs_5_.refs_3_) | copy-start | bytes 884740
  8.7 6.9 %copy-start.6 = (bf16[192,320]{1,0:T(8,128)(2,1)S(1)}, bf16[192,320]{1,0:T(8,128)(2,1)}, u32[]{:S(2)}) copy-start(bf16[192,320]{1,0:T(8,128)(2,1)} %get-tuple-element.40.refs_6_.refs_4_) | copy-start | bytes 368644
  8.7 6.9 %copy-start.7 = (bf16[192,256]{1,0:T(8,128)(2,1)S(1)}, bf16[192,256]{1,0:T(8,128)(2,1)}, u32[]{:S(2)}) copy-start(bf16[192,256]{1,0:T(8,128)(2,1)} %get-tuple-element.38.refs_4_.refs_2_) | copy-start | bytes 294916
  8.7 6.9 %copy-start.8 = (f32[32,128]{1,0:T(8,128)S(1)}, f32[32,128]{1,0:T(8,128)}, u32[]{:S(2)}) copy-start(f32[32,128]{1,0:T(8,128)} %get-tuple-element.41.refs_7_.refs_5_) | copy-start | bytes 49156
  8.7 6.9 %copy-start.9 = (f32[32,128]{1,0:T(8,128)S(1)}, f32[32,128]{1,0:T(8,128)}, u32[]{:S(2)}) copy-start(f32[32,128]{1,0:T(8,128)} %get-tuple-element.42.refs_8_.refs_6_) | copy-start | bytes 49156
  10.2 13.0 %collective-permute-start.2 = (bf16[16,16,512]{2,1,0:T(8,128)(2,1)S(1)}, bf16[16,16,512]{2,1,0:T(8,128)(2,1)S(1)}, u32[]{:S(2)}, u32[]{:S(2)}) collective-permute-start(bf16[16,16,512]{2,1,0:T(8,128)(2,1)S(1)} %get-tuple-element.46), channel_id=1, source_target_pairs={{0,8},{8,16},{16,24},{24,32},{32,40},{40,48},{48,56},{56,64},{64,7... | collective-permute-start | bytes 786440 | tf_op jit(solution)/shard_map/ppermute | solution.py:694
  10.2 12.9 %collective-permute-start.3 = (bf16[16,16,512]{2,1,0:T(8,128)(2,1)S(1)}, bf16[16,16,512]{2,1,0:T(8,128)(2,1)S(1)}, u32[]{:S(2)}, u32[]{:S(2)}) collective-permute-start(bf16[16,16,512]{2,1,0:T(8,128)(2,1)S(1)} %get-tuple-element.47), channel_id=1, source_target_pairs={{0,120},{8,0},{16,8},{24,16},{32,24},{40,32},{48,40},{56,48},{64,5... | collective-permute-start | bytes 786440 | tf_op jit(solution)/shard_map/ppermute | solution.py:694
  22.2 9.9 %collective-permute-start.4 = (bf16[5,64,512]{2,1,0:T(8,128)(2,1)S(1)}, bf16[5,64,512]{2,1,0:T(8,128)(2,1)S(1)}, u32[]{:S(2)}, u32[]{:S(2)}) collective-permute-start(bf16[5,64,512]{2,1,0:T(8,128)(2,1)S(1)} %get-tuple-element.54), channel_id=1, source_target_pairs={{0,1},{1,0},{2,3},{3,2},{4,5},{5,4},{6,7},{7,6},{8,9},{9,8},{10,11... | collective-permute-start | bytes 983048 | tf_op jit(solution)/shard_map/ppermute | solution.py:694
  24.3 10.6 %collective-permute-start.5 = (bf16[9,16,640]{2,1,0:T(8,128)(2,1)S(1)}, bf16[9,16,640]{2,1,0:T(8,128)(2,1)S(1)}, u32[]{:S(2)}, u32[]{:S(2)}) collective-permute-start(bf16[9,16,640]{2,1,0:T(8,128)(2,1)S(1)} %get-tuple-element.55), channel_id=1, source_target_pairs={{0,1},{1,0},{2,3},{3,2},{4,5},{5,4},{6,7},{7,6},{8,9},{9,8},{10,11... | collective-permute-start | bytes 552968 | tf_op jit(solution)/shard_map/ppermute | solution.py:694
  26.4 4.6 %copy-start.4 = (f32[2,64,512]{2,1,0:T(8,128)S(1)}, f32[2,64,512]{2,1,0:T(8,128)}, u32[]{:S(2)}) copy-start(f32[2,64,512]{2,1,0:T(8,128)} %get-tuple-element.34.refs_0_.refs_6_.refs_2_.refs_4_.refs_3_) | copy-start | bytes 786436
  31.0 5.0 %collective-permute-start.6 = (bf16[5,16,640]{2,1,0:T(8,128)(2,1)S(1)}, bf16[5,16,640]{2,1,0:T(8,128)(2,1)S(1)}, u32[]{:S(2)}, u32[]{:S(2)}) collective-permute-start(bf16[5,16,640]{2,1,0:T(8,128)(2,1)S(1)} %get-tuple-element.63), channel_id=1, source_target_pairs={{0,1},{1,0},{2,3},{3,2},{4,5},{5,4},{6,7},{7,6},{8,9},{9,8},{10,11... | collective-permute-start | bytes 307208 | tf_op jit(solution)/shard_map/ppermute | solution.py:694
